TPU v7x, 32 devices: a whole 2x2x4 slice. The times are simulated.
32 devices in a mesh: comp: 2 (over core), lat: 4 (over y, x), lon: 4 (over z).
Axes of the slice: x: 2, y: 2, z: 4, core: 2. Of those that a mesh axis runs over, the one named last changes fastest.
Arguments:
- state: float32 [2, 80, 32, 512], P('comp', None, 'lat', 'lon')
- mixing: float32 [2, 80, 80], P('comp')
- diffusivity: float32 [2, 80], P('comp'), may hold values from 0.22 to 0.25
- weights: float32 [2, 64], P('comp'), may hold values from 0.25 to 1
- links: int32 [2, 4, 4, 4, 8], P('comp', 'lat', 'lon'), may hold values from 0 to 63, as said below
- land: int32 [32, 4], P('lat', 'lon'), may hold values 0 or 1
- depth: int32 [32, 4], P('lat', 'lon'), may hold values from 79 to 80
Outputs:
- advanced: float32 [2, 80, 32, 512], P('comp', None, 'lat', 'lon')
Inputs may be any that keep to these rules, and one draw needn't show every extreme that they name: Entries are source row below 8, destination lon index below 4, destination row below 8, weight index below 64. A device's links come in 2 consecutive groups of 4, each group with one destination, distinct within the device; in every latitude row of a section, the first group of every device has the same destination.
All inputs are finite; a program needn't handle non-finite values. No bound on the sum of `land` on one device may be relied on, other than what follows from the above.
Results may differ from a plain program's by a relative error of at most 0.0003.
Values sent between devices are 32-bit elements; how exact they have to be, the bound alone decides.
No kernel may reach another device: no remote copies, remote signals or barrier semaphores. Data moves between devices by JAX's collectives and lax.ppermute only.
A program may use at most 64 MiB of HBM per device.

v0:
```python
import jax
import jax.numpy as jnp
from jax import lax
from jax.sharding import PartitionSpec as P

STEPS = 4
CAP = 4


coupling_rate = 0.5


def swapped(value, axis, bit):
    mask = 2**bit
    pairs = [(source, source ^ mask) for source in range(lax.axis_size(axis))]
    return lax.ppermute(value, axis, pairs)


def padded_2(shard, sides, width):
    for axis, dim in sides:
        size, length = (lax.axis_size(axis), shard.shape[dim])
        up = [(i, (i + 1) % size) for i in range(size)]
        down = [(j, i) for i, j in up]
        last = lax.slice_in_dim(shard, length - width, length, axis=dim)
        first = lax.slice_in_dim(shard, 0, width, axis=dim)
        before = lax.ppermute(last, axis, up)
        after = lax.ppermute(first, axis, down)
        shard = jnp.concatenate([before, shard, after], axis=dim)
    return shard


def advance(padded, diffuse, flux_one, active, mix_mat):
    middle = padded[:, 1:-1, 1:-1]
    neighbours = (
        padded[:, 2:, 1:-1] + padded[:, :-2, 1:-1] + padded[:, 1:-1, 2:] + padded[:, 1:-1, :-2]
    )
    moved = middle + diffuse * (neighbours - 4.0 * middle)
    moved = moved.at[0].add(flux_one)
    levels = middle.shape[0]
    mixed = jnp.dot(
        mix_mat,
        (moved * active).reshape(levels, -1),
        precision=lax.Precision.HIGHEST,
        preferred_element_type=jnp.float32,
    ).reshape(middle.shape)
    return active * mixed + (1.0 - active) * middle


def on_device(state, mixing, diffusivity, weights, links, land, depth):
    tracer = state[0]
    mix_mat = mixing[0]
    diffuse = diffusivity[0][:, None, None]
    levels, row_count, cell_count = tracer.shape
    ocean_flag = lax.axis_index("comp") == 1
    sea_cells = jnp.broadcast_to(land.astype(jnp.float32), (row_count, cell_count))
    deep_cells = jnp.broadcast_to((land * depth).astype(jnp.float32), (row_count, cell_count))
    level_ids = jnp.arange(levels, dtype=jnp.float32)[:, None, None]
    surface = tracer[0]
    link_table = links.reshape(4, -1)
    sources = link_table[0]
    targets = link_table[1]
    dest_rows = link_table[2]
    weight_ids = link_table[3]
    row_ids = jnp.arange(row_count, dtype=jnp.int32)
    picker = (sources[:, None] == row_ids[None, :]).astype(jnp.float32)
    picked = jnp.dot(
        picker, surface, precision=lax.Precision.HIGHEST, preferred_element_type=jnp.float32
    )
    table = weights[0]
    weight_link = jnp.sum(
        jnp.where(
            weight_ids[:, None] == jnp.arange(table.shape[0], dtype=jnp.int32)[None, :],
            table[None, :],
            0.0,
        ),
        axis=1,
    )
    values = picked * weight_link[:, None]
    lon_count = lax.axis_size("lon")
    group_dest = targets.reshape(-1, CAP)[:, 0]
    placing = (jnp.arange(lon_count, dtype=jnp.int32)[:, None] == group_dest[None, :]).astype(
        jnp.float32
    )
    slots_out = jnp.einsum(
        "ng,gkc->nkc", placing, values.reshape(-1, CAP, cell_count), precision=lax.Precision.HIGHEST
    )
    link_meta = jnp.stack([weight_link, dest_rows.astype(jnp.float32)], axis=-1).reshape(-1, CAP, 2)
    meta_out = jnp.einsum("ng,gke->nke", placing, link_meta, precision=lax.Precision.HIGHEST)
    crossed, cross_meta = swapped((slots_out, meta_out), "comp", 0)
    received, recv_meta = (
        lax.all_to_all(crossed, "lon", split_axis=0, concat_axis=0, tiled=True),
        lax.all_to_all(cross_meta, "lon", split_axis=0, concat_axis=0, tiled=True),
    )
    recv_rows = recv_meta[..., 1].reshape(-1)
    recv_wts = recv_meta[..., 0].reshape(-1)
    select = (row_ids.astype(jnp.float32)[:, None] == recv_rows[None, :]).astype(jnp.float32)
    accum = jnp.dot(
        select,
        received.reshape(-1, cell_count),
        precision=lax.Precision.HIGHEST,
        preferred_element_type=jnp.float32,
    )
    totals = jnp.dot(
        select,
        recv_wts[:, None],
        precision=lax.Precision.HIGHEST,
        preferred_element_type=jnp.float32,
    )
    imported = accum / jnp.maximum(totals, 1.0)
    flux_field = coupling_rate * sea_cells * (imported - surface)
    lat_pos = lax.axis_index("lat")
    lat_count = lax.axis_size("lat")
    ocean_part = (level_ids < deep_cells[None]).astype(jnp.float32)
    active = jnp.where(ocean_flag, ocean_part, jnp.ones_like(ocean_part))
    padded_ids = jnp.arange(row_count + 2, dtype=jnp.int32)
    row_keep = jnp.where(padded_ids == 0, (lat_pos > 0).astype(jnp.float32), 1.0)
    row_keep = jnp.where(
        padded_ids == row_count + 1, (lat_pos < lat_count - 1).astype(jnp.float32), row_keep
    )
    for step in range(STEPS):
        padded = padded_2(tracer, (("lat", 1), ("lon", 2)), 1)
        padded = padded * row_keep[None, :, None]
        tracer = advance(padded, diffuse, flux_field, active, mix_mat)
    return tracer[None]


def solution(mesh):
    in_specs = (
        P("comp", None, "lat", "lon"),
        P("comp", None, None),
        P("comp", None),
        P("comp", None),
        P("comp", "lat", "lon", None, None),
        P("lat", "lon"),
        P("lat", "lon"),
    )
    out_specs = P("comp", None, "lat", "lon")
    return jax.shard_map(
        on_device, mesh=mesh, in_specs=in_specs, out_specs=out_specs, check_vma=False
    )
```

profile of v0, /device:TPU:0, one launch (start us, length us, event | category | flops | bytes accessed | tf_op | source)
XLA Modules:
  0.0 82.8 jit_solution(9322550979765003629)
XLA Ops:
  0.0 0.7 convert_reduce_fusion
  0.7 0.8 slice_reduce_fusion.3
  1.8 0.8 %select_reduce_fusion = f32[8]{0:T(128)S(1)} fusion(f32[64]{0:T(128)} %bitcast.96, s32[8]{0:T(128)S(1)} %get-tuple-element.72), kind=kLoop, calls=%fused_computation.84 | loop fusion | flops 1528 | bytes 320 | tf_op jit(solution)/shard_map/reduce_sum | solution.py:70
  3.4 0.9 %convolution_multiply_fusion = f32[8,128]{1,0:T(8,128)S(1)} fusion(f32[1,80,8,128]{3,2,1,0:T(8,128)} %param.15, f32[8]{0:T(128)S(1)} %select_reduce_fusion, s32[8]{0:T(128)S(1)} %get-tuple-element.73), kind=kOutput, calls=%fused_computation.12 | convolution fusion | flops 99392 | bytes 8256 | tf_op jit(solution)/shard_map/dot_general | solution.py:66
  4.6 1.1 %fusion.68 = (f32[80,1,128]{2,1,0:T(1,128)S(1)}, f32[80,1,128]{2,1,0:T(1,128)S(1)}) fusion(f32[80,8,128]{2,1,0:T(8,128)} %bitcast.84), kind=kLoop, calls=%fused_computation.121 | loop fusion | bytes 163840 | tf_op jit(solution)/shard_map/slice | solution.py:24
  5.8 3.0 %collective-permute-start = (f32[80,1,128]{2,1,0:T(1,128)S(1)}, f32[80,1,128]{2,1,0:T(1,128)S(1)}, u32[]{:S(2)}, u32[]{:S(2)}) collective-permute-start(f32[80,1,128]{2,1,0:T(1,128)S(1)} %get-tuple-element.69), channel_id=1, source_target_pairs={{0,4},{4,8},{8,12},{12,0},{1,5},{5,9},{9,13},{13,1},{2,6},{6,10},{... | collective-permute-start | bytes 122888 | tf_op jit(solution)/shard_map/ppermute | solution.py:26
  8.8 1.0 %collective-permute-start.1 = (f32[80,1,128]{2,1,0:T(1,128)S(1)}, f32[80,1,128]{2,1,0:T(1,128)S(1)}, u32[]{:S(2)}, u32[]{:S(2)}) collective-permute-start(f32[80,1,128]{2,1,0:T(1,128)S(1)} %get-tuple-element.70), channel_id=1, source_target_pairs={{4,0},{8,4},{12,8},{0,12},{5,1},{9,5},{13,9},{1,13},{6,2},{10,6},{... | collective-permute-start | bytes 122888 | tf_op jit(solution)/shard_map/ppermute | solution.py:27
  9.8 0.7 multiply_bitcast_fusion
  10.5 0.7 convert_bitcast_fusion
  11.1 0.6 copy.34
  11.7 5.3 %all-to-all-start = ((f32[4,4,2]{1,2,0:T(2,128)}), f32[4,4,2]{1,2,0:T(2,128)S(1)}, u32[]{:S(2)}, u32[]{:S(2)}) async-start(f32[4,4,2]{1,2,0:T(2,128)} %copy.34), calls=%async_computation | async-start | bytes 8192 | tf_op jit(solution)/shard_map/all_to_all | solution.py:92
  17.0 5.6 %all-to-all-done = f32[4,4,2]{1,2,0:T(2,128)S(1)} async-done(((f32[4,4,2]{1,2,0:T(2,128)}), f32[4,4,2]{1,2,0:T(2,128)S(1)}, u32[]{:S(2)}, u32[]{:S(2)}) %all-to-all-start) | async-done | bytes 160 | tf_op jit(solution)/shard_map/all_to_all | solution.py:92
  22.8 1.1 %pad_maximum_fusion = f32[80,10,128]{2,1,0:T(8,128)S(1)} fusion(f32[80,1,128]{2,1,0:T(1,128)S(1)} %collective-permute-done.1, f32[80,8,128]{2,1,0:T(8,128)} %bitcast.85, f32[80,1,128]{2,1,0:T(1,128)S(1)} %collective-permute-done), kind=kLoop, calls=%fused_computation.15 | loop fusion | flops 204800 | bytes 819200 | tf_op jit(solution)/shard_map/concatenate | solution.py:28
  24.6 0.6 collective-permute-start.3
  25.2 1.5 %collective-permute-start.2 = (f32[80,10,1]{0,2,1:T(1,128)S(1)}, f32[80,10,1]{0,2,1:T(1,128)S(1)}, u32[]{:S(2)}, u32[]{:S(2)}) collective-permute-start(f32[80,10,1]{0,2,1:T(1,128)S(1)} %copy.30), channel_id=1, source_target_pairs={{0,1},{1,2},{2,3},{3,0},{4,5},{5,6},{6,7},{7,4},{8,9},{9,10},{10,1... | collective-permute-start | bytes 9608 | tf_op jit(solution)/shard_map/ppermute | solution.py:26
  26.8 0.6 copy.36
  27.4 3.6 %all-to-all-start.1 = ((f32[4,4,128]{2,1,0:T(4,128)}), f32[4,4,128]{2,1,0:T(4,128)S(1)}, u32[]{:S(2)}, u32[]{:S(2)}) async-start(f32[4,4,128]{2,1,0:T(4,128)} %copy.36), calls=%async_computation.1 | async-start | bytes 16384 | tf_op jit(solution)/shard_map/all_to_all | solution.py:91
  31.9 0.9 %maximum_multiply_fusion = f32[80,10,130]{2,1,0:T(8,128)S(1)} fusion(f32[80,10,1]{2,1,0:T(8,128)S(1)} %copy.33, f32[80,1,128]{2,1,0:T(1,128)S(1)} %collective-permute-done.1, f32[80,8,128]{2,1,0:T(8,128)S(1)} %bitcast.86, f32[80,1,128]{2,1,0:T(1,128)S(1)} %collective-permute-done, f32[80,10,1]{2,1,0:T(8,128)S(1)} %copy.32, f32[10]{0:T(128)S(1)} %compare_select_fusion.1), kind=kLoop, calls=%fused_computation | loop fusion | flops 520000 | bytes 832040 | tf_op jit(solution)/shard_map/mul | solution.py:122
  32.8 0.5 fusion.27
  33.3 3.4 %all-to-all-done.1 = f32[4,4,128]{2,1,0:T(4,128)S(1)} async-done(((f32[4,4,128]{2,1,0:T(4,128)}), f32[4,4,128]{2,1,0:T(4,128)S(1)}, u32[]{:S(2)}, u32[]{:S(2)}) %all-to-all-start.1) | async-done | bytes 8224 | tf_op jit(solution)/shard_map/all_to_all | solution.py:91
  37.0 0.5 convolution_bitcast_fusion.3
  37.8 0.6 collective-permute-start.6
  38.4 2.3 %collective-permute-start.7 = (f32[80,1,128]{2,1,0:T(1,128)S(1)}, f32[80,1,128]{2,1,0:T(1,128)S(1)}, u32[]{:S(2)}, u32[]{:S(2)}) collective-permute-start(f32[80,1,128]{2,1,0:T(1,128)S(1)} %get-tuple-element.68), channel_id=1, source_target_pairs={{4,0},{8,4},{12,8},{0,12},{5,1},{9,5},{13,9},{1,13},{6,2},{10,6},{... | collective-permute-start | bytes 122888 | tf_op jit(solution)/shard_map/ppermute | solution.py:27
  40.7 2.0 %collective-permute-done.6 = f32[80,1,128]{2,1,0:T(1,128)S(1)} collective-permute-done((f32[80,1,128]{2,1,0:T(1,128)S(1)}, f32[80,1,128]{2,1,0:T(1,128)S(1)}, u32[]{:S(2)}, u32[]{:S(2)}) %collective-permute-start.6) | collective-permute-done | bytes 40992 | tf_op jit(solution)/shard_map/ppermute | solution.py:26
  42.7 0.5 collective-permute-done.7
  43.8 0.6 collective-permute-start.8
  44.6 3.2 %collective-permute-start.9 = (f32[80,10,1]{0,2,1:T(1,128)S(1)}, f32[80,10,1]{0,2,1:T(1,128)S(1)}, u32[]{:S(2)}, u32[]{:S(2)}) collective-permute-start(f32[80,10,1]{0,2,1:T(1,128)S(1)} %copy.38), channel_id=1, source_target_pairs={{1,0},{2,1},{3,2},{0,3},{5,4},{6,5},{7,6},{4,7},{9,8},{10,9},{11,1... | collective-permute-start | bytes 9608 | tf_op jit(solution)/shard_map/ppermute | solution.py:27
  47.9 1.4 %collective-permute-done.8 = f32[80,10,1]{0,2,1:T(1,128)S(1)} collective-permute-done((f32[80,10,1]{0,2,1:T(1,128)S(1)}, f32[80,10,1]{0,2,1:T(1,128)S(1)}, u32[]{:S(2)}, u32[]{:S(2)}) %collective-permute-start.8) | collective-permute-done | bytes 3232 | tf_op jit(solution)/shard_map/ppermute | solution.py:26
  50.0 0.9 %maximum_multiply_fusion.1 = f32[80,10,130]{2,1,0:T(8,128)S(1)} fusion(f32[80,10,1]{2,1,0:T(8,128)S(1)} %copy.40, f32[80,1,128]{2,1,0:T(1,128)S(1)} %collective-permute-done.7, f32[80,8,128]{2,1,0:T(8,128)S(1)} %fusion.13, f32[80,1,128]{2,1,0:T(1,128)S(1)} %collective-permute-done.6, f32[80,10,1]{2,1,0:T(8,128)S(1)} %copy.39, f32[10]{0:T(128)S(1)} %compare_select_fusion.1), kind=kLoop, calls=%fused_computation.1 | loop fusion | flops 520000 | bytes 832040 | tf_op jit(solution)/shard_map/mul | solution.py:122
  50.9 0.5 fusion.24
  51.5 0.5 convolution_bitcast_fusion.2
  52.3 2.5 %collective-permute-start.10 = (f32[80,1,128]{2,1,0:T(1,128)S(1)}, f32[80,1,128]{2,1,0:T(1,128)S(1)}, u32[]{:S(2)}, u32[]{:S(2)}) collective-permute-start(f32[80,1,128]{2,1,0:T(1,128)S(1)} %get-tuple-element.65), channel_id=1, source_target_pairs={{0,4},{4,8},{8,12},{12,0},{1,5},{5,9},{9,13},{13,1},{2,6},{6,10},{... | collective-permute-start | bytes 122888 | tf_op jit(solution)/shard_map/ppermute | solution.py:26
  55.3 2.0 %collective-permute-done.10 = f32[80,1,128]{2,1,0:T(1,128)S(1)} collective-permute-done((f32[80,1,128]{2,1,0:T(1,128)S(1)}, f32[80,1,128]{2,1,0:T(1,128)S(1)}, u32[]{:S(2)}, u32[]{:S(2)}) %collective-permute-start.10) | collective-permute-done | bytes 40992 | tf_op jit(solution)/shard_map/ppermute | solution.py:26
  57.3 1.6 %collective-permute-done.11 = f32[80,1,128]{2,1,0:T(1,128)S(1)} collective-permute-done((f32[80,1,128]{2,1,0:T(1,128)S(1)}, f32[80,1,128]{2,1,0:T(1,128)S(1)}, u32[]{:S(2)}, u32[]{:S(2)}) %collective-permute-start.11) | collective-permute-done | bytes 40992 | tf_op jit(solution)/shard_map/ppermute | solution.py:27
  59.7 4.0 %collective-permute-start.13 = (f32[80,10,1]{0,2,1:T(1,128)S(1)}, f32[80,10,1]{0,2,1:T(1,128)S(1)}, u32[]{:S(2)}, u32[]{:S(2)}) collective-permute-start(f32[80,10,1]{0,2,1:T(1,128)S(1)} %copy.42), channel_id=1, source_target_pairs={{1,0},{2,1},{3,2},{0,3},{5,4},{6,5},{7,6},{4,7},{9,8},{10,9},{11,1... | collective-permute-start | bytes 9608 | tf_op jit(solution)/shard_map/ppermute | solution.py:27
  63.7 1.2 %collective-permute-done.12 = f32[80,10,1]{0,2,1:T(1,128)S(1)} collective-permute-done((f32[80,10,1]{0,2,1:T(1,128)S(1)}, f32[80,10,1]{0,2,1:T(1,128)S(1)}, u32[]{:S(2)}, u32[]{:S(2)}) %collective-permute-start.12) | collective-permute-done | bytes 3232 | tf_op jit(solution)/shard_map/ppermute | solution.py:26
  65.6 0.9 %maximum_multiply_fusion.2 = f32[80,10,130]{2,1,0:T(8,128)S(1)} fusion(f32[80,10,1]{2,1,0:T(8,128)S(1)} %copy.44, f32[80,1,128]{2,1,0:T(1,128)S(1)} %collective-permute-done.11, f32[80,8,128]{2,1,0:T(8,128)S(1)} %fusion.10, f32[80,1,128]{2,1,0:T(1,128)S(1)} %collective-permute-done.10, f32[80,10,1]{2,1,0:T(8,128)S(1)} %copy.43, f32[10]{0:T(128)S(1)} %compare_select_fusion.1), kind=kLoop, calls=%fused_computation.2 | loop fusion | flops 520000 | bytes 832040 | tf_op jit(solution)/shard_map/mul | solution.py:122
  66.6 0.5 fusion.21
  67.9 1.0 %collective-permute-start.14 = (f32[80,1,128]{2,1,0:T(1,128)S(1)}, f32[80,1,128]{2,1,0:T(1,128)S(1)}, u32[]{:S(2)}, u32[]{:S(2)}) collective-permute-start(f32[80,1,128]{2,1,0:T(1,128)S(1)} %get-tuple-element.63), channel_id=1, source_target_pairs={{0,4},{4,8},{8,12},{12,0},{1,5},{5,9},{9,13},{13,1},{2,6},{6,10},{... | collective-permute-start | bytes 122888 | tf_op jit(solution)/shard_map/ppermute | solution.py:26
  69.0 2.0 %collective-permute-start.15 = (f32[80,1,128]{2,1,0:T(1,128)S(1)}, f32[80,1,128]{2,1,0:T(1,128)S(1)}, u32[]{:S(2)}, u32[]{:S(2)}) collective-permute-start(f32[80,1,128]{2,1,0:T(1,128)S(1)} %get-tuple-element.64), channel_id=1, source_target_pairs={{4,0},{8,4},{12,8},{0,12},{5,1},{9,5},{13,9},{1,13},{6,2},{10,6},{... | collective-permute-start | bytes 122888 | tf_op jit(solution)/shard_map/ppermute | solution.py:27
  70.9 2.0 %collective-permute-done.14 = f32[80,1,128]{2,1,0:T(1,128)S(1)} collective-permute-done((f32[80,1,128]{2,1,0:T(1,128)S(1)}, f32[80,1,128]{2,1,0:T(1,128)S(1)}, u32[]{:S(2)}, u32[]{:S(2)}) %collective-permute-start.14) | collective-permute-done | bytes 40992 | tf_op jit(solution)/shard_map/ppermute | solution.py:26
  73.6 1.0 %collective-permute-start.16 = (f32[80,10,1]{0,2,1:T(1,128)S(1)}, f32[80,10,1]{0,2,1:T(1,128)S(1)}, u32[]{:S(2)}, u32[]{:S(2)}) collective-permute-start(f32[80,10,1]{0,2,1:T(1,128)S(1)} %copy.45), channel_id=1, source_target_pairs={{0,1},{1,2},{2,3},{3,0},{4,5},{5,6},{6,7},{7,4},{8,9},{9,10},{10,1... | collective-permute-start | bytes 9608 | tf_op jit(solution)/shard_map/ppermute | solution.py:26
  74.8 2.9 %collective-permute-start.17 = (f32[80,10,1]{0,2,1:T(1,128)S(1)}, f32[80,10,1]{0,2,1:T(1,128)S(1)}, u32[]{:S(2)}, u32[]{:S(2)}) collective-permute-start(f32[80,10,1]{0,2,1:T(1,128)S(1)} %copy.46), channel_id=1, source_target_pairs={{1,0},{2,1},{3,2},{0,3},{5,4},{6,5},{7,6},{4,7},{9,8},{10,9},{11,1... | collective-permute-start | bytes 9608 | tf_op jit(solution)/shard_map/ppermute | solution.py:27
  77.7 1.3 %collective-permute-done.16 = f32[80,10,1]{0,2,1:T(1,128)S(1)} collective-permute-done((f32[80,10,1]{0,2,1:T(1,128)S(1)}, f32[80,10,1]{0,2,1:T(1,128)S(1)}, u32[]{:S(2)}, u32[]{:S(2)}) %collective-permute-start.16) | collective-permute-done | bytes 3232 | tf_op jit(solution)/shard_map/ppermute | solution.py:26
  79.8 0.9 %maximum_multiply_fusion.3 = f32[80,10,130]{2,1,0:T(8,128)S(1)} fusion(f32[80,10,1]{2,1,0:T(8,128)S(1)} %copy.48, f32[80,1,128]{2,1,0:T(1,128)S(1)} %collective-permute-done.15, f32[80,8,128]{2,1,0:T(8,128)S(1)} %fusion.7, f32[80,1,128]{2,1,0:T(1,128)S(1)} %collective-permute-done.14, f32[80,10,1]{2,1,0:T(8,128)S(1)} %copy.47, f32[10]{0:T(128)S(1)} %compare_select_fusion.1), kind=kLoop, calls=%fused_computation.3 | loop fusion | flops 520000 | bytes 832040 | tf_op jit(solution)/shard_map/mul | solution.py:122
  80.7 0.5 fusion.18
  81.3 0.5 convolution_bitcast_fusion
  81.9 0.9 %fusion.4 = f32[80,8,128]{2,1,0:T(8,128)} fusion(f32[10,8,8,128]{3,2,1,0:T(8,128)S(1)} %copy.56, f32[80,10,130]{2,1,0:T(8,128)S(1)} %maximum_multiply_fusion.3, f32[8]{0:T(128)S(1)} %convert_bitcast_fusion, pred[]{:T(512)S(6)} %eq.77), kind=kLoop, calls=%fused_computation.20 | loop fusion | flops 573440 | bytes 983073 | tf_op jit(solution)/shard_map/add | solution.py:46
  (74 shorter events, 10.4 us)
Async XLA Ops:
  0.0 37.0 %copy-start = (f32[1,80,80]{2,1,0:T(8,128)S(1)}, f32[1,80,80]{2,1,0:T(8,128)}, u32[]{:S(2)}) copy-start(f32[1,80,80]{2,1,0:T(8,128)} %param.16) | copy-start | bytes 76804
  3.0 8.2 %collective-permute-start.4 = (f32[4,4,2]{1,0,2:T(4,128)S(1)}, f32[4,4,2]{1,0,2:T(4,128)S(1)}, u32[]{:S(2)}, u32[]{:S(2)}) collective-permute-start(f32[4,4,2]{1,0,2:T(4,128)S(1)} %fusion.47), channel_id=1, source_target_pairs={{0,16},{16,0},{1,17},{17,1},{2,18},{18,2},{3,19},{19,3},{4,20},{20... | collective-permute-start | bytes 392 | tf_op jit(solution)/shard_map/ppermute | solution.py:16
  4.6 22.2 %collective-permute-start.5 = (f32[4,4,128]{2,0,1:T(4,128)S(1)}, f32[4,4,128]{2,0,1:T(4,128)S(1)}, u32[]{:S(2)}, u32[]{:S(2)}) collective-permute-start(f32[4,4,128]{2,0,1:T(4,128)S(1)} %fusion.44), channel_id=1, source_target_pairs={{0,16},{16,0},{1,17},{17,1},{2,18},{18,2},{3,19},{19,3},{4,20},{20... | collective-permute-start | bytes 24584 | tf_op jit(solution)/shard_map/ppermute | solution.py:16
  5.8 17.0 %collective-permute-start = (f32[80,1,128]{2,1,0:T(1,128)S(1)}, f32[80,1,128]{2,1,0:T(1,128)S(1)}, u32[]{:S(2)}, u32[]{:S(2)}) collective-permute-start(f32[80,1,128]{2,1,0:T(1,128)S(1)} %get-tuple-element.69), channel_id=1, source_target_pairs={{0,4},{4,8},{8,12},{12,0},{1,5},{5,9},{9,13},{13,1},{2,6},{6,10},{... | collective-permute-start | bytes 122888 | tf_op jit(solution)/shard_map/ppermute | solution.py:26
  8.8 14.0 %collective-permute-start.1 = (f32[80,1,128]{2,1,0:T(1,128)S(1)}, f32[80,1,128]{2,1,0:T(1,128)S(1)}, u32[]{:S(2)}, u32[]{:S(2)}) collective-permute-start(f32[80,1,128]{2,1,0:T(1,128)S(1)} %get-tuple-element.70), channel_id=1, source_target_pairs={{4,0},{8,4},{12,8},{0,12},{5,1},{9,5},{13,9},{1,13},{6,2},{10,6},{... | collective-permute-start | bytes 122888 | tf_op jit(solution)/shard_map/ppermute | solution.py:27
  11.7 10.9 %all-to-all-start = ((f32[4,4,2]{1,2,0:T(2,128)}), f32[4,4,2]{1,2,0:T(2,128)S(1)}, u32[]{:S(2)}, u32[]{:S(2)}) async-start(f32[4,4,2]{1,2,0:T(2,128)} %copy.34), calls=%async_computation | async-start | bytes 8192 | tf_op jit(solution)/shard_map/all_to_all | solution.py:92
  24.1 7.7 %copy-start.1 = (f32[1,80,8,128]{3,2,1,0:T(8,128)S(1)}, f32[1,80,8,128]{3,2,1,0:T(8,128)}, u32[]{:S(2)}) copy-start(f32[1,80,8,128]{3,2,1,0:T(8,128)} %param.15) | copy-start | bytes 983044
  24.6 6.9 %collective-permute-start.3 = (f32[80,10,1]{0,2,1:T(1,128)S(1)}, f32[80,10,1]{0,2,1:T(1,128)S(1)}, u32[]{:S(2)}, u32[]{:S(2)}) collective-permute-start(f32[80,10,1]{0,2,1:T(1,128)S(1)} %copy.31), channel_id=1, source_target_pairs={{1,0},{2,1},{3,2},{0,3},{5,4},{6,5},{7,6},{4,7},{9,8},{10,9},{11,1... | collective-permute-start | bytes 9608 | tf_op jit(solution)/shard_map/ppermute | solution.py:27
  25.2 5.9 %collective-permute-start.2 = (f32[80,10,1]{0,2,1:T(1,128)S(1)}, f32[80,10,1]{0,2,1:T(1,128)S(1)}, u32[]{:S(2)}, u32[]{:S(2)}) collective-permute-start(f32[80,10,1]{0,2,1:T(1,128)S(1)} %copy.30), channel_id=1, source_target_pairs={{0,1},{1,2},{2,3},{3,0},{4,5},{5,6},{6,7},{7,4},{8,9},{9,10},{10,1... | collective-permute-start | bytes 9608 | tf_op jit(solution)/shard_map/ppermute | solution.py:26
  27.4 9.2 %all-to-all-start.1 = ((f32[4,4,128]{2,1,0:T(4,128)}), f32[4,4,128]{2,1,0:T(4,128)S(1)}, u32[]{:S(2)}, u32[]{:S(2)}) async-start(f32[4,4,128]{2,1,0:T(4,128)} %copy.36), calls=%async_computation.1 | async-start | bytes 16384 | tf_op jit(solution)/shard_map/all_to_all | solution.py:91
  31.8 0.9 %copy-start.2 = (f32[1,80]{1,0:T(1,128)S(1)}, f32[1,80]{1,0:T(1,128)}, u32[]{:S(2)}) copy-start(f32[1,80]{1,0:T(1,128)} %param.17) | copy-start | bytes 964
  37.8 5.0 %collective-permute-start.6 = (f32[80,1,128]{2,1,0:T(1,128)S(1)}, f32[80,1,128]{2,1,0:T(1,128)S(1)}, u32[]{:S(2)}, u32[]{:S(2)}) collective-permute-start(f32[80,1,128]{2,1,0:T(1,128)S(1)} %get-tuple-element.67), channel_id=1, source_target_pairs={{0,4},{4,8},{8,12},{12,0},{1,5},{5,9},{9,13},{13,1},{2,6},{6,10},{... | collective-permute-start | bytes 122888 | tf_op jit(solution)/shard_map/ppermute | solution.py:26
  38.4 4.8 %collective-permute-start.7 = (f32[80,1,128]{2,1,0:T(1,128)S(1)}, f32[80,1,128]{2,1,0:T(1,128)S(1)}, u32[]{:S(2)}, u32[]{:S(2)}) collective-permute-start(f32[80,1,128]{2,1,0:T(1,128)S(1)} %get-tuple-element.68), channel_id=1, source_target_pairs={{4,0},{8,4},{12,8},{0,12},{5,1},{9,5},{13,9},{1,13},{6,2},{10,6},{... | collective-permute-start | bytes 122888 | tf_op jit(solution)/shard_map/ppermute | solution.py:27
  43.8 5.4 %collective-permute-start.8 = (f32[80,10,1]{0,2,1:T(1,128)S(1)}, f32[80,10,1]{0,2,1:T(1,128)S(1)}, u32[]{:S(2)}, u32[]{:S(2)}) collective-permute-start(f32[80,10,1]{0,2,1:T(1,128)S(1)} %copy.37), channel_id=1, source_target_pairs={{0,1},{1,2},{2,3},{3,0},{4,5},{5,6},{6,7},{7,4},{8,9},{9,10},{10,1... | collective-permute-start | bytes 9608 | tf_op jit(solution)/shard_map/ppermute | solution.py:26
  44.6 5.0 %collective-permute-start.9 = (f32[80,10,1]{0,2,1:T(1,128)S(1)}, f32[80,10,1]{0,2,1:T(1,128)S(1)}, u32[]{:S(2)}, u32[]{:S(2)}) collective-permute-start(f32[80,10,1]{0,2,1:T(1,128)S(1)} %copy.38), channel_id=1, source_target_pairs={{1,0},{2,1},{3,2},{0,3},{5,4},{6,5},{7,6},{4,7},{9,8},{10,9},{11,1... | collective-permute-start | bytes 9608 | tf_op jit(solution)/shard_map/ppermute | solution.py:27
  52.3 5.0 %collective-permute-start.10 = (f32[80,1,128]{2,1,0:T(1,128)S(1)}, f32[80,1,128]{2,1,0:T(1,128)S(1)}, u32[]{:S(2)}, u32[]{:S(2)}) collective-permute-start(f32[80,1,128]{2,1,0:T(1,128)S(1)} %get-tuple-element.65), channel_id=1, source_target_pairs={{0,4},{4,8},{8,12},{12,0},{1,5},{5,9},{9,13},{13,1},{2,6},{6,10},{... | collective-permute-start | bytes 122888 | tf_op jit(solution)/shard_map/ppermute | solution.py:26
  54.8 4.0 %collective-permute-start.11 = (f32[80,1,128]{2,1,0:T(1,128)S(1)}, f32[80,1,128]{2,1,0:T(1,128)S(1)}, u32[]{:S(2)}, u32[]{:S(2)}) collective-permute-start(f32[80,1,128]{2,1,0:T(1,128)S(1)} %get-tuple-element.66), channel_id=1, source_target_pairs={{4,0},{8,4},{12,8},{0,12},{5,1},{9,5},{13,9},{1,13},{6,2},{10,6},{... | collective-permute-start | bytes 122888 | tf_op jit(solution)/shard_map/ppermute | solution.py:27
  59.4 5.4 %collective-permute-start.12 = (f32[80,10,1]{0,2,1:T(1,128)S(1)}, f32[80,10,1]{0,2,1:T(1,128)S(1)}, u32[]{:S(2)}, u32[]{:S(2)}) collective-permute-start(f32[80,10,1]{0,2,1:T(1,128)S(1)} %copy.41), channel_id=1, source_target_pairs={{0,1},{1,2},{2,3},{3,0},{4,5},{5,6},{6,7},{7,4},{8,9},{9,10},{10,1... | collective-permute-start | bytes 9608 | tf_op jit(solution)/shard_map/ppermute | solution.py:26
  59.7 5.6 %collective-permute-start.13 = (f32[80,10,1]{0,2,1:T(1,128)S(1)}, f32[80,10,1]{0,2,1:T(1,128)S(1)}, u32[]{:S(2)}, u32[]{:S(2)}) collective-permute-start(f32[80,10,1]{0,2,1:T(1,128)S(1)} %copy.42), channel_id=1, source_target_pairs={{1,0},{2,1},{3,2},{0,3},{5,4},{6,5},{7,6},{4,7},{9,8},{10,9},{11,1... | collective-permute-start | bytes 9608 | tf_op jit(solution)/shard_map/ppermute | solution.py:27
  67.9 5.0 %collective-permute-start.14 = (f32[80,1,128]{2,1,0:T(1,128)S(1)}, f32[80,1,128]{2,1,0:T(1,128)S(1)}, u32[]{:S(2)}, u32[]{:S(2)}) collective-permute-start(f32[80,1,128]{2,1,0:T(1,128)S(1)} %get-tuple-element.63), channel_id=1, source_target_pairs={{0,4},{4,8},{8,12},{12,0},{1,5},{5,9},{9,13},{13,1},{2,6},{6,10},{... | collective-permute-start | bytes 122888 | tf_op jit(solution)/shard_map/ppermute | solution.py:26
  69.0 4.0 %collective-permute-start.15 = (f32[80,1,128]{2,1,0:T(1,128)S(1)}, f32[80,1,128]{2,1,0:T(1,128)S(1)}, u32[]{:S(2)}, u32[]{:S(2)}) collective-permute-start(f32[80,1,128]{2,1,0:T(1,128)S(1)} %get-tuple-element.64), channel_id=1, source_target_pairs={{4,0},{8,4},{12,8},{0,12},{5,1},{9,5},{13,9},{1,13},{6,2},{10,6},{... | collective-permute-start | bytes 122888 | tf_op jit(solution)/shard_map/ppermute | solution.py:27
  73.6 5.5 %collective-permute-start.16 = (f32[80,10,1]{0,2,1:T(1,128)S(1)}, f32[80,10,1]{0,2,1:T(1,128)S(1)}, u32[]{:S(2)}, u32[]{:S(2)}) collective-permute-start(f32[80,10,1]{0,2,1:T(1,128)S(1)} %copy.45), channel_id=1, source_target_pairs={{0,1},{1,2},{2,3},{3,0},{4,5},{5,6},{6,7},{7,4},{8,9},{9,10},{10,1... | collective-permute-start | bytes 9608 | tf_op jit(solution)/shard_map/ppermute | solution.py:26
  74.8 4.6 %collective-permute-start.17 = (f32[80,10,1]{0,2,1:T(1,128)S(1)}, f32[80,10,1]{0,2,1:T(1,128)S(1)}, u32[]{:S(2)}, u32[]{:S(2)}) collective-permute-start(f32[80,10,1]{0,2,1:T(1,128)S(1)} %copy.46), channel_id=1, source_target_pairs={{1,0},{2,1},{3,2},{0,3},{5,4},{6,5},{7,6},{4,7},{9,8},{10,9},{11,1... | collective-permute-start | bytes 9608 | tf_op jit(solution)/shard_map/ppermute | solution.py:27
where the time goes:
time: 83.2 us; the launch traced here: 82.8 us
  starting transfers between devices  36.2 us (44%)
  waiting for transfers between devices  20.9 us (25%)
  other arithmetic  11.8 us (14%)
  local copies, waits for them, and re-layouts  9.78 us (12%)
  matrix products  3.62 us (4%)
    ppermute x8, starting transfers between devices, padded_2(): after = lax.ppermute(first, axis, down)  16.4 us
    ppermute x8, starting transfers between devices, padded_2(): before = lax.ppermute(last, axis, up)  10.3 us
    ppermute x8, waiting for transfers between devices, padded_2(): before = lax.ppermute(last, axis, up)  9.8 us
    all_to_all x1, waiting for transfers between devices, on_device(): lax.all_to_all(cross_meta, 'lon', split_axis=0, concat_axis=0, tiled=True)  5.57 us
    all_to_all x1, starting transfers between devices, on_device(): lax.all_to_all(cross_meta, 'lon', split_axis=0, concat_axis=0, tiled=True)  5.28 us
    mul x4, other arithmetic, on_device(): padded = padded * row_keep[None, :, None]  3.68 us
    all_to_all x1, starting transfers between devices, on_device(): lax.all_to_all(crossed, 'lon', split_axis=0, concat_axis=0, tiled=True)  3.64 us
    all_to_all x1, waiting for transfers between devices, on_device(): lax.all_to_all(crossed, 'lon', split_axis=0, concat_axis=0, tiled=True)  3.37 us
  transfers between devices with their start and end apart: 20, of which 11 were waited for; matrix products, arithmetic and copies ran while one was open for 13% of the time, Pallas kernels for 0%

commit v1 on v0

v1 whole, which is shorter than its diff:
```python
import functools

import jax
import jax.numpy as jnp
from jax import lax
from jax.experimental import pallas as pl
from jax.experimental.pallas import tpu as pltpu
from jax.sharding import PartitionSpec as P

STEPS = 4
EDGE = 8
AXES = ("comp", "lat", "lon")
VMEM_LIMIT = 32 * 1024 * 1024

coupling_rate = 0.5


def vmem_spec():
    return pl.BlockSpec(memory_space=pltpu.VMEM)


def lane_ids(shape):
    return lax.broadcasted_iota(jnp.int32, shape, len(shape) - 1)


def roll(value, shift):
    shift = shift % value.shape[-1]
    return value if shift == 0 else pltpu.roll(value, shift, 1)


def as_column(row):
    n = row.shape[1]
    diagonal = lax.broadcasted_iota(jnp.int32, (n, n), 0) == lane_ids((n, n))
    return jnp.sum(jnp.where(diagonal, row, 0.0), axis=1, keepdims=True)


def spread(column):
    rows = column.shape[0]
    shape = (rows, 128)
    mine = lane_ids(shape) // EDGE == lax.broadcasted_iota(jnp.int32, shape, 0)
    return jnp.sum(jnp.where(mine, column, 0.0), axis=0, keepdims=True)


def pack_kernel(surface_ref, links_ref, weights_ref, land_ref, depth_ref, out_ref):
    surface = surface_ref[0, 0]
    rows = surface.shape[0]
    table = links_ref[0, 0, 0].astype(jnp.float32)
    count = table.shape[1]
    source = as_column(table[0:1])
    weight_id = as_column(table[3:4])
    entries = weights_ref.shape[1]
    weight = jnp.sum(
        jnp.where(weight_id == lane_ids((count, entries)).astype(jnp.float32), weights_ref[...], 0.0),
        axis=1,
        keepdims=True,
    )
    picked = jnp.zeros((count, surface.shape[1]), jnp.float32)
    for row in range(rows):
        picked = jnp.where(source == float(row), surface[row : row + 1], picked)
    out_ref[0:count] = weight * picked
    code = table[1:2] * float(rows) + table[2:3]
    diagonal = lax.broadcasted_iota(jnp.int32, (count, 128), 0) == lane_ids((count, 128))
    weight_row = jnp.sum(jnp.where(diagonal, weight, 0.0), axis=0, keepdims=True)
    code_row = jnp.sum(jnp.where(diagonal, as_column(code), 0.0), axis=0, keepdims=True)
    land = land_ref[...].astype(jnp.float32)
    deep = land * depth_ref[...].astype(jnp.float32)
    out_ref[count : count + 1] = code_row
    out_ref[count + 1 : count + 2] = weight_row
    out_ref[count + 2 : count + 3] = spread(land)
    out_ref[count + 3 : count + 4] = spread(deep)
    out_ref[count + 4 :] = jnp.zeros((4, 128), jnp.float32)


def edge_kernel(state_ref, mixing_ref, diffuse_ref, edge_ref, first_ref, second_ref, mix_ref, rate_ref):
    levels, rows, cells = state_ref.shape[1:]
    half = levels // 2
    odd = lax.rem(lax.axis_index("lat"), 2) == 1
    lane = lane_ids((levels, 128))
    packed = jnp.zeros((levels, 128), jnp.float32)
    tiles = []
    for row in range(rows):
        tile = state_ref[0, :, row, :]
        tiles.append(tile)
        start = row * EDGE
        packed = jnp.where((lane >= start) & (lane < start + 4), roll(tile, start), packed)
        packed = jnp.where((lane >= start + 4) & (lane < start + 8), roll(tile, start + 8), packed)
    edge_ref[...] = jnp.where(lane_ids((half, 128)) < 64, packed[:half], roll(packed[half:], 64))
    for k in range(4):
        low, high = tiles[k], tiles[rows - 4 + k]
        first_ref[k] = jnp.where(odd, low, high)
        second_ref[k] = jnp.where(odd, high, low)
    mix = mixing_ref[0]
    top = mix.astype(jnp.bfloat16)
    rest = (mix - top.astype(jnp.float32)).astype(jnp.bfloat16)
    mix_ref[...] = jnp.zeros_like(mix_ref)
    mix_ref[:, 0:levels] = top
    mix_ref[:, levels : 2 * levels] = top
    mix_ref[:, 2 * levels : 3 * levels] = rest
    rate_ref[...] = jnp.broadcast_to(as_column(diffuse_ref[...]), rate_ref.shape)


def flux_kernel(count, slices, east_west, *refs):
    surface_ref, land_ref, depth_ref, *packs, out_ref = refs
    surface = surface_ref[0, 0]
    rows = surface.shape[0]
    half = out_ref.shape[0] - 2 * rows - 8
    lon, lon_count = lax.axis_index("lon"), lax.axis_size("lon")
    odd = lax.rem(lon, 2) == 1
    ocean = lax.axis_index("comp") == 1
    here = lon * rows
    after = lax.rem(lon + 1, lon_count) * rows
    before = lax.rem(lon + lon_count - 1, lon_count) * rows
    index = lax.broadcasted_iota(jnp.int32, (3 * rows, count), 0)
    wanted = jnp.where(
        index < rows, here + index, jnp.where(index < 2 * rows, after + index - rows, before + index - 2 * rows)
    ).astype(jnp.float32)
    accum = jnp.zeros((3 * rows, 128), jnp.float32)
    totals = jnp.zeros((3 * rows, 1), jnp.float32)
    for which, offset in slices:
        ref = packs[which]
        hit = (wanted == ref[offset + count : offset + count + 1, 0:count]).astype(jnp.float32)
        accum += jnp.dot(
            hit,
            ref[offset : offset + count],
            precision=lax.Precision.HIGHEST,
            preferred_element_type=jnp.float32,
        )
        totals += jnp.sum(
            hit * ref[offset + count + 1 : offset + count + 2, 0:count], axis=1, keepdims=True
        )
    imported = accum / jnp.maximum(totals, 1.0)
    land = land_ref[...].astype(jnp.float32)
    deep = land * depth_ref[...].astype(jnp.float32)
    all_levels = float(2 * half)
    deep = jnp.where(ocean, deep, all_levels)
    (first, first_at), (second, second_at) = east_west
    lane = lane_ids((1, 128))
    from_east = lax.rem(lane, EDGE) < 4

    def beside(offset_rows, size):
        one = packs[first][first_at + offset_rows : first_at + offset_rows + size]
        two = packs[second][second_at + offset_rows : second_at + offset_rows + size]
        east_is_one = lane_ids((size, 128)) % EDGE < 4
        return jnp.where(east_is_one != odd, one, two)

    middle = beside(0, half)
    land_beside = beside(half + count + 2, 1)
    deep_beside = jnp.where(ocean, beside(half + count + 3, 1), all_levels)
    imported_beside = jnp.zeros((1, 128), jnp.float32)
    for row in range(rows):
        start = row * EDGE
        east = roll(imported[rows + row : rows + row + 1], start)
        west = roll(imported[2 * rows + row : 2 * rows + row + 1], start + 8)
        mine = (lane >= start) & (lane < start + EDGE)
        imported_beside = jnp.where(mine, jnp.where(from_east, east, west), imported_beside)
    flux_beside = coupling_rate * land_beside * (imported_beside - middle[0:1])
    out_ref[0:half] = middle
    out_ref[half : half + rows] = coupling_rate * land * (imported[0:rows] - surface)
    out_ref[half + rows : half + 2 * rows] = jnp.broadcast_to(deep, (rows, 128))
    out_ref[half + 2 * rows : half + 2 * rows + 1] = flux_beside
    out_ref[half + 2 * rows + 1 : half + 2 * rows + 2] = deep_beside
    out_ref[half + 2 * rows + 2 :] = jnp.zeros((6, 128), jnp.float32)


def update_kernel(
    state_ref, own_ref, rows1_ref, rows2_ref, msg1_ref, msg2_ref, mix_ref, rate_ref, out_ref, x_ref, y_ref
):
    levels, rows, cells = state_ref.shape[1:]
    half = levels // 2
    slots = rows + 2 * STEPS
    odd = lax.rem(lax.axis_index("lat"), 2) == 1
    own = own_ref[...]
    one, two = msg1_ref[...], msg2_ref[...]
    top, bottom = jnp.where(odd, one, two), jnp.where(odd, two, one)
    first_at = jnp.where(odd, 0, rows + STEPS)
    for k in range(STEPS):
        x_ref[first_at + k] = rows1_ref[k]
        x_ref[rows + STEPS - first_at + k] = rows2_ref[k]
    for row in range(rows):
        x_ref[STEPS + row] = state_ref[0, :, row, :]

    def per_slot(value, at, slot):
        if slot < STEPS:
            at, value = at + rows - STEPS + slot, value[0]
        elif slot < STEPS + rows:
            at, value = at + slot - STEPS, value[1]
        else:
            at, value = at + slot - STEPS - rows, value[2]
        return value[at : at + 1]

    parts = (top, own, bottom)
    flux_rows = [per_slot(parts, half, s) for s in range(slots)]
    deep_rows = [per_slot(parts, half + rows, s) for s in range(slots)]

    lane1 = lane_ids((1, 128))
    lane = lane_ids((levels, 128))
    level = lax.broadcasted_iota(jnp.int32, (levels, 128), 0).astype(jnp.float32)
    first_level = lax.broadcasted_iota(jnp.int32, (8, 128), 0) == 0
    place = lane % EDGE

    def unfolded(fold, width):
        a, b, c = (roll(v, s) for v, s in zip(fold, (-4 * EDGE, 4 * EDGE, 12 * EDGE)))
        at = lane_ids(a.shape)
        return jnp.where(at < 4 * EDGE, a, jnp.where(at < 12 * EDGE, b, c))

    low = unfolded([v[:half] for v in parts], 128)
    high = unfolded([roll(v[:half], 64) for v in parts], 128)
    mid = jnp.concatenate([low, high], axis=0)
    at = half + 2 * rows
    flux_mid = unfolded([v[at : at + 1] for v in parts], 128)
    deep_mid = unfolded([v[at + 1 : at + 2] for v in parts], 128)
    left = jnp.zeros((levels, 128), jnp.float32)
    right = left
    flux_left = flux_right = deep_side = jnp.zeros((1, 128), jnp.float32)
    for slot in range(slots):
        start = slot * EDGE
        tile = x_ref[slot]
        mine = (lane >= start) & (lane < start + EDGE)
        left = jnp.where(mine, roll(tile, start + EDGE), left)
        right = jnp.where(mine, roll(tile, start), right)
        mine1 = (lane1 >= start) & (lane1 < start + EDGE)
        flux_left = jnp.where(mine1, roll(flux_rows[slot], start + EDGE), flux_left)
        flux_right = jnp.where(mine1, roll(flux_rows[slot], start), flux_right)
        deep_side = jnp.where(mine1, deep_rows[slot], deep_side)

    mixer = mix_ref[...]
    pad = jnp.zeros((mixer.shape[1] - 3 * levels, 256), jnp.bfloat16)

    def injection(row):
        return jnp.where(first_level, row, 0.0)

    def moved(x, neighbours, flux, active):
        rate = rate_ref[...]
        value = (1.0 - 4.0 * rate) * x + rate * neighbours
        value = jnp.concatenate([value[:8] + injection(flux), value[8:]], axis=0)
        return jnp.where(active, value, 0.0)

    def mixed(values):
        value = jnp.concatenate(values, axis=1)
        hi = value.astype(jnp.bfloat16)
        lo = (value - hi.astype(jnp.float32)).astype(jnp.bfloat16)
        full = jnp.concatenate([hi, lo, hi, pad[:, : value.shape[1]]], axis=0)
        out = jnp.dot(mixer, full, preferred_element_type=jnp.float32)
        return [out[:, 128 * k : 128 * (k + 1)] for k in range(len(values))]

    def strip(tile, west, east):
        around = roll(tile, EDGE) + roll(tile, -EDGE)
        to_west, to_east = roll(tile, 1), roll(tile, -1)
        if west is not None:
            to_west = jnp.where(place == 0, roll(west, 1 - EDGE), to_west)
        if east is not None:
            to_east = jnp.where(place == EDGE - 1, roll(east, EDGE - 1), to_east)
        return around + to_west + to_east

    source, target = x_ref, y_ref
    for step in range(STEPS):
        last = step == STEPS - 1
        active_side, active_mid = level < deep_side, level < deep_mid
        z_left = moved(left, strip(left, None, mid), flux_left, active_side)
        z_right = moved(right, strip(right, mid, None), flux_right, active_side)
        new_left, new_right = mixed([z_left, z_right])
        if not last:
            z_mid = moved(mid, strip(mid, left, right), flux_mid, active_mid)
            mid = jnp.where(active_mid, mixed([z_mid])[0], mid)
        left = jnp.where(active_side, new_left, left)
        right = jnp.where(active_side, new_right, right)
        for slot in range(step + 1, slots - step - 1, 2):
            old, values, masks = [], [], []
            for s in (slot, slot + 1):
                x = source[s]
                neighbours = source[s - 1] + source[s + 1] + roll(x, 1) + roll(x, -1)
                active = level < deep_rows[s]
                old.append(x)
                masks.append(active)
                values.append(moved(x, neighbours, flux_rows[s], active))
            for s, x, active, new in zip((slot, slot + 1), old, masks, mixed(values)):
                new = jnp.where(active, new, x)
                if not last:
                    target[s] = new
                    continue
                new = jnp.where(lane < 4, roll(right, -s * EDGE), new)
                new = jnp.where(lane >= cells - 4, roll(left, cells - EDGE - s * EDGE), new)
                out_ref[0, :, s - STEPS, :] = new
        source, target = target, source


def kernel_call(body, out_shape, blocks, scratch=(), flops=0, nbytes=0):
    return pl.pallas_call(
        body,
        out_shape=out_shape,
        in_specs=blocks,
        out_specs=jax.tree.map(lambda _: vmem_spec(), out_shape),
        scratch_shapes=scratch,
        compiler_params=pltpu.CompilerParams(vmem_limit_bytes=VMEM_LIMIT),
        cost_estimate=pl.CostEstimate(flops=flops, bytes_accessed=nbytes, transcendentals=0),
    )


def f32(*shape):
    return jax.ShapeDtypeStruct(shape, jnp.float32)


def exchange(value, axis, partner):
    size = lax.axis_size(axis)
    pairs = [(i, partner(i)) for i in range(size) if 0 <= partner(i) < size]
    return lax.ppermute(value, axis, pairs)


def on_device(state, mixing, diffusivity, weights, links, land, depth):
    levels, rows, cells = state.shape[1:]
    half = levels // 2
    count = links.shape[-1]
    pack_rows = count + 8
    lon_count = lax.axis_size("lon")

    def near(i):
        return i ^ 1

    def far(i):
        return i - 1 if i % 2 == 0 else i + 1

    def far_round(i):
        return far(i) % lon_count

    surface = lax.slice_in_dim(state, 0, 1, axis=1)
    pack = kernel_call(
        pack_kernel, f32(pack_rows, 128), [vmem_spec()] * 5, flops=20000, nbytes=20000
    )(surface, links, weights, land, depth)
    crossed = exchange(pack, "comp", near)
    edge, up_down_1, up_down_2, mix_parts, rates = kernel_call(
        edge_kernel,
        (
            f32(half, 128),
            f32(STEPS, levels, 128),
            f32(STEPS, levels, 128),
            jax.ShapeDtypeStruct((levels, 256), jnp.bfloat16),
            f32(levels, 128),
        ),
        [vmem_spec()] * 3,
        flops=400000,
        nbytes=900000,
    )(state, mixing, diffusivity)
    rows_1 = exchange(up_down_1, "lat", near)
    rows_2 = exchange(up_down_2, "lat", far)

    mine = jnp.concatenate([edge, crossed], axis=0)
    beside_1 = exchange(mine, "lon", near)
    if lon_count == 4:
        onward = jnp.concatenate([mine, beside_1[half:]], axis=0)
        beside_2 = exchange(onward, "lon", far_round)
        packs = [crossed, beside_1, beside_2]
        slices = [(0, 0), (1, half), (2, half), (2, half + pack_rows)]
        east_west = ((1, 0), (2, 0))
    else:
        beside_2 = exchange(mine, "lon", far_round)
        packs = [lax.all_gather(crossed, "lon", axis=0, tiled=True), beside_1, beside_2]
        slices = [(0, k * pack_rows) for k in range(lon_count)]
        east_west = ((1, 0), (2, 0))
    message = kernel_call(
        functools.partial(flux_kernel, count, slices, east_west),
        f32(half + 2 * rows + 8, 128),
        [vmem_spec()] * (3 + len(packs)),
        flops=200000,
        nbytes=100000,
    )(surface, land, depth, *packs)
    message_1 = exchange(message, "lat", near)
    message_2 = exchange(message, "lat", far)
    return kernel_call(
        update_kernel,
        f32(*state.shape),
        [vmem_spec()] * 8,
        scratch=[pltpu.VMEM((rows + 2 * STEPS, levels, 128), jnp.float32)] * 2,
        flops=300000000,
        nbytes=1500000,
    )(state, message, rows_1, rows_2, message_1, message_2, mix_parts, rates)


def solution(mesh):
    in_specs = (
        P("comp", None, "lat", "lon"),
        P("comp", None, None),
        P("comp", None),
        P("comp", None),
        P("comp", "lat", "lon", None, None),
        P("lat", "lon"),
        P("lat", "lon"),
    )
    out_specs = P("comp", None, "lat", "lon")
    return jax.shard_map(
        on_device, mesh=mesh, in_specs=in_specs, out_specs=out_specs, check_vma=False
    )
```

time: 83.2 us -> 28.6 us (0.34)
  starting transfers between devices: 36.2 us -> 16.1 us
  waiting for transfers between devices: 20.9 us -> 4.27 us
  other arithmetic: 11.8 us -> 0.01 us
  local copies, waits for them, and re-layouts: 9.78 us -> 3.31 us
  Pallas kernels: 0 us -> 4.57 us
  matrix products: 3.62 us -> 0 us
    ppermute x18 -> x7, starting transfers between devices: 27.3 us -> 16.1 us  [exchange(): return lax.ppermute(value, axis, pairs)]
    all_to_all x2 -> x0, waiting for transfers between devices: 8.95 us -> none  [the longest x1 5.57 us: on_device(): lax.all_to_all(cross_meta, 'lon', split_axis=0, concat_axis=0, tiled=True)]
    all_to_all x2 -> x0, starting transfers between devices: 8.92 us -> none  [the longest x1 5.28 us: on_device(): lax.all_to_all(cross_meta, 'lon', split_axis=0, concat_axis=0, tiled=True)]
    ppermute x18 -> x7, waiting for transfers between devices: 12 us -> 4.27 us  [exchange(): return lax.ppermute(value, axis, pairs)]
    mul x9 -> x0, other arithmetic: 4.8 us -> none  [the longest x4 3.68 us: on_device(): padded = padded * row_keep[None, :, None]]
    pallas_call x0 -> x4, Pallas kernels: none -> 4.57 us  [the longest x1 3.53 us: on_device(): kernel_call(update_kernel, f32(*state.shape), [vmem_spec()] * 8, scratch=...]
    slice x19 -> x2, local copies, waits for them, and re-layouts: 4.99 us -> 0.72 us  [the longest x1 0.72 us: on_device(): surface = lax.slice_in_dim(state, 0, 1, axis=1)]
    ppermute x10 -> x0, local copies, waits for them, and re-layouts: 4.13 us -> none  [the longest x4 1.46 us: padded_2(): after = lax.ppermute(first, axis, down)]
  transfers between devices with their start and end apart: 20 -> 7, of which waited for: 11 -> 2; matrix products, arithmetic and copies ran while one was open for 13% -> 0% of each run, Pallas kernels for 0% -> 3%
where the time goes in v1:
time: 28.6 us; the launch traced here: 28.3 us
  starting transfers between devices  16.1 us (56%)
  Pallas kernels  4.57 us (16%)
  waiting for transfers between devices  4.27 us (15%)
  local copies, waits for them, and re-layouts  3.31 us (12%)
    ppermute x7, starting transfers between devices, exchange(): return lax.ppermute(value, axis, pairs)  16.1 us
    ppermute x7, waiting for transfers between devices, exchange(): return lax.ppermute(value, axis, pairs)  4.27 us
    pallas_call x1, Pallas kernels, on_device(): kernel_call(update_kernel, f32(*state.shape), [vmem_spec()] * 8, scratch=...  3.53 us
    unnamed x16, local copies, waits for them, and re-layouts  2.59 us
    slice x1, local copies, waits for them, and re-layouts, on_device(): surface = lax.slice_in_dim(state, 0, 1, axis=1)  0.72 us
  transfers between devices with their start and end apart: 7, of which 2 were waited for; matrix products, arithmetic and copies ran while one was open for 0% of the time, Pallas kernels for 3%

profile of v1, /device:TPU:0, one launch (start us, length us, event | category | flops | bytes accessed | tf_op | source)
XLA Modules:
  0.0 28.3 jit_solution(6252187239895147366)
XLA Ops:
  0.0 0.0 copy-start.6
  0.0 0.7 %copy.10.land_ref.refs_1_ = s32[8,1]{1,0:T(8,128)S(1)} copy(s32[8,1]{0,1:T(1,128)} %param.12) | data formatting | bytes 64 | tf_op args[5]
  0.7 0.0 copy-done.6
  0.7 0.1 copy.11.depth_ref.refs_2_
  0.8 0.0 copy-start.3
  0.8 0.0 copy-start.5
  0.8 0.7 %slice.6.surface_ref.refs_0_ = f32[1,1,8,128]{3,2,1,0:T(8,128)S(1)} slice(f32[1,80,8,128]{3,2,1,0:T(8,128)} %state_ref.3), slice={[0:1], [0:1], [0:8], [0:128]} | slice | bytes 8192 | tf_op jit(solution)/shard_map/slice | solution.py:325
  1.5 0.0 copy-done.3
  1.6 0.0 copy-done.5
  1.6 0.0 copy-start.4
  1.6 0.2 shard_map.73
  1.7 0.5 %collective-permute-start = (f32[16,128]{1,0:T(8,128)S(1)}, f32[16,128]{1,0:T(8,128)S(1)}, u32[]{:S(2)}, u32[]{:S(2)}) collective-permute-start(f32[16,128]{1,0:T(8,128)S(1)} %shard_map.73), channel_id=1, source_target_pairs={{0,16},{16,0},{1,17},{17,1},{2,18},{18,2},{3,19},{19,3},{4,20},{20... | collective-permute-start | bytes 24584 | tf_op jit(solution)/shard_map/ppermute | solution.py:306
  2.2 0.0 copy-done.4
  2.2 0.0 copy-start
  2.2 1.0 %copy-done = f32[1,80,8,128]{3,2,1,0:T(8,128)S(1)} copy-done((f32[1,80,8,128]{3,2,1,0:T(8,128)S(1)}, f32[1,80,8,128]{3,2,1,0:T(8,128)}, u32[]{:S(2)}) %copy-start) | copy-done | bytes 327704
  3.2 0.0 copy-start.2
  3.2 0.8 %copy-done.2 = f32[1,80,80]{2,1,0:T(8,128)S(1)} copy-done((f32[1,80,80]{2,1,0:T(8,128)S(1)}, f32[1,80,80]{2,1,0:T(8,128)}, u32[]{:S(2)}) %copy-start.2) | copy-done | bytes 25624
  4.0 0.0 copy-start.1
  4.0 0.6 %shard_map.74 = (f32[40,128]{1,0:T(8,128)S(1)}, f32[4,80,128]{2,1,0:T(8,128)S(1)}, f32[4,80,128]{2,1,0:T(8,128)S(1)}, bf16[80,256]{1,0:T(8,128)(2,1)S(1)}, f32[80,128]{1,0:T(8,128)S(1)}) custom-call(f32[1,80,8,128]{3,2,1,0:T(8,128)S(1)} %copy-done, f32[1,80,80]{2,1,0:T(8,128)S(1)} %copy-done.2, f32[1,80]{1,0:T(1,128)S(1)} %copy-done.4), custom_call_target="tpu_custom_call" | custom-call | flops 400000 | bytes 900000 | tf_op jit(solution)/shard_map/pallas_call | solution.py:330
  4.5 0.0 collective-permute-done.refs_3_
  4.5 3.1 %collective-permute-start.1 = (f32[56,128]{1,0:T(8,128)S(1)}, f32[56,128]{1,0:T(8,128)S(1)}, u32[]{:S(2)}, u32[]{:S(2)}) collective-permute-start(f32[56,128]{1,0:T(8,128)S(1)} %pad_maximum_fusion.1), channel_id=1, source_target_pairs={{0,1},{1,0},{2,3},{3,2},{4,5},{5,4},{6,7},{7,6},{8,9},{9,8},{10,11... | collective-permute-start | bytes 86024 | tf_op jit(solution)/shard_map/ppermute | solution.py:306
  7.6 1.5 %collective-permute-start.3 = (f32[4,80,128]{2,1,0:T(8,128)S(1)}, f32[4,80,128]{2,1,0:T(8,128)S(1)}, u32[]{:S(2)}, u32[]{:S(2)}) collective-permute-start(f32[4,80,128]{2,1,0:T(8,128)S(1)} %get-tuple-element.11), channel_id=1, source_target_pairs={{0,4},{4,0},{8,12},{12,8},{1,5},{5,1},{9,13},{13,9},{2,6},{6,2},{1... | collective-permute-start | bytes 491528 | tf_op jit(solution)/shard_map/ppermute | solution.py:306
  9.1 0.7 %collective-permute-start.4 = (f32[4,80,128]{2,1,0:T(8,128)S(1)}, f32[4,80,128]{2,1,0:T(8,128)S(1)}, u32[]{:S(2)}, u32[]{:S(2)}) collective-permute-start(f32[4,80,128]{2,1,0:T(8,128)S(1)} %get-tuple-element.12), channel_id=1, source_target_pairs={{4,8},{8,4},{5,9},{9,5},{6,10},{10,6},{7,11},{11,7},{20,24},{24,20... | collective-permute-start | bytes 491528 | tf_op jit(solution)/shard_map/ppermute | solution.py:306
  9.8 0.0 collective-permute-done.1.refs_4_
  9.8 3.7 %collective-permute-start.2 = (f32[72,128]{1,0:T(8,128)S(1)}, f32[72,128]{1,0:T(8,128)S(1)}, u32[]{:S(2)}, u32[]{:S(2)}) collective-permute-start(f32[72,128]{1,0:T(8,128)S(1)} %pad_maximum_fusion), channel_id=1, source_target_pairs={{0,3},{1,2},{2,1},{3,0},{4,7},{5,6},{6,5},{7,4},{8,11},{9,10},{10,... | collective-permute-start | bytes 110600 | tf_op jit(solution)/shard_map/ppermute | solution.py:306
  13.5 2.1 %collective-permute-done.2.refs_5_ = f32[72,128]{1,0:T(8,128)S(1)} collective-permute-done((f32[72,128]{1,0:T(8,128)S(1)}, f32[72,128]{1,0:T(8,128)S(1)}, u32[]{:S(2)}, u32[]{:S(2)}) %collective-permute-start.2) | collective-permute-done | bytes 36896 | tf_op jit(solution)/shard_map/ppermute | solution.py:306
  15.6 0.3 %shard_map.75.own_ref = f32[64,128]{1,0:T(8,128)S(1)} custom-call(f32[1,1,8,128]{3,2,1,0:T(8,128)S(1)} %slice.6.surface_ref.refs_0_, s32[8,1]{1,0:T(8,128)S(1)} %copy.10.land_ref.refs_1_, s32[8,1]{1,0:T(8,128)S(1)} %copy.11.depth_ref.refs_2_, f32[16,128]{1,0:T(8,128)S(1)} %collective-permute-done.refs_3_, f32[56,128]{1,0:T(8,128)S(1)} %collective-permute-done.1.refs_4_, ...), custom_call_target="tpu_custom_call" | custom-call | flops 200000 | bytes 100000 | tf_op jit(solution)/shard_map/pallas_call | solution.py:359
  16.0 0.7 %collective-permute-start.6 = (f32[64,128]{1,0:T(8,128)S(1)}, f32[64,128]{1,0:T(8,128)S(1)}, u32[]{:S(2)}, u32[]{:S(2)}) collective-permute-start(f32[64,128]{1,0:T(8,128)S(1)} %shard_map.75.own_ref), channel_id=1, source_target_pairs={{4,8},{8,4},{5,9},{9,5},{6,10},{10,6},{7,11},{11,7},{20,24},{24,20... | collective-permute-start | bytes 98312 | tf_op jit(solution)/shard_map/ppermute | solution.py:306
  16.6 6.0 %collective-permute-start.5 = (f32[64,128]{1,0:T(8,128)S(1)}, f32[64,128]{1,0:T(8,128)S(1)}, u32[]{:S(2)}, u32[]{:S(2)}) collective-permute-start(f32[64,128]{1,0:T(8,128)S(1)} %shard_map.75.own_ref), channel_id=1, source_target_pairs={{0,4},{4,0},{8,12},{12,8},{1,5},{5,1},{9,13},{13,9},{2,6},{6,2},{1... | collective-permute-start | bytes 98312 | tf_op jit(solution)/shard_map/ppermute | solution.py:306
  22.7 0.0 collective-permute-done.6.msg2_ref
  22.7 2.1 %collective-permute-done.5.msg1_ref = f32[64,128]{1,0:T(8,128)S(1)} collective-permute-done((f32[64,128]{1,0:T(8,128)S(1)}, f32[64,128]{1,0:T(8,128)S(1)}, u32[]{:S(2)}, u32[]{:S(2)}) %collective-permute-start.5) | collective-permute-done | bytes 32800 | tf_op jit(solution)/shard_map/ppermute | solution.py:306
  24.8 0.0 collective-permute-done.3.rows1_ref
  24.8 0.0 collective-permute-done.4.rows2_ref
  24.8 0.0 copy-done.1
  24.8 3.5 %shard_map.76 = f32[1,80,8,128]{3,2,1,0:T(8,128)} custom-call(f32[1,80,8,128]{3,2,1,0:T(8,128)S(1)} %copy-done.1, f32[64,128]{1,0:T(8,128)S(1)} %shard_map.75.own_ref, f32[4,80,128]{2,1,0:T(8,128)S(1)} %collective-permute-done.3.rows1_ref, f32[4,80,128]{2,1,0:T(8,128)S(1)} %collective-permute-done.4.rows2_ref, ...), custom_call_target="tpu_custom_call" | custom-call | flops 300000000 | bytes 1500000 | tf_op jit(solution)/shard_map/pallas_call | solution.py:368
  (3 shorter events, 0.0 us)
Async XLA Ops:
  0.0 0.7 %copy-start.6 = (s32[8,1]{0,1:T(1,128)S(1)}, s32[8,1]{0,1:T(1,128)}, u32[]{:S(2)}) copy-start(s32[8,1]{0,1:T(1,128)} %param.13) | copy-start | bytes 100
  0.8 0.7 %copy-start.3 = (s32[1,1,1,4,8]{4,3,2,1,0:T(4,128)S(1)}, s32[1,1,1,4,8]{4,3,2,1,0:T(4,128)}, u32[]{:S(2)}) copy-start(s32[1,1,1,4,8]{4,3,2,1,0:T(4,128)} %links_ref.1) | copy-start | bytes 388
  0.8 0.7 %copy-start.5 = (f32[1,64]{1,0:T(1,128)S(1)}, f32[1,64]{1,0:T(1,128)}, u32[]{:S(2)}) copy-start(f32[1,64]{1,0:T(1,128)} %weights_ref.1) | copy-start | bytes 772
  1.6 0.7 %copy-start.4 = (f32[1,80]{1,0:T(1,128)S(1)}, f32[1,80]{1,0:T(1,128)}, u32[]{:S(2)}) copy-start(f32[1,80]{1,0:T(1,128)} %diffuse_ref.1) | copy-start | bytes 964
  1.7 2.8 %collective-permute-start = (f32[16,128]{1,0:T(8,128)S(1)}, f32[16,128]{1,0:T(8,128)S(1)}, u32[]{:S(2)}, u32[]{:S(2)}) collective-permute-start(f32[16,128]{1,0:T(8,128)S(1)} %shard_map.73), channel_id=1, source_target_pairs={{0,16},{16,0},{1,17},{17,1},{2,18},{18,2},{3,19},{19,3},{4,20},{20... | collective-permute-start | bytes 24584 | tf_op jit(solution)/shard_map/ppermute | solution.py:306
  2.2 1.0 %copy-start = (f32[1,80,8,128]{3,2,1,0:T(8,128)S(1)}, f32[1,80,8,128]{3,2,1,0:T(8,128)}, u32[]{:S(2)}) copy-start(f32[1,80,8,128]{3,2,1,0:T(8,128)} %state_ref.3) | copy-start | bytes 983044
  3.2 0.8 %copy-start.2 = (f32[1,80,80]{2,1,0:T(8,128)S(1)}, f32[1,80,80]{2,1,0:T(8,128)}, u32[]{:S(2)}) copy-start(f32[1,80,80]{2,1,0:T(8,128)} %mixing_ref.1) | copy-start | bytes 76804
  4.0 20.9 %copy-start.1 = (f32[1,80,8,128]{3,2,1,0:T(8,128)S(1)}, f32[1,80,8,128]{3,2,1,0:T(8,128)}, u32[]{:S(2)}) copy-start(f32[1,80,8,128]{3,2,1,0:T(8,128)} %state_ref.3) | copy-start | bytes 983044
  4.5 5.2 %collective-permute-start.1 = (f32[56,128]{1,0:T(8,128)S(1)}, f32[56,128]{1,0:T(8,128)S(1)}, u32[]{:S(2)}, u32[]{:S(2)}) collective-permute-start(f32[56,128]{1,0:T(8,128)S(1)} %pad_maximum_fusion.1), channel_id=1, source_target_pairs={{0,1},{1,0},{2,3},{3,2},{4,5},{5,4},{6,7},{7,6},{8,9},{9,8},{10,11... | collective-permute-start | bytes 86024 | tf_op jit(solution)/shard_map/ppermute | solution.py:306
  7.6 17.2 %collective-permute-start.3 = (f32[4,80,128]{2,1,0:T(8,128)S(1)}, f32[4,80,128]{2,1,0:T(8,128)S(1)}, u32[]{:S(2)}, u32[]{:S(2)}) collective-permute-start(f32[4,80,128]{2,1,0:T(8,128)S(1)} %get-tuple-element.11), channel_id=1, source_target_pairs={{0,4},{4,0},{8,12},{12,8},{1,5},{5,1},{9,13},{13,9},{2,6},{6,2},{1... | collective-permute-start | bytes 491528 | tf_op jit(solution)/shard_map/ppermute | solution.py:306
  9.1 15.7 %collective-permute-start.4 = (f32[4,80,128]{2,1,0:T(8,128)S(1)}, f32[4,80,128]{2,1,0:T(8,128)S(1)}, u32[]{:S(2)}, u32[]{:S(2)}) collective-permute-start(f32[4,80,128]{2,1,0:T(8,128)S(1)} %get-tuple-element.12), channel_id=1, source_target_pairs={{4,8},{8,4},{5,9},{9,5},{6,10},{10,6},{7,11},{11,7},{20,24},{24,20... | collective-permute-start | bytes 491528 | tf_op jit(solution)/shard_map/ppermute | solution.py:306
  9.8 5.8 %collective-permute-start.2 = (f32[72,128]{1,0:T(8,128)S(1)}, f32[72,128]{1,0:T(8,128)S(1)}, u32[]{:S(2)}, u32[]{:S(2)}) collective-permute-start(f32[72,128]{1,0:T(8,128)S(1)} %pad_maximum_fusion), channel_id=1, source_target_pairs={{0,3},{1,2},{2,1},{3,0},{4,7},{5,6},{6,5},{7,4},{8,11},{9,10},{10,... | collective-permute-start | bytes 110600 | tf_op jit(solution)/shard_map/ppermute | solution.py:306
  16.0 6.7 %collective-permute-start.6 = (f32[64,128]{1,0:T(8,128)S(1)}, f32[64,128]{1,0:T(8,128)S(1)}, u32[]{:S(2)}, u32[]{:S(2)}) collective-permute-start(f32[64,128]{1,0:T(8,128)S(1)} %shard_map.75.own_ref), channel_id=1, source_target_pairs={{4,8},{8,4},{5,9},{9,5},{6,10},{10,6},{7,11},{11,7},{20,24},{24,20... | collective-permute-start | bytes 98312 | tf_op jit(solution)/shard_map/ppermute | solution.py:306
  16.6 8.2 %collective-permute-start.5 = (f32[64,128]{1,0:T(8,128)S(1)}, f32[64,128]{1,0:T(8,128)S(1)}, u32[]{:S(2)}, u32[]{:S(2)}) collective-permute-start(f32[64,128]{1,0:T(8,128)S(1)} %shard_map.75.own_ref), channel_id=1, source_target_pairs={{0,4},{4,0},{8,12},{12,8},{1,5},{5,1},{9,13},{13,9},{2,6},{6,2},{1... | collective-permute-start | bytes 98312 | tf_op jit(solution)/shard_map/ppermute | solution.py:306

commit v2 on v1

--- a/solution.py
+++ b/solution.py
@@ -10,7 +10,8 @@
 STEPS = 4
 EDGE = 8
 AXES = ("comp", "lat", "lon")
-VMEM_LIMIT = 32 * 1024 * 1024
+VMEM_LIMIT = 8 * 1024 * 1024
+FRONT_VMEM_LIMIT = 4 * 1024 * 1024
 
 coupling_rate = 0.5
 
@@ -41,10 +42,30 @@
     return jnp.sum(jnp.where(mine, column, 0.0), axis=0, keepdims=True)
 
 
-def pack_kernel(surface_ref, links_ref, weights_ref, land_ref, depth_ref, out_ref):
-    surface = surface_ref[0, 0]
+def pack_kernel(
+    state_hbm, weights_hbm, links_hbm, land_hbm, depth_hbm,
+    out_ref, block_ref, surface_ref, links_ref, weights_ref, land_ref, depth_ref, sems,
+):
+    copies = [
+        pltpu.make_async_copy(source, target, sems.at[k])
+        for k, (source, target) in enumerate(
+            (
+                (links_hbm.at[0, 0, 0], links_ref),
+                (weights_hbm, weights_ref),
+                (land_hbm, land_ref),
+                (depth_hbm, depth_ref),
+                (state_hbm.at[0, 0], surface_ref),
+                (state_hbm.at[0], block_ref),
+            )
+        )
+    ]
+    for copy in copies:
+        copy.start()
+    for copy in copies[:-1]:
+        copy.wait()
+    surface = surface_ref[...]
     rows = surface.shape[0]
-    table = links_ref[0, 0, 0].astype(jnp.float32)
+    table = links_ref[...].astype(jnp.float32)
     count = table.shape[1]
     source = as_column(table[0:1])
     weight_id = as_column(table[3:4])
@@ -62,24 +83,37 @@
     diagonal = lax.broadcasted_iota(jnp.int32, (count, 128), 0) == lane_ids((count, 128))
     weight_row = jnp.sum(jnp.where(diagonal, weight, 0.0), axis=0, keepdims=True)
     code_row = jnp.sum(jnp.where(diagonal, as_column(code), 0.0), axis=0, keepdims=True)
-    land = land_ref[...].astype(jnp.float32)
-    deep = land * depth_ref[...].astype(jnp.float32)
+    land = as_column(land_ref[...].astype(jnp.float32))
+    deep = land * as_column(depth_ref[...].astype(jnp.float32))
     out_ref[count : count + 1] = code_row
     out_ref[count + 1 : count + 2] = weight_row
     out_ref[count + 2 : count + 3] = spread(land)
     out_ref[count + 3 : count + 4] = spread(deep)
     out_ref[count + 4 :] = jnp.zeros((4, 128), jnp.float32)
-
-
-def edge_kernel(state_ref, mixing_ref, diffuse_ref, edge_ref, first_ref, second_ref, mix_ref, rate_ref):
-    levels, rows, cells = state_ref.shape[1:]
+    copies[-1].wait()
+
+
+def operator_kernel(mixing_ref, diffuse_ref, mix_ref, rate_ref):
+    levels = mixing_ref.shape[1]
+    mix = mixing_ref[0]
+    top = mix.astype(jnp.bfloat16)
+    rest = (mix - top.astype(jnp.float32)).astype(jnp.bfloat16)
+    mix_ref[...] = jnp.zeros_like(mix_ref)
+    mix_ref[:, 0:levels] = top
+    mix_ref[:, levels : 2 * levels] = top
+    mix_ref[:, 2 * levels : 3 * levels] = rest
+    rate_ref[...] = jnp.broadcast_to(as_column(diffuse_ref[...]), rate_ref.shape)
+
+
+def edge_kernel(state_ref, edge_ref, first_ref, second_ref):
+    levels, rows, cells = state_ref.shape
     half = levels // 2
     odd = lax.rem(lax.axis_index("lat"), 2) == 1
     lane = lane_ids((levels, 128))
     packed = jnp.zeros((levels, 128), jnp.float32)
     tiles = []
     for row in range(rows):
-        tile = state_ref[0, :, row, :]
+        tile = state_ref[:, row, :]
         tiles.append(tile)
         start = row * EDGE
         packed = jnp.where((lane >= start) & (lane < start + 4), roll(tile, start), packed)
@@ -89,19 +123,11 @@
         low, high = tiles[k], tiles[rows - 4 + k]
         first_ref[k] = jnp.where(odd, low, high)
         second_ref[k] = jnp.where(odd, high, low)
-    mix = mixing_ref[0]
-    top = mix.astype(jnp.bfloat16)
-    rest = (mix - top.astype(jnp.float32)).astype(jnp.bfloat16)
-    mix_ref[...] = jnp.zeros_like(mix_ref)
-    mix_ref[:, 0:levels] = top
-    mix_ref[:, levels : 2 * levels] = top
-    mix_ref[:, 2 * levels : 3 * levels] = rest
-    rate_ref[...] = jnp.broadcast_to(as_column(diffuse_ref[...]), rate_ref.shape)
 
 
 def flux_kernel(count, slices, east_west, *refs):
-    surface_ref, land_ref, depth_ref, *packs, out_ref = refs
-    surface = surface_ref[0, 0]
+    surface_ref, *packs, out_ref = refs
+    surface = surface_ref[0]
     rows = surface.shape[0]
     half = out_ref.shape[0] - 2 * rows - 8
     lon, lon_count = lax.axis_index("lon"), lax.axis_size("lon")
@@ -129,8 +155,13 @@
             hit * ref[offset + count + 1 : offset + count + 2, 0:count], axis=1, keepdims=True
         )
     imported = accum / jnp.maximum(totals, 1.0)
-    land = land_ref[...].astype(jnp.float32)
-    deep = land * depth_ref[...].astype(jnp.float32)
+    here_which, here_at = slices[0]
+    own_rows = packs[here_which]
+    at = here_at + count + 2
+    spread_rows = own_rows[at : at + 2]
+    column = lax.broadcasted_iota(jnp.int32, (rows, 128), 0) * EDGE == lane_ids((rows, 128))
+    land = jnp.sum(jnp.where(column, spread_rows[0:1], 0.0), axis=1, keepdims=True)
+    deep = jnp.sum(jnp.where(column, spread_rows[1:2], 0.0), axis=1, keepdims=True)
     all_levels = float(2 * half)
     deep = jnp.where(ocean, deep, all_levels)
     (first, first_at), (second, second_at) = east_west
@@ -165,19 +196,21 @@
 def update_kernel(
     state_ref, own_ref, rows1_ref, rows2_ref, msg1_ref, msg2_ref, mix_ref, rate_ref, out_ref, x_ref, y_ref
 ):
-    levels, rows, cells = state_ref.shape[1:]
+    levels, rows, cells = state_ref.shape
     half = levels // 2
     slots = rows + 2 * STEPS
-    odd = lax.rem(lax.axis_index("lat"), 2) == 1
+    lat = lax.axis_index("lat")
+    odd = lax.rem(lat, 2) == 1
+    inside = (lat > 0) & (lat < lax.axis_size("lat") - 1)
     own = own_ref[...]
-    one, two = msg1_ref[...], msg2_ref[...]
+    one, two = msg1_ref[...], jnp.where(inside, msg2_ref[...], 0.0)
     top, bottom = jnp.where(odd, one, two), jnp.where(odd, two, one)
     first_at = jnp.where(odd, 0, rows + STEPS)
     for k in range(STEPS):
         x_ref[first_at + k] = rows1_ref[k]
-        x_ref[rows + STEPS - first_at + k] = rows2_ref[k]
+        x_ref[rows + STEPS - first_at + k] = jnp.where(inside, rows2_ref[k], 0.0)
     for row in range(rows):
-        x_ref[STEPS + row] = state_ref[0, :, row, :]
+        x_ref[STEPS + row] = state_ref[:, row, :]
 
     def per_slot(value, at, slot):
         if slot < STEPS:
@@ -284,14 +317,15 @@
         source, target = target, source
 
 
-def kernel_call(body, out_shape, blocks, scratch=(), flops=0, nbytes=0):
+def kernel_call(body, out_shape, blocks, scratch=(), flops=0, nbytes=0, vmem=VMEM_LIMIT, grid=()):
     return pl.pallas_call(
         body,
         out_shape=out_shape,
+        grid=grid,
         in_specs=blocks,
         out_specs=jax.tree.map(lambda _: vmem_spec(), out_shape),
         scratch_shapes=scratch,
-        compiler_params=pltpu.CompilerParams(vmem_limit_bytes=VMEM_LIMIT),
+        compiler_params=pltpu.CompilerParams(vmem_limit_bytes=vmem),
         cost_estimate=pl.CostEstimate(flops=flops, bytes_accessed=nbytes, transcendentals=0),
     )
 
@@ -311,60 +345,77 @@
     half = levels // 2
     count = links.shape[-1]
     pack_rows = count + 8
-    lon_count = lax.axis_size("lon")
+    lat_count, lon_count = lax.axis_size("lat"), lax.axis_size("lon")
 
     def near(i):
         return i ^ 1
 
-    def far(i):
-        return i - 1 if i % 2 == 0 else i + 1
-
     def far_round(i):
-        return far(i) % lon_count
-
-    surface = lax.slice_in_dim(state, 0, 1, axis=1)
-    pack = kernel_call(
-        pack_kernel, f32(pack_rows, 128), [vmem_spec()] * 5, flops=20000, nbytes=20000
-    )(surface, links, weights, land, depth)
+        return (i - 1 if i % 2 == 0 else i + 1) % lon_count
+
+    def far_lat(i):
+        return (i - 1 if i % 2 == 0 else i + 1) % lat_count
+
+    in_hbm = pl.BlockSpec(memory_space=pltpu.HBM)
+    pack, block = kernel_call(
+        pack_kernel,
+        (f32(pack_rows, 128), f32(levels, rows, cells)),
+        [in_hbm] * 5,
+        scratch=[
+            pltpu.VMEM((rows, cells), jnp.float32),
+            pltpu.VMEM((4, count), jnp.int32),
+            pltpu.VMEM((1, weights.shape[1]), jnp.float32),
+            pltpu.VMEM((1, rows), jnp.int32),
+            pltpu.VMEM((1, rows), jnp.int32),
+            pltpu.SemaphoreType.DMA((6,)),
+        ],
+        flops=2_000_000_000,
+        nbytes=700_000,
+        vmem=FRONT_VMEM_LIMIT,
+    )(state, weights, links, land.reshape(1, rows), depth.reshape(1, rows))
     crossed = exchange(pack, "comp", near)
-    edge, up_down_1, up_down_2, mix_parts, rates = kernel_call(
+    edge, up_down_1, up_down_2 = kernel_call(
         edge_kernel,
-        (
-            f32(half, 128),
-            f32(STEPS, levels, 128),
-            f32(STEPS, levels, 128),
-            jax.ShapeDtypeStruct((levels, 256), jnp.bfloat16),
-            f32(levels, 128),
-        ),
-        [vmem_spec()] * 3,
-        flops=400000,
-        nbytes=900000,
-    )(state, mixing, diffusivity)
-    rows_1 = exchange(up_down_1, "lat", near)
-    rows_2 = exchange(up_down_2, "lat", far)
-
+        (f32(half, 128), f32(STEPS, levels, 128), f32(STEPS, levels, 128)),
+        [vmem_spec()],
+        flops=2_000_000_000,
+        nbytes=900_000,
+        vmem=FRONT_VMEM_LIMIT,
+    )(block)
+    mix_parts, rates = kernel_call(
+        operator_kernel,
+        (jax.ShapeDtypeStruct((levels, 256), jnp.bfloat16), f32(levels, 128)),
+        [vmem_spec()] * 2,
+        flops=100_000,
+        nbytes=100_000,
+        vmem=FRONT_VMEM_LIMIT,
+    )(mixing, diffusivity)
     mine = jnp.concatenate([edge, crossed], axis=0)
     beside_1 = exchange(mine, "lon", near)
+    beside_2 = exchange(mine, "lon", far_round)
+    east_west = ((1, 0), (2, 0))
     if lon_count == 4:
-        onward = jnp.concatenate([mine, beside_1[half:]], axis=0)
-        beside_2 = exchange(onward, "lon", far_round)
-        packs = [crossed, beside_1, beside_2]
-        slices = [(0, 0), (1, half), (2, half), (2, half + pack_rows)]
-        east_west = ((1, 0), (2, 0))
+        across = exchange(crossed, "lon", lambda i: i ^ 2)
+        packs = [crossed, beside_1, beside_2, across]
+        slices = [(0, 0), (1, half), (2, half), (3, 0)]
     else:
-        beside_2 = exchange(mine, "lon", far_round)
-        packs = [lax.all_gather(crossed, "lon", axis=0, tiled=True), beside_1, beside_2]
-        slices = [(0, k * pack_rows) for k in range(lon_count)]
-        east_west = ((1, 0), (2, 0))
+        packs = [crossed, beside_1, beside_2, lax.all_gather(crossed, "lon", axis=0, tiled=True)]
+        slices = [(3, k * pack_rows) for k in range(lon_count)]
+    up_down_1, up_down_2, beside_1 = lax.optimization_barrier((up_down_1, up_down_2, beside_1))
+    rows_1 = exchange(up_down_1, "lat", near)
+    rows_2 = exchange(up_down_2, "lat", far_lat)
     message = kernel_call(
         functools.partial(flux_kernel, count, slices, east_west),
         f32(half + 2 * rows + 8, 128),
-        [vmem_spec()] * (3 + len(packs)),
-        flops=200000,
-        nbytes=100000,
-    )(surface, land, depth, *packs)
+        [pl.BlockSpec((1, rows, cells), lambda i: (0, 0, 0))]
+        + [pl.BlockSpec(p.shape, lambda i: (0, 0)) for p in packs],
+        grid=(1,),
+        flops=5_000_000_000,
+        nbytes=100_000,
+        vmem=FRONT_VMEM_LIMIT,
+    )(block, *packs)
     message_1 = exchange(message, "lat", near)
-    message_2 = exchange(message, "lat", far)
+    message_2 = exchange(message, "lat", far_lat)
     return kernel_call(
         update_kernel,
         f32(*state.shape),
@@ -372,7 +423,7 @@
         scratch=[pltpu.VMEM((rows + 2 * STEPS, levels, 128), jnp.float32)] * 2,
         flops=300000000,
         nbytes=1500000,
-    )(state, message, rows_1, rows_2, message_1, message_2, mix_parts, rates)
+    )(block, message, rows_1, rows_2, message_1, message_2, mix_parts, rates)
 
 
 def solution(mesh):

time: 28.6 us -> 23.9 us (0.84)
  starting transfers between devices: 16.1 us -> 12.1 us
  local copies, waits for them, and re-layouts: 3.31 us -> 1.69 us
  waiting for transfers between devices: 4.27 us -> 5.06 us
    ppermute x7 -> x8, starting transfers between devices: 16.1 us -> 12.1 us  [exchange(): return lax.ppermute(value, axis, pairs)]
    unnamed x16 -> x15, local copies, waits for them, and re-layouts: 2.59 us -> 1.68 us
    ppermute x7 -> x8, waiting for transfers between devices: 4.27 us -> 5.06 us  [exchange(): return lax.ppermute(value, axis, pairs)]
    slice x2 -> x0, local copies, waits for them, and re-layouts: 0.72 us -> none  [the longest x1 0.72 us: on_device(): surface = lax.slice_in_dim(state, 0, 1, axis=1)]
  transfers between devices with their start and end apart: 7 -> 8, of which waited for: 2 -> 3; matrix products, arithmetic and copies ran while one was open for 0% -> 0% of each run, Pallas kernels for 3% -> 4%
where the time goes in v2:
time: 23.9 us; the launch traced here: 23.7 us
  starting transfers between devices  12.1 us (51%)
  waiting for transfers between devices  5.06 us (21%)
  Pallas kernels  4.84 us (20%)
  local copies, waits for them, and re-layouts  1.69 us (7%)
    ppermute x8, starting transfers between devices, exchange(): return lax.ppermute(value, axis, pairs)  12.1 us
    ppermute x8, waiting for transfers between devices, exchange(): return lax.ppermute(value, axis, pairs)  5.06 us
    pallas_call x1, Pallas kernels, on_device(): kernel_call(update_kernel, f32(*state.shape), [vmem_spec()] * 8, scratch=...  3.56 us
    unnamed x15, local copies, waits for them, and re-layouts  1.68 us
    pallas_call x1, Pallas kernels, on_device(): kernel_call(edge_kernel, (f32(half, 128), f32(STEPS, levels, 128), f32(ST...  0.49 us
  transfers between devices with their start and end apart: 8, of which 3 were waited for; matrix products, arithmetic and copies ran while one was open for 0% of the time, Pallas kernels for 4%

profile of v2, /device:TPU:0, one launch (start us, length us, event | category | flops | bytes accessed | tf_op | source)
XLA Modules:
  0.0 23.7 jit_solution(14770176752953200514)
XLA Ops:
  0.0 0.0 copy-start.3
  0.0 0.0 copy-start.4
  0.0 0.0 copy-start.5
  0.0 0.0 copy-start.6
  0.0 0.7 %copy-done.3 = s32[1,1,1,4,8]{4,3,2,1,0:T(4,128)S(1)} copy-done((s32[1,1,1,4,8]{4,3,2,1,0:T(4,128)S(1)}, s32[1,1,1,4,8]{4,3,2,1,0:T(4,128)}, u32[]{:S(2)}) %copy-start.3) | copy-done | bytes 152
  0.7 0.0 copy-done.4
  0.7 0.0 copy-done.5
  0.7 0.0 copy-done.6
  0.7 0.0 copy-start.2
  0.7 1.0 %copy-done.2 = f32[1,80,8,128]{3,2,1,0:T(8,128)S(1)} copy-done((f32[1,80,8,128]{3,2,1,0:T(8,128)S(1)}, f32[1,80,8,128]{3,2,1,0:T(8,128)}, u32[]{:S(2)}) %copy-start.2) | copy-done | bytes 327704
  1.7 0.3 %shard_map.73 = (f32[16,128]{1,0:T(8,128)S(1)}, f32[80,8,128]{2,1,0:T(8,128)S(1)}) custom-call(f32[1,80,8,128]{3,2,1,0:T(8,128)S(1)} %copy-done.2, f32[1,64]{1,0:T(1,128)S(1)} %copy-done.4, s32[1,1,1,4,8]{4,3,2,1,0:T(4,128)S(1)} %copy-done.3, s32[1,8]{1,0:T(1,128)S(1)} %bitcast.2, s32[1,8]{1,0:T(1,128)S(1)} %bitcast.3), custom_call_target="tpu_custom_call" | custom-call | flops 2000000000 | bytes 700000 | tf_op jit(solution)/shard_map/pallas_call | solution.py:360
  2.0 0.5 %collective-permute-start = (f32[16,128]{1,0:T(8,128)S(1)}, f32[16,128]{1,0:T(8,128)S(1)}, u32[]{:S(2)}, u32[]{:S(2)}) collective-permute-start(f32[16,128]{1,0:T(8,128)S(1)} %get-tuple-element.15), channel_id=1, source_target_pairs={{0,16},{16,0},{1,17},{17,1},{2,18},{18,2},{3,19},{19,3},{4,20},{20... | collective-permute-start | bytes 24584 | tf_op jit(solution)/shard_map/ppermute | solution.py:340
  2.5 0.5 %shard_map.74 = (f32[40,128]{1,0:T(8,128)S(1)}, f32[4,80,128]{2,1,0:T(8,128)S(1)}, f32[4,80,128]{2,1,0:T(8,128)S(1)}) custom-call(f32[80,8,128]{2,1,0:T(8,128)S(1)} %get-tuple-element.14.state_ref.refs_0_), custom_call_target="tpu_custom_call" | custom-call | flops 2000000000 | bytes 900000 | tf_op jit(solution)/shard_map/pallas_call | solution.py:377
  3.0 0.3 %collective-permute-done.refs_1_ = f32[16,128]{1,0:T(8,128)S(1)} collective-permute-done((f32[16,128]{1,0:T(8,128)S(1)}, f32[16,128]{1,0:T(8,128)S(1)}, u32[]{:S(2)}, u32[]{:S(2)}) %collective-permute-start) | collective-permute-done | bytes 8224 | tf_op jit(solution)/shard_map/ppermute | solution.py:340
  3.4 2.9 %collective-permute-start.1 = (f32[56,128]{1,0:T(8,128)S(1)}, f32[56,128]{1,0:T(8,128)S(1)}, u32[]{:S(2)}, u32[]{:S(2)}) collective-permute-start(f32[56,128]{1,0:T(8,128)S(1)} %constant_dynamic-update-slice_fusion), channel_id=1, source_target_pairs={{0,1},{1,0},{2,3},{3,2},{4,5},{5,4},{6,7},{7,6},{8,9},{9,8},{10,11... | collective-permute-start | bytes 86024 | tf_op jit(solution)/shard_map/ppermute | solution.py:340
  6.3 2.5 %collective-permute-start.2 = (f32[56,128]{1,0:T(8,128)S(1)}, f32[56,128]{1,0:T(8,128)S(1)}, u32[]{:S(2)}, u32[]{:S(2)}) collective-permute-start(f32[56,128]{1,0:T(8,128)S(1)} %constant_dynamic-update-slice_fusion), channel_id=1, source_target_pairs={{0,3},{1,2},{2,1},{3,0},{4,7},{5,6},{6,5},{7,4},{8,11},{9,10},{10,... | collective-permute-start | bytes 86024 | tf_op jit(solution)/shard_map/ppermute | solution.py:340
  8.8 0.1 collective-permute-start.3
  8.9 0.0 collective-permute-done.1.refs_2_
  8.9 0.0 copy-start
  8.9 0.0 copy-start.1
  8.9 1.5 %collective-permute-start.4 = (f32[4,80,128]{2,1,0:T(8,128)S(1)}, f32[4,80,128]{2,1,0:T(8,128)S(1)}, u32[]{:S(2)}, u32[]{:S(2)}) collective-permute-start(f32[4,80,128]{2,1,0:T(8,128)S(1)} %get-tuple-element.19), channel_id=1, source_target_pairs={{0,4},{4,0},{8,12},{12,8},{1,5},{5,1},{9,13},{13,9},{2,6},{6,2},{1... | collective-permute-start | bytes 491528 | tf_op jit(solution)/shard_map/ppermute | solution.py:340
  10.4 1.5 %collective-permute-start.5 = (f32[4,80,128]{2,1,0:T(8,128)S(1)}, f32[4,80,128]{2,1,0:T(8,128)S(1)}, u32[]{:S(2)}, u32[]{:S(2)}) collective-permute-start(f32[4,80,128]{2,1,0:T(8,128)S(1)} %get-tuple-element.20), channel_id=1, source_target_pairs={{0,12},{4,8},{8,4},{12,0},{1,13},{5,9},{9,5},{13,1},{2,14},{6,10},... | collective-permute-start | bytes 491528 | tf_op jit(solution)/shard_map/ppermute | solution.py:340
  11.9 1.4 %collective-permute-done.3.refs_4_ = f32[16,128]{1,0:T(8,128)S(1)} collective-permute-done((f32[16,128]{1,0:T(8,128)S(1)}, f32[16,128]{1,0:T(8,128)S(1)}, u32[]{:S(2)}, u32[]{:S(2)}) %collective-permute-start.3) | collective-permute-done | bytes 8224 | tf_op jit(solution)/shard_map/ppermute | solution.py:340
  13.3 0.0 collective-permute-done.2.refs_3_
  13.3 0.3 %shard_map.75.own_ref = f32[64,128]{1,0:T(8,128)S(1)} custom-call(f32[80,8,128]{2,1,0:T(8,128)S(1)} %get-tuple-element.14.state_ref.refs_0_, f32[16,128]{1,0:T(8,128)S(1)} %collective-permute-done.refs_1_, f32[56,128]{1,0:T(8,128)S(1)} %collective-permute-done.1.refs_2_, f32[56,128]{1,0:T(8,128)S(1)} %collective-permute-done.2.refs_3_, ...), custom_call_target="tpu_custom_call" | custom-call | flops 5000000000 | bytes 100000 | tf_op jit(solution)/shard_map/pallas_call | solution.py:407
  13.7 2.5 %collective-permute-start.7 = (f32[64,128]{1,0:T(8,128)S(1)}, f32[64,128]{1,0:T(8,128)S(1)}, u32[]{:S(2)}, u32[]{:S(2)}) collective-permute-start(f32[64,128]{1,0:T(8,128)S(1)} %shard_map.75.own_ref), channel_id=1, source_target_pairs={{0,12},{4,8},{8,4},{12,0},{1,13},{5,9},{9,5},{13,1},{2,14},{6,10},... | collective-permute-start | bytes 98312 | tf_op jit(solution)/shard_map/ppermute | solution.py:340
  16.2 0.5 %collective-permute-start.6 = (f32[64,128]{1,0:T(8,128)S(1)}, f32[64,128]{1,0:T(8,128)S(1)}, u32[]{:S(2)}, u32[]{:S(2)}) collective-permute-start(f32[64,128]{1,0:T(8,128)S(1)} %shard_map.75.own_ref), channel_id=1, source_target_pairs={{0,4},{4,0},{8,12},{12,8},{1,5},{5,1},{9,13},{13,9},{2,6},{6,2},{1... | collective-permute-start | bytes 98312 | tf_op jit(solution)/shard_map/ppermute | solution.py:340
  16.7 0.0 copy-done
  16.7 0.0 copy-done.1
  16.7 0.1 shard_map.76
  16.8 3.3 %collective-permute-done.7.msg2_ref = f32[64,128]{1,0:T(8,128)S(1)} collective-permute-done((f32[64,128]{1,0:T(8,128)S(1)}, f32[64,128]{1,0:T(8,128)S(1)}, u32[]{:S(2)}, u32[]{:S(2)}) %collective-permute-start.7) | collective-permute-done | bytes 32800 | tf_op jit(solution)/shard_map/ppermute | solution.py:340
  20.1 0.0 collective-permute-done.6.msg1_ref
  20.1 0.0 collective-permute-done.4.rows1_ref
  20.2 0.0 collective-permute-done.5.rows2_ref
  20.2 3.6 %shard_map.77 = f32[1,80,8,128]{3,2,1,0:T(8,128)} custom-call(f32[80,8,128]{2,1,0:T(8,128)S(1)} %get-tuple-element.14.state_ref.refs_0_, f32[64,128]{1,0:T(8,128)S(1)} %shard_map.75.own_ref, f32[4,80,128]{2,1,0:T(8,128)S(1)} %collective-permute-done.4.rows1_ref, f32[4,80,128]{2,1,0:T(8,128)S(1)} %collective-permute-done.5.rows2_ref, ...), custom_call_target="tpu_custom_call" | custom-call | flops 300000000 | bytes 1500000 | tf_op jit(solution)/shard_map/pallas_call | solution.py:419
  (2 shorter events, 0.0 us)
Async XLA Ops:
  0.0 0.7 %copy-start.3 = (s32[1,1,1,4,8]{4,3,2,1,0:T(4,128)S(1)}, s32[1,1,1,4,8]{4,3,2,1,0:T(4,128)}, u32[]{:S(2)}) copy-start(s32[1,1,1,4,8]{4,3,2,1,0:T(4,128)} %links_hbm.1) | copy-start | bytes 388
  0.0 0.7 %copy-start.4 = (f32[1,64]{1,0:T(1,128)S(1)}, f32[1,64]{1,0:T(1,128)}, u32[]{:S(2)}) copy-start(f32[1,64]{1,0:T(1,128)} %weights_hbm.1) | copy-start | bytes 772
  0.0 0.7 %copy-start.5 = (s32[8,1]{0,1:T(1,128)S(1)}, s32[8,1]{0,1:T(1,128)}, u32[]{:S(2)}) copy-start(s32[8,1]{0,1:T(1,128)} %param.12) | copy-start | bytes 100
  0.0 0.7 %copy-start.6 = (s32[8,1]{0,1:T(1,128)S(1)}, s32[8,1]{0,1:T(1,128)}, u32[]{:S(2)}) copy-start(s32[8,1]{0,1:T(1,128)} %param.13) | copy-start | bytes 100
  0.7 1.0 %copy-start.2 = (f32[1,80,8,128]{3,2,1,0:T(8,128)S(1)}, f32[1,80,8,128]{3,2,1,0:T(8,128)}, u32[]{:S(2)}) copy-start(f32[1,80,8,128]{3,2,1,0:T(8,128)} %state_hbm.1) | copy-start | bytes 983044
  2.0 1.3 %collective-permute-start = (f32[16,128]{1,0:T(8,128)S(1)}, f32[16,128]{1,0:T(8,128)S(1)}, u32[]{:S(2)}, u32[]{:S(2)}) collective-permute-start(f32[16,128]{1,0:T(8,128)S(1)} %get-tuple-element.15), channel_id=1, source_target_pairs={{0,16},{16,0},{1,17},{17,1},{2,18},{18,2},{3,19},{19,3},{4,20},{20... | collective-permute-start | bytes 24584 | tf_op jit(solution)/shard_map/ppermute | solution.py:340
  3.4 5.5 %collective-permute-start.1 = (f32[56,128]{1,0:T(8,128)S(1)}, f32[56,128]{1,0:T(8,128)S(1)}, u32[]{:S(2)}, u32[]{:S(2)}) collective-permute-start(f32[56,128]{1,0:T(8,128)S(1)} %constant_dynamic-update-slice_fusion), channel_id=1, source_target_pairs={{0,1},{1,0},{2,3},{3,2},{4,5},{5,4},{6,7},{7,6},{8,9},{9,8},{10,11... | collective-permute-start | bytes 86024 | tf_op jit(solution)/shard_map/ppermute | solution.py:340
  6.3 7.0 %collective-permute-start.2 = (f32[56,128]{1,0:T(8,128)S(1)}, f32[56,128]{1,0:T(8,128)S(1)}, u32[]{:S(2)}, u32[]{:S(2)}) collective-permute-start(f32[56,128]{1,0:T(8,128)S(1)} %constant_dynamic-update-slice_fusion), channel_id=1, source_target_pairs={{0,3},{1,2},{2,1},{3,0},{4,7},{5,6},{6,5},{7,4},{8,11},{9,10},{10,... | collective-permute-start | bytes 86024 | tf_op jit(solution)/shard_map/ppermute | solution.py:340
  8.8 4.5 %collective-permute-start.3 = (f32[16,128]{1,0:T(8,128)S(1)}, f32[16,128]{1,0:T(8,128)S(1)}, u32[]{:S(2)}, u32[]{:S(2)}) collective-permute-start(f32[16,128]{1,0:T(8,128)S(1)} %collective-permute-done.refs_1_), channel_id=1, source_target_pairs={{0,2},{1,3},{2,0},{3,1},{4,6},{5,7},{6,4},{7,5},{8,10},{9,11},{10,... | collective-permute-start | bytes 24584 | tf_op jit(solution)/shard_map/ppermute | solution.py:340
  8.9 7.8 %copy-start = (f32[1,80,80]{2,1,0:T(8,128)S(1)}, f32[1,80,80]{2,1,0:T(8,128)}, u32[]{:S(2)}) copy-start(f32[1,80,80]{2,1,0:T(8,128)} %mixing_ref.1) | copy-start | bytes 76804
  8.9 7.8 %copy-start.1 = (f32[1,80]{1,0:T(1,128)S(1)}, f32[1,80]{1,0:T(1,128)}, u32[]{:S(2)}) copy-start(f32[1,80]{1,0:T(1,128)} %diffuse_ref.1) | copy-start | bytes 964
  8.9 11.3 %collective-permute-start.4 = (f32[4,80,128]{2,1,0:T(8,128)S(1)}, f32[4,80,128]{2,1,0:T(8,128)S(1)}, u32[]{:S(2)}, u32[]{:S(2)}) collective-permute-start(f32[4,80,128]{2,1,0:T(8,128)S(1)} %get-tuple-element.19), channel_id=1, source_target_pairs={{0,4},{4,0},{8,12},{12,8},{1,5},{5,1},{9,13},{13,9},{2,6},{6,2},{1... | collective-permute-start | bytes 491528 | tf_op jit(solution)/shard_map/ppermute | solution.py:340
  10.4 9.7 %collective-permute-start.5 = (f32[4,80,128]{2,1,0:T(8,128)S(1)}, f32[4,80,128]{2,1,0:T(8,128)S(1)}, u32[]{:S(2)}, u32[]{:S(2)}) collective-permute-start(f32[4,80,128]{2,1,0:T(8,128)S(1)} %get-tuple-element.20), channel_id=1, source_target_pairs={{0,12},{4,8},{8,4},{12,0},{1,13},{5,9},{9,5},{13,1},{2,14},{6,10},... | collective-permute-start | bytes 491528 | tf_op jit(solution)/shard_map/ppermute | solution.py:340
  13.7 6.5 %collective-permute-start.7 = (f32[64,128]{1,0:T(8,128)S(1)}, f32[64,128]{1,0:T(8,128)S(1)}, u32[]{:S(2)}, u32[]{:S(2)}) collective-permute-start(f32[64,128]{1,0:T(8,128)S(1)} %shard_map.75.own_ref), channel_id=1, source_target_pairs={{0,12},{4,8},{8,4},{12,0},{1,13},{5,9},{9,5},{13,1},{2,14},{6,10},... | collective-permute-start | bytes 98312 | tf_op jit(solution)/shard_map/ppermute | solution.py:340
  16.2 4.0 %collective-permute-start.6 = (f32[64,128]{1,0:T(8,128)S(1)}, f32[64,128]{1,0:T(8,128)S(1)}, u32[]{:S(2)}, u32[]{:S(2)}) collective-permute-start(f32[64,128]{1,0:T(8,128)S(1)} %shard_map.75.own_ref), channel_id=1, source_target_pairs={{0,4},{4,0},{8,12},{12,8},{1,5},{5,1},{9,13},{13,9},{2,6},{6,2},{1... | collective-permute-start | bytes 98312 | tf_op jit(solution)/shard_map/ppermute | solution.py:340

commit v3 on v2

v3 whole, which is shorter than its diff:
```python
import functools

import jax
import jax.numpy as jnp
from jax import lax
from jax.experimental import pallas as pl
from jax.experimental.pallas import tpu as pltpu
from jax.sharding import PartitionSpec as P

STEPS = 4
EDGE = 8
AXES = ("comp", "lat", "lon")
VMEM_LIMIT = 8 * 1024 * 1024
FRONT_VMEM_LIMIT = 4 * 1024 * 1024

coupling_rate = 0.5


def vmem_spec():
    return pl.BlockSpec(memory_space=pltpu.VMEM)


def lane_ids(shape):
    return lax.broadcasted_iota(jnp.int32, shape, len(shape) - 1)


def roll(value, shift):
    shift = shift % value.shape[-1]
    return value if shift == 0 else pltpu.roll(value, shift, 1)


def as_column(row):
    n = row.shape[1]
    diagonal = lax.broadcasted_iota(jnp.int32, (n, n), 0) == lane_ids((n, n))
    return jnp.sum(jnp.where(diagonal, row, 0.0), axis=1, keepdims=True)


def spread(column):
    rows = column.shape[0]
    shape = (rows, 128)
    mine = lane_ids(shape) // EDGE == lax.broadcasted_iota(jnp.int32, shape, 0)
    return jnp.sum(jnp.where(mine, column, 0.0), axis=0, keepdims=True)


def zero_kernel(out_ref):
    out_ref[...] = jnp.zeros_like(out_ref)


def pack_kernel(state_ref, weights_ref, links_ref, land_ref, depth_ref, zero_ref, out_ref):
    surface = state_ref[0, 0]
    rows = surface.shape[0]
    table = links_ref[0, 0, 0].astype(jnp.float32)
    count = table.shape[1]
    source = as_column(table[0:1])
    weight_id = as_column(table[3:4])
    entries = weights_ref.shape[1]
    weight = jnp.sum(
        jnp.where(weight_id == lane_ids((count, entries)).astype(jnp.float32), weights_ref[...], 0.0),
        axis=1,
        keepdims=True,
    )
    picked = jnp.zeros((count, surface.shape[1]), jnp.float32)
    for row in range(rows):
        picked = jnp.where(source == float(row), surface[row : row + 1], picked)
    out_ref[0:count] = weight * picked
    code = table[1:2] * float(rows) + table[2:3]
    diagonal = lax.broadcasted_iota(jnp.int32, (count, 128), 0) == lane_ids((count, 128))
    weight_row = jnp.sum(jnp.where(diagonal, weight, 0.0), axis=0, keepdims=True)
    code_row = jnp.sum(jnp.where(diagonal, as_column(code), 0.0), axis=0, keepdims=True)
    land = as_column(land_ref[...].astype(jnp.float32))
    deep = land * as_column(depth_ref[...].astype(jnp.float32))
    out_ref[count : count + 1] = code_row
    out_ref[count + 1 : count + 2] = weight_row
    out_ref[count + 2 : count + 3] = spread(land)
    out_ref[count + 3 : count + 4] = spread(deep)
    out_ref[count + 4 :] = zero_ref[0:4]


def operator_kernel(mixing_ref, diffuse_ref, mix_ref, rate_ref):
    levels = mixing_ref.shape[1]
    mix = mixing_ref[0]
    top = mix.astype(jnp.bfloat16)
    rest = (mix - top.astype(jnp.float32)).astype(jnp.bfloat16)
    mix_ref[...] = jnp.zeros_like(mix_ref)
    mix_ref[:, 0:levels] = top
    mix_ref[:, levels : 2 * levels] = top
    mix_ref[:, 2 * levels : 3 * levels] = rest
    rate = jnp.broadcast_to(as_column(diffuse_ref[...]), (levels, 128))
    rate_ref[0] = rate
    rate_ref[1] = 1.0 - 4.0 * rate


def edge_kernel(state_ref, edge_ref, first_ref, second_ref, surface_ref):
    levels, rows, cells = state_ref.shape[1:]
    surface_ref[...] = state_ref[0, 0]
    half = levels // 2
    odd = lax.rem(lax.axis_index("lat"), 2) == 1
    lane = lane_ids((levels, 128))
    first = last = jnp.zeros((levels, 128), jnp.float32)
    tiles = []
    for row in range(rows):
        tile = state_ref[0, :, row, :]
        tiles.append(tile)
        turned = roll(tile, row * EDGE)
        first = jnp.where(lane // EDGE == row, turned, first)
        last = jnp.where(lane // EDGE == (row - 1) % (128 // EDGE), turned, last)
    packed = jnp.where(lane % EDGE < 4, first, roll(last, EDGE))
    edge_ref[...] = jnp.where(lane_ids((half, 128)) < 64, packed[:half], roll(packed[half:], 64))
    for k in range(4):
        low, high = tiles[k], tiles[rows - 4 + k]
        first_ref[k] = jnp.where(odd, low, high)
        second_ref[k] = jnp.where(odd, high, low)


def flux_kernel(count, slices, east_west, *refs):
    surface_ref, *packs, out_ref = refs
    surface = surface_ref[...]
    rows = surface.shape[0]
    half = out_ref.shape[0] - 2 * rows - 8
    lon, lon_count = lax.axis_index("lon"), lax.axis_size("lon")
    odd = lax.rem(lon, 2) == 1
    ocean = lax.axis_index("comp") == 1
    here = lon * rows
    after = lax.rem(lon + 1, lon_count) * rows
    before = lax.rem(lon + lon_count - 1, lon_count) * rows
    index = lax.broadcasted_iota(jnp.int32, (3 * rows, count), 0)
    wanted = jnp.where(
        index < rows, here + index, jnp.where(index < 2 * rows, after + index - rows, before + index - 2 * rows)
    ).astype(jnp.float32)
    accum = jnp.zeros((3 * rows, 128), jnp.float32)
    totals = jnp.zeros((3 * rows, 1), jnp.float32)
    for which, offset in slices:
        ref = packs[which]
        hit = (wanted == ref[offset + count : offset + count + 1, 0:count]).astype(jnp.float32)
        accum += jnp.dot(
            hit,
            ref[offset : offset + count],
            precision=lax.Precision.HIGHEST,
            preferred_element_type=jnp.float32,
        )
        totals += jnp.sum(
            hit * ref[offset + count + 1 : offset + count + 2, 0:count], axis=1, keepdims=True
        )
    imported = accum / jnp.maximum(totals, 1.0)
    here_which, here_at = slices[0]
    own_rows = packs[here_which]
    at = here_at + count + 2
    spread_rows = own_rows[at : at + 2]
    column = lax.broadcasted_iota(jnp.int32, (rows, 128), 0) * EDGE == lane_ids((rows, 128))
    land = jnp.sum(jnp.where(column, spread_rows[0:1], 0.0), axis=1, keepdims=True)
    deep = jnp.sum(jnp.where(column, spread_rows[1:2], 0.0), axis=1, keepdims=True)
    all_levels = float(2 * half)
    deep = jnp.where(ocean, deep, all_levels)
    (first, first_at), (second, second_at) = east_west
    lane = lane_ids((1, 128))
    from_east = lax.rem(lane, EDGE) < 4

    def beside(offset_rows, size):
        one = packs[first][first_at + offset_rows : first_at + offset_rows + size]
        two = packs[second][second_at + offset_rows : second_at + offset_rows + size]
        east_is_one = lane_ids((size, 128)) % EDGE < 4
        return jnp.where(east_is_one != odd, one, two)

    middle = beside(0, half)
    land_beside = beside(half + count + 2, 1)
    deep_beside = jnp.where(ocean, beside(half + count + 3, 1), all_levels)
    imported_beside = jnp.zeros((1, 128), jnp.float32)
    for row in range(rows):
        start = row * EDGE
        east = roll(imported[rows + row : rows + row + 1], start)
        west = roll(imported[2 * rows + row : 2 * rows + row + 1], start + 8)
        mine = (lane >= start) & (lane < start + EDGE)
        imported_beside = jnp.where(mine, jnp.where(from_east, east, west), imported_beside)
    flux_beside = coupling_rate * land_beside * (imported_beside - middle[0:1])
    out_ref[0:half] = middle
    out_ref[half : half + rows] = coupling_rate * land * (imported[0:rows] - surface)
    out_ref[half + rows : half + 2 * rows] = jnp.broadcast_to(deep, (rows, 128))
    out_ref[half + 2 * rows : half + 2 * rows + 1] = flux_beside
    out_ref[half + 2 * rows + 1 : half + 2 * rows + 2] = deep_beside
    out_ref[half + 2 * rows + 2 :] = jnp.zeros((6, 128), jnp.float32)


def halves(value):
    hi = value.astype(jnp.bfloat16)
    return hi, (value - hi.astype(jnp.float32)).astype(jnp.bfloat16)


class Update:
    def __init__(self, mix_ref, rate_ref):
        self.mixer, self.rate_ref = mix_ref[...], rate_ref
        self.levels = rate_ref.shape[1]
        self.pad = jnp.zeros((self.mixer.shape[1] - 3 * self.levels, 256), jnp.bfloat16)
        tail = lax.broadcasted_iota(jnp.int32, (8, 128), 0)
        self.first = tail == 0
        self.tail = (tail + (self.levels - 8)).astype(jnp.float32)

    def moved(self, x, neighbours, flux, deep):
        value = self.rate_ref[1] * x + self.rate_ref[0] * neighbours
        head = value[:8] + jnp.where(self.first, flux, 0.0)
        tail = jnp.where(self.tail < deep, value[-8:], 0.0)
        return jnp.concatenate([head, value[8:-8], tail], axis=0)

    def mixed(self, values):
        value = jnp.concatenate(values, axis=1)
        hi, lo = halves(value)
        full = jnp.concatenate([hi, lo, hi, self.pad[:, : value.shape[1]]], axis=0)
        out = jnp.dot(self.mixer, full, preferred_element_type=jnp.float32)
        return [out[:, 128 * k : 128 * (k + 1)] for k in range(len(values))]

    def settled(self, new, x, deep):
        sea = jnp.broadcast_to(deep, (self.levels - 8, 128)) > 0.0
        body = jnp.where(sea, new[:-8], x[:-8])
        tail = jnp.where(self.tail < deep, new[-8:], x[-8:])
        return jnp.concatenate([body, tail], axis=0)

    def rows(self, tiles, flux, deep):
        values = [
            self.moved(x, above + below + roll(x, 1) + roll(x, -1), f, d)
            for (above, x, below), f, d in zip(tiles, flux, deep)
        ]
        return [self.settled(new, t[1], d) for new, t, d in zip(self.mixed(values), tiles, deep)]


def lat_place():
    lat = lax.axis_index("lat")
    return lax.rem(lat, 2) == 1, (lat > 0) & (lat < lax.axis_size("lat") - 1)


def inner_kernel(state_ref, own_ref, rows1_ref, rows2_ref, mix_ref, rate_ref, x_ref, side_ref, *inner_refs):
    levels, rows, cells = state_ref.shape[1:]
    half = levels // 2
    slots = rows + 2 * STEPS
    odd, inside = lat_place()
    first_at = jnp.where(odd, 0, rows + STEPS)
    for k in range(STEPS):
        x_ref[first_at + k] = rows1_ref[k]
        x_ref[rows + STEPS - first_at + k] = jnp.where(inside, rows2_ref[k], 0.0)
    for row in range(rows):
        x_ref[STEPS + row] = state_ref[0, :, row, :]
    update = Update(mix_ref, rate_ref)
    flux = [own_ref[half + r : half + r + 1] for r in range(rows)]
    deep = [own_ref[half + rows + r : half + rows + r + 1] for r in range(rows)]
    source, first = x_ref, 0
    for step in range(STEPS):
        target, at = inner_refs[step], STEPS + step
        for slot in range(at, slots - at, 2):
            pair = (slot, slot + 1)
            tiles = [[source[s - first + k] for k in (-1, 0, 1)] for s in pair]
            new = update.rows(tiles, [flux[s - STEPS] for s in pair], [deep[s - STEPS] for s in pair])
            for s, tile in zip(pair, new):
                target[s - at] = tile
        source, first = target, at
    lane = lane_ids((levels, 128))
    left = right = jnp.zeros((levels, 128), jnp.float32)
    for slot in range(slots):
        start = slot * EDGE
        turned = roll(x_ref[slot], start)
        right = jnp.where(lane // EDGE == slot, turned, right)
        left = jnp.where(lane // EDGE == (slot - 1) % slots, turned, left)
    side_ref[0] = roll(left, EDGE)
    side_ref[1] = right


def outer_kernel(own_ref, msg1_ref, msg2_ref, mix_ref, rate_ref, x_ref, side_ref, *refs):
    inner_refs, out_ref, outer_refs = refs[:STEPS], refs[STEPS], refs[STEPS + 1 :]
    levels, rows, cells = out_ref.shape[1:]
    half = levels // 2
    slots = rows + 2 * STEPS
    odd, inside = lat_place()
    own = own_ref[...]
    one, two = msg1_ref[...], jnp.where(inside, msg2_ref[...], 0.0)
    top, bottom = jnp.where(odd, one, two), jnp.where(odd, two, one)
    parts = (top, own, bottom)

    def per_slot(at, slot):
        if slot < STEPS:
            at, value = at + rows - STEPS + slot, top
        elif slot < STEPS + rows:
            at, value = at + slot - STEPS, own
        else:
            at, value = at + slot - STEPS - rows, bottom
        return value[at : at + 1]

    flux_rows = [per_slot(half, s) for s in range(slots)]
    deep_rows = [per_slot(half + rows, s) for s in range(slots)]
    lane1 = lane_ids((1, 128))
    lane = lane_ids((levels, 128))
    place = lane % EDGE

    def unfolded(fold):
        a, b, c = (roll(v, s) for v, s in zip(fold, (-4 * EDGE, 4 * EDGE, 12 * EDGE)))
        at = lane_ids(a.shape)
        return jnp.where(at < 4 * EDGE, a, jnp.where(at < 12 * EDGE, b, c))

    low = unfolded([v[:half] for v in parts])
    high = unfolded([roll(v[:half], 64) for v in parts])
    mid = jnp.concatenate([low, high], axis=0)
    at = half + 2 * rows
    flux_mid = unfolded([v[at : at + 1] for v in parts])
    deep_mid = unfolded([v[at + 1 : at + 2] for v in parts])
    left, right = side_ref[0], side_ref[1]
    flux_left = flux_right = deep_side = jnp.zeros((1, 128), jnp.float32)
    for slot in range(slots):
        start = slot * EDGE
        mine1 = (lane1 >= start) & (lane1 < start + EDGE)
        flux_left = jnp.where(mine1, roll(flux_rows[slot], start + EDGE), flux_left)
        flux_right = jnp.where(mine1, roll(flux_rows[slot], start), flux_right)
        deep_side = jnp.where(mine1, deep_rows[slot], deep_side)

    def strip(tile, west, east):
        around = roll(tile, EDGE) + roll(tile, -EDGE)
        to_west, to_east = roll(tile, 1), roll(tile, -1)
        if west is not None:
            to_west = jnp.where(place == 0, roll(west, 1 - EDGE), to_west)
        if east is not None:
            to_east = jnp.where(place == EDGE - 1, roll(east, EDGE - 1), to_east)
        return around + to_west + to_east

    update = Update(mix_ref, rate_ref)

    def tile_at(step, s):
        if step == 0:
            return x_ref[s]
        if 3 + step <= s <= slots - 4 - step:
            return inner_refs[step - 1][s - 3 - step]
        return outer_refs[step - 1][s - step if s < slots // 2 else s - (slots - 6 - step)]

    def put(s, tile):
        tile = jnp.where((lane < 4) | (lane >= cells - 4), roll(sides, -s * EDGE), tile)
        out_ref[0, :, s - STEPS, :] = tile

    for step in range(STEPS):
        last = step == STEPS - 1
        z_left = update.moved(left, strip(left, None, mid), flux_left, deep_side)
        z_right = update.moved(right, strip(right, mid, None), flux_right, deep_side)
        new_left, new_right = update.mixed([z_left, z_right])
        if not last:
            z_mid = update.moved(mid, strip(mid, left, right), flux_mid, deep_mid)
            mid = update.settled(update.mixed([z_mid])[0], mid, deep_mid)
        left = update.settled(new_left, left, deep_side)
        right = update.settled(new_right, right, deep_side)
        if last:
            sides = jnp.where(place < 4, right, roll(left, -EDGE))
        low_rows = list(range(step + 1, step + 4))
        todo = low_rows + [slots - 1 - s for s in reversed(low_rows)]
        for k in range(0, len(todo), 2):
            pair = todo[k : k + 2]
            tiles = [[tile_at(step, s + j) for j in (-1, 0, 1)] for s in pair]
            new = update.rows(tiles, [flux_rows[s] for s in pair], [deep_rows[s] for s in pair])
            for j, (s, tile) in enumerate(zip(pair, new)):
                if last:
                    put(s, tile)
                else:
                    outer_refs[step][k + j] = tile
    for s in (slots // 2 - 1, slots // 2):
        put(s, inner_refs[STEPS - 1][s - slots // 2 + 1])


def kernel_call(body, out_shape, blocks, scratch=(), flops=0, nbytes=0, vmem=VMEM_LIMIT, grid=()):
    return pl.pallas_call(
        body,
        out_shape=out_shape,
        grid=grid,
        in_specs=blocks,
        out_specs=jax.tree.map(lambda _: vmem_spec(), out_shape),
        scratch_shapes=scratch,
        compiler_params=pltpu.CompilerParams(vmem_limit_bytes=vmem),
        cost_estimate=pl.CostEstimate(flops=flops, bytes_accessed=nbytes, transcendentals=0),
    )


def f32(*shape):
    return jax.ShapeDtypeStruct(shape, jnp.float32)


def exchange(value, axis, partner):
    size = lax.axis_size(axis)
    pairs = [(i, partner(i)) for i in range(size) if 0 <= partner(i) < size]
    return lax.ppermute(value, axis, pairs)


def on_device(state, mixing, diffusivity, weights, links, land, depth):
    levels, rows, cells = state.shape[1:]
    half = levels // 2
    count = links.shape[-1]
    pack_rows = count + 8
    lat_count, lon_count = lax.axis_size("lat"), lax.axis_size("lon")

    def near(i):
        return i ^ 1

    def far_round(i):
        return (i - 1 if i % 2 == 0 else i + 1) % lon_count

    def far_lat(i):
        return (i - 1 if i % 2 == 0 else i + 1) % lat_count

    zeros = kernel_call(
        zero_kernel, f32(8, 128), [], flops=2_000_000_000, nbytes=4096, vmem=FRONT_VMEM_LIMIT
    )()
    pack = kernel_call(
        pack_kernel,
        f32(pack_rows, 128),
        [vmem_spec()] * 6,
        flops=2_000_000_000,
        nbytes=700_000,
        vmem=FRONT_VMEM_LIMIT,
    )(state, weights, links, land.reshape(1, rows), depth.reshape(1, rows), zeros)
    state, pack = lax.optimization_barrier((state, pack))
    crossed = exchange(pack, "comp", near)
    edge, up_down_1, up_down_2, surface = kernel_call(
        edge_kernel,
        (f32(half, 128), f32(STEPS, levels, 128), f32(STEPS, levels, 128), f32(rows, cells)),
        [vmem_spec()],
        flops=2_000_000_000,
        nbytes=900_000,
        vmem=FRONT_VMEM_LIMIT,
    )(state)
    mine = jnp.concatenate([edge, crossed], axis=0)
    beside_1 = exchange(mine, "lon", near)
    beside_2 = exchange(mine, "lon", far_round)
    east_west = ((1, 0), (2, 0))
    if lon_count == 4:
        across = exchange(crossed, "lon", lambda i: i ^ 2)
        packs = [crossed, beside_1, beside_2, across]
        slices = [(0, 0), (1, half), (2, half), (3, 0)]
    else:
        packs = [crossed, beside_1, beside_2, lax.all_gather(crossed, "lon", axis=0, tiled=True)]
        slices = [(3, k * pack_rows) for k in range(lon_count)]
    rows_1 = exchange(up_down_1, "lat", near)
    rows_2 = exchange(up_down_2, "lat", far_lat)
    mixing, packs[1] = lax.optimization_barrier((mixing, packs[1]))
    operators = kernel_call(
        operator_kernel,
        (
            jax.ShapeDtypeStruct((levels, 256), jnp.bfloat16),
            f32(2, levels, 128),
        ),
        [vmem_spec()] * 2,
        flops=100_000,
        nbytes=100_000,
        vmem=FRONT_VMEM_LIMIT,
    )(mixing, diffusivity)
    rows_1, operators, packs[0] = lax.optimization_barrier((rows_1, operators, packs[0]))
    message = kernel_call(
        functools.partial(flux_kernel, count, slices, east_west),
        f32(half + 2 * rows + 8, 128),
        [vmem_spec()] * (1 + len(packs)),
        flops=3_000_000_000,
        nbytes=100_000,
        vmem=FRONT_VMEM_LIMIT,
    )(surface, *packs)
    message_1 = exchange(message, "lat", near)
    message_2 = exchange(message, "lat", far_lat)
    laid_out = kernel_call(
        inner_kernel,
        (f32(rows + 2 * STEPS, levels, 128), f32(2, levels, 128))
        + tuple(f32(rows - 2 * k, levels, 128) for k in range(STEPS)),
        [vmem_spec()] * 6,
        flops=2_000_000_000,
        nbytes=2_000_000,
    )(state, message, rows_1, rows_2, *operators)
    return kernel_call(
        outer_kernel,
        f32(*state.shape),
        [vmem_spec()] * (5 + len(laid_out)),
        scratch=[pltpu.VMEM((6, levels, 128), jnp.float32)] * (STEPS - 1),
        flops=300_000_000,
        nbytes=2_000_000,
    )(message, message_1, message_2, *operators, *laid_out)


def solution(mesh):
    in_specs = (
        P("comp", None, "lat", "lon"),
        P("comp", None, None),
        P("comp", None),
        P("comp", None),
        P("comp", "lat", "lon", None, None),
        P("lat", "lon"),
        P("lat", "lon"),
    )
    out_specs = P("comp", None, "lat", "lon")
    return jax.shard_map(
        on_device, mesh=mesh, in_specs=in_specs, out_specs=out_specs, check_vma=False
    )
```

time: 23.9 us -> 22 us (0.921)
  waiting for transfers between devices: 5.06 us -> 3.77 us
  local copies, waits for them, and re-layouts: 1.69 us -> 0.98 us
  Pallas kernels: 4.84 us -> 5.19 us
  starting transfers between devices: 12.1 us -> 11.8 us
    ppermute x8, waiting for transfers between devices: 5.06 us -> 3.77 us  [exchange(): return lax.ppermute(value, axis, pairs)]
    unnamed x15, local copies, waits for them, and re-layouts: 1.68 us -> 0.98 us
    pallas_call x2 -> x4, Pallas kernels: 3.89 us -> 4.2 us  [the longest x1 2.64 us: on_device(): kernel_call(outer_kernel, f32(*state.shape), [vmem_spec()] * (5 + len(lai...]
    ppermute x8, starting transfers between devices: 12.1 us -> 11.8 us  [exchange(): return lax.ppermute(value, axis, pairs)]
  transfers between devices with their start and end apart: 8 -> 8, of which waited for: 3 -> 2; matrix products, arithmetic and copies ran while one was open for 0% -> 0% of each run, Pallas kernels for 4% -> 11%
where the time goes in v3:
time: 22 us; the launch traced here: 21.8 us
  starting transfers between devices  11.8 us (54%)
  Pallas kernels  5.19 us (24%)
  waiting for transfers between devices  3.77 us (17%)
  local copies, waits for them, and re-layouts  0.98 us (4%)
    ppermute x8, starting transfers between devices, exchange(): return lax.ppermute(value, axis, pairs)  11.8 us
    ppermute x8, waiting for transfers between devices, exchange(): return lax.ppermute(value, axis, pairs)  3.77 us
    pallas_call x1, Pallas kernels, on_device(): kernel_call(outer_kernel, f32(*state.shape), [vmem_spec()] * (5 + len(lai...  2.64 us
    pallas_call x1, Pallas kernels, on_device(): kernel_call(inner_kernel, (f32(rows + 2 * STEPS, levels, 128), f32(2, lev...  1.39 us
    unnamed x15, local copies, waits for them, and re-layouts  0.98 us
    pallas_call x1, Pallas kernels, on_device(): kernel_call(edge_kernel, (f32(half, 128), f32(STEPS, levels, 128), f32(ST...  0.53 us
  transfers between devices with their start and end apart: 8, of which 2 were waited for; matrix products, arithmetic and copies ran while one was open for 0% of the time, Pallas kernels for 11%

profile of v3, /device:TPU:0, one launch (start us, length us, event | category | flops | bytes accessed | tf_op | source)
XLA Modules:
  0.0 21.8 jit_solution(2825660850131656175)
XLA Ops:
  0.0 0.0 copy-start.2
  0.0 0.0 copy-start.3
  0.0 0.0 copy-start.4
  0.0 0.0 copy-start.5
  0.0 0.0 copy-start.6
  0.0 0.9 %copy-done.2 = f32[1,80,8,128]{3,2,1,0:T(8,128)S(1)} copy-done((f32[1,80,8,128]{3,2,1,0:T(8,128)S(1)}, f32[1,80,8,128]{3,2,1,0:T(8,128)}, u32[]{:S(2)}) %copy-start.2) | copy-done | bytes 327704
  1.0 0.0 copy-done.3
  1.0 0.0 copy-done.4
  1.0 0.0 copy-done.5
  1.0 0.0 copy-done.6
  1.0 0.2 shard_map.74
  1.2 0.5 %collective-permute-start.1 = (f32[16,128]{1,0:T(8,128)S(1)}, f32[16,128]{1,0:T(8,128)S(1)}, u32[]{:S(2)}, u32[]{:S(2)}) collective-permute-start(f32[16,128]{1,0:T(8,128)S(1)} %shard_map.74), channel_id=1, source_target_pairs={{0,16},{16,0},{1,17},{17,1},{2,18},{18,2},{3,19},{19,3},{4,20},{20... | collective-permute-start | bytes 24584 | tf_op jit(solution)/shard_map/ppermute | solution.py:379
  1.6 0.5 %shard_map.75 = (f32[40,128]{1,0:T(8,128)S(1)}, f32[4,80,128]{2,1,0:T(8,128)S(1)}, f32[4,80,128]{2,1,0:T(8,128)S(1)}, f32[8,128]{1,0:T(8,128)S(1)}) custom-call(f32[1,80,8,128]{3,2,1,0:T(8,128)S(1)} %copy-done.2), custom_call_target="tpu_custom_call" | custom-call | flops 2000000000 | bytes 900000 | tf_op jit(solution)/shard_map/pallas_call | solution.py:411
  2.2 0.0 copy-start
  2.2 2.6 %collective-permute-start = (f32[4,80,128]{2,1,0:T(8,128)S(1)}, f32[4,80,128]{2,1,0:T(8,128)S(1)}, u32[]{:S(2)}, u32[]{:S(2)}) collective-permute-start(f32[4,80,128]{2,1,0:T(8,128)S(1)} %get-tuple-element.27), channel_id=1, source_target_pairs={{0,4},{4,0},{8,12},{12,8},{1,5},{5,1},{9,13},{13,9},{2,6},{6,2},{1... | collective-permute-start | bytes 491528 | tf_op jit(solution)/shard_map/ppermute | solution.py:379
  4.7 0.0 collective-permute-done.1.refs_1_
  4.7 0.0 copy-start.1
  4.7 1.6 %collective-permute-start.2 = (f32[56,128]{1,0:T(8,128)S(1)}, f32[56,128]{1,0:T(8,128)S(1)}, u32[]{:S(2)}, u32[]{:S(2)}) collective-permute-start(f32[56,128]{1,0:T(8,128)S(1)} %constant_dynamic-update-slice_fusion), channel_id=1, source_target_pairs={{0,1},{1,0},{2,3},{3,2},{4,5},{5,4},{6,7},{7,6},{8,9},{9,8},{10,11... | collective-permute-start | bytes 86024 | tf_op jit(solution)/shard_map/ppermute | solution.py:379
  6.4 2.5 %collective-permute-start.3 = (f32[56,128]{1,0:T(8,128)S(1)}, f32[56,128]{1,0:T(8,128)S(1)}, u32[]{:S(2)}, u32[]{:S(2)}) collective-permute-start(f32[56,128]{1,0:T(8,128)S(1)} %constant_dynamic-update-slice_fusion), channel_id=1, source_target_pairs={{0,3},{1,2},{2,1},{3,0},{4,7},{5,6},{6,5},{7,4},{8,11},{9,10},{10,... | collective-permute-start | bytes 86024 | tf_op jit(solution)/shard_map/ppermute | solution.py:379
  8.9 0.1 collective-permute-start.4
  9.0 1.5 %collective-permute-start.7 = (f32[4,80,128]{2,1,0:T(8,128)S(1)}, f32[4,80,128]{2,1,0:T(8,128)S(1)}, u32[]{:S(2)}, u32[]{:S(2)}) collective-permute-start(f32[4,80,128]{2,1,0:T(8,128)S(1)} %get-tuple-element.38), channel_id=1, source_target_pairs={{0,12},{4,8},{8,4},{12,0},{1,13},{5,9},{9,5},{13,1},{2,14},{6,10},... | collective-permute-start | bytes 491528 | tf_op jit(solution)/shard_map/ppermute | solution.py:379
  10.5 0.0 collective-permute-done.2.refs_2_
  10.5 0.0 copy-done
  10.5 0.0 copy-done.1
  10.5 0.1 shard_map.76
  10.6 0.0 collective-permute-done.rows1_ref
  10.6 2.8 %collective-permute-done.4.refs_4_ = f32[16,128]{1,0:T(8,128)S(1)} collective-permute-done((f32[16,128]{1,0:T(8,128)S(1)}, f32[16,128]{1,0:T(8,128)S(1)}, u32[]{:S(2)}, u32[]{:S(2)}) %collective-permute-start.4) | collective-permute-done | bytes 8224 | tf_op jit(solution)/shard_map/ppermute | solution.py:379
  13.4 0.0 collective-permute-done.3.refs_3_
  13.4 0.4 %shard_map.77.own_ref = f32[64,128]{1,0:T(8,128)S(1)} custom-call(f32[8,128]{1,0:T(8,128)S(1)} %get-tuple-element.26.refs_0_, f32[16,128]{1,0:T(8,128)S(1)} %collective-permute-done.1.refs_1_, f32[56,128]{1,0:T(8,128)S(1)} %collective-permute-done.2.refs_2_, f32[56,128]{1,0:T(8,128)S(1)} %collective-permute-done.3.refs_3_, ...), custom_call_target="tpu_custom_call" | custom-call | flops 3000000000 | bytes 100000 | tf_op jit(solution)/shard_map/pallas_call | solution.py:445
  13.8 0.6 %collective-permute-start.5 = (f32[64,128]{1,0:T(8,128)S(1)}, f32[64,128]{1,0:T(8,128)S(1)}, u32[]{:S(2)}, u32[]{:S(2)}) collective-permute-start(f32[64,128]{1,0:T(8,128)S(1)} %shard_map.77.own_ref), channel_id=1, source_target_pairs={{0,4},{4,0},{8,12},{12,8},{1,5},{5,1},{9,13},{13,9},{2,6},{6,2},{1... | collective-permute-start | bytes 98312 | tf_op jit(solution)/shard_map/ppermute | solution.py:379
  14.4 2.4 %collective-permute-start.6 = (f32[64,128]{1,0:T(8,128)S(1)}, f32[64,128]{1,0:T(8,128)S(1)}, u32[]{:S(2)}, u32[]{:S(2)}) collective-permute-start(f32[64,128]{1,0:T(8,128)S(1)} %shard_map.77.own_ref), channel_id=1, source_target_pairs={{0,12},{4,8},{8,4},{12,0},{1,13},{5,9},{9,5},{13,1},{2,14},{6,10},... | collective-permute-start | bytes 98312 | tf_op jit(solution)/shard_map/ppermute | solution.py:379
  16.8 0.0 collective-permute-done.7.rows2_ref
  16.8 1.4 %shard_map.78 = (f32[16,80,128]{2,1,0:T(8,128)S(1)}, f32[2,80,128]{2,1,0:T(8,128)S(1)}, f32[8,80,128]{2,1,0:T(8,128)S(1)}, f32[6,80,128]{2,1,0:T(8,128)S(1)}, f3...) custom-call(f32[1,80,8,128]{3,2,1,0:T(8,128)S(1)} %copy-done.2, f32[64,128]{1,0:T(8,128)S(1)} %shard_map.77.own_ref, ...), custom_call_target="tpu_custom_call" | custom-call | flops 2000000000 | bytes 2000000 | tf_op jit(solution)/shard_map/pallas_call | solution.py:455
  18.2 0.0 collective-permute-done.5.msg1_ref
  18.2 1.0 %collective-permute-done.6.msg2_ref = f32[64,128]{1,0:T(8,128)S(1)} collective-permute-done((f32[64,128]{1,0:T(8,128)S(1)}, f32[64,128]{1,0:T(8,128)S(1)}, u32[]{:S(2)}, u32[]{:S(2)}) %collective-permute-start.6) | collective-permute-done | bytes 32800 | tf_op jit(solution)/shard_map/ppermute | solution.py:379
  19.2 2.6 %shard_map.79 = f32[1,80,8,128]{3,2,1,0:T(8,128)} custom-call(f32[64,128]{1,0:T(8,128)S(1)} %shard_map.77.own_ref, f32[64,128]{1,0:T(8,128)S(1)} %collective-permute-done.5.msg1_ref, f32[64,128]{1,0:T(8,128)S(1)} %collective-permute-done.6.msg2_ref, bf16[80,256]{1,0:T(8,128)(2,1)S(1)} %get-tuple-element.35.mix_ref, ...), custom_call_target="tpu_custom_call" | custom-call | flops 300000000 | bytes 2000000 | tf_op jit(solution)/shard_map/pallas_call | solution.py:463
  (3 shorter events, 0.0 us)
Async XLA Ops:
  0.0 1.0 %copy-start.2 = (f32[1,80,8,128]{3,2,1,0:T(8,128)S(1)}, f32[1,80,8,128]{3,2,1,0:T(8,128)}, u32[]{:S(2)}) copy-start(f32[1,80,8,128]{3,2,1,0:T(8,128)} %state_ref.3) | copy-start | bytes 983044
  0.0 1.0 %copy-start.3 = (s32[1,1,1,4,8]{4,3,2,1,0:T(4,128)S(1)}, s32[1,1,1,4,8]{4,3,2,1,0:T(4,128)}, u32[]{:S(2)}) copy-start(s32[1,1,1,4,8]{4,3,2,1,0:T(4,128)} %links_ref.1) | copy-start | bytes 388
  0.0 1.0 %copy-start.4 = (f32[1,64]{1,0:T(1,128)S(1)}, f32[1,64]{1,0:T(1,128)}, u32[]{:S(2)}) copy-start(f32[1,64]{1,0:T(1,128)} %weights_ref.1) | copy-start | bytes 772
  0.0 1.0 %copy-start.5 = (s32[8,1]{0,1:T(1,128)S(1)}, s32[8,1]{0,1:T(1,128)}, u32[]{:S(2)}) copy-start(s32[8,1]{0,1:T(1,128)} %param.12) | copy-start | bytes 100
  0.0 1.0 %copy-start.6 = (s32[8,1]{0,1:T(1,128)S(1)}, s32[8,1]{0,1:T(1,128)}, u32[]{:S(2)}) copy-start(s32[8,1]{0,1:T(1,128)} %param.13) | copy-start | bytes 100
  1.2 3.6 %collective-permute-start.1 = (f32[16,128]{1,0:T(8,128)S(1)}, f32[16,128]{1,0:T(8,128)S(1)}, u32[]{:S(2)}, u32[]{:S(2)}) collective-permute-start(f32[16,128]{1,0:T(8,128)S(1)} %shard_map.74), channel_id=1, source_target_pairs={{0,16},{16,0},{1,17},{17,1},{2,18},{18,2},{3,19},{19,3},{4,20},{20... | collective-permute-start | bytes 24584 | tf_op jit(solution)/shard_map/ppermute | solution.py:379
  2.2 8.3 %copy-start = (f32[1,80,80]{2,1,0:T(8,128)S(1)}, f32[1,80,80]{2,1,0:T(8,128)}, u32[]{:S(2)}) copy-start(f32[1,80,80]{2,1,0:T(8,128)} %mixing_ref) | copy-start | bytes 76804
  2.2 8.4 %collective-permute-start = (f32[4,80,128]{2,1,0:T(8,128)S(1)}, f32[4,80,128]{2,1,0:T(8,128)S(1)}, u32[]{:S(2)}, u32[]{:S(2)}) collective-permute-start(f32[4,80,128]{2,1,0:T(8,128)S(1)} %get-tuple-element.27), channel_id=1, source_target_pairs={{0,4},{4,0},{8,12},{12,8},{1,5},{5,1},{9,13},{13,9},{2,6},{6,2},{1... | collective-permute-start | bytes 491528 | tf_op jit(solution)/shard_map/ppermute | solution.py:379
  4.7 5.7 %copy-start.1 = (f32[1,80]{1,0:T(1,128)S(1)}, f32[1,80]{1,0:T(1,128)}, u32[]{:S(2)}) copy-start(f32[1,80]{1,0:T(1,128)} %diffuse_ref.1) | copy-start | bytes 964
  4.7 5.7 %collective-permute-start.2 = (f32[56,128]{1,0:T(8,128)S(1)}, f32[56,128]{1,0:T(8,128)S(1)}, u32[]{:S(2)}, u32[]{:S(2)}) collective-permute-start(f32[56,128]{1,0:T(8,128)S(1)} %constant_dynamic-update-slice_fusion), channel_id=1, source_target_pairs={{0,1},{1,0},{2,3},{3,2},{4,5},{5,4},{6,7},{7,6},{8,9},{9,8},{10,11... | collective-permute-start | bytes 86024 | tf_op jit(solution)/shard_map/ppermute | solution.py:379
  6.4 7.0 %collective-permute-start.3 = (f32[56,128]{1,0:T(8,128)S(1)}, f32[56,128]{1,0:T(8,128)S(1)}, u32[]{:S(2)}, u32[]{:S(2)}) collective-permute-start(f32[56,128]{1,0:T(8,128)S(1)} %constant_dynamic-update-slice_fusion), channel_id=1, source_target_pairs={{0,3},{1,2},{2,1},{3,0},{4,7},{5,6},{6,5},{7,4},{8,11},{9,10},{10,... | collective-permute-start | bytes 86024 | tf_op jit(solution)/shard_map/ppermute | solution.py:379
  8.9 4.5 %collective-permute-start.4 = (f32[16,128]{1,0:T(8,128)S(1)}, f32[16,128]{1,0:T(8,128)S(1)}, u32[]{:S(2)}, u32[]{:S(2)}) collective-permute-start(f32[16,128]{1,0:T(8,128)S(1)} %collective-permute-done.1.refs_1_), channel_id=1, source_target_pairs={{0,2},{1,3},{2,0},{3,1},{4,6},{5,7},{6,4},{7,5},{8,10},{9,11},{10,... | collective-permute-start | bytes 24584 | tf_op jit(solution)/shard_map/ppermute | solution.py:379
  9.0 7.8 %collective-permute-start.7 = (f32[4,80,128]{2,1,0:T(8,128)S(1)}, f32[4,80,128]{2,1,0:T(8,128)S(1)}, u32[]{:S(2)}, u32[]{:S(2)}) collective-permute-start(f32[4,80,128]{2,1,0:T(8,128)S(1)} %get-tuple-element.38), channel_id=1, source_target_pairs={{0,12},{4,8},{8,4},{12,0},{1,13},{5,9},{9,5},{13,1},{2,14},{6,10},... | collective-permute-start | bytes 491528 | tf_op jit(solution)/shard_map/ppermute | solution.py:379
  13.8 4.5 %collective-permute-start.5 = (f32[64,128]{1,0:T(8,128)S(1)}, f32[64,128]{1,0:T(8,128)S(1)}, u32[]{:S(2)}, u32[]{:S(2)}) collective-permute-start(f32[64,128]{1,0:T(8,128)S(1)} %shard_map.77.own_ref), channel_id=1, source_target_pairs={{0,4},{4,0},{8,12},{12,8},{1,5},{5,1},{9,13},{13,9},{2,6},{6,2},{1... | collective-permute-start | bytes 98312 | tf_op jit(solution)/shard_map/ppermute | solution.py:379
  14.4 4.8 %collective-permute-start.6 = (f32[64,128]{1,0:T(8,128)S(1)}, f32[64,128]{1,0:T(8,128)S(1)}, u32[]{:S(2)}, u32[]{:S(2)}) collective-permute-start(f32[64,128]{1,0:T(8,128)S(1)} %shard_map.77.own_ref), channel_id=1, source_target_pairs={{0,12},{4,8},{8,4},{12,0},{1,13},{5,9},{9,5},{13,1},{2,14},{6,10},... | collective-permute-start | bytes 98312 | tf_op jit(solution)/shard_map/ppermute | solution.py:379

commit v4 on v3

--- a/solution.py
+++ b/solution.py
@@ -9,6 +9,7 @@
 
 STEPS = 4
 EDGE = 8
+FOLD = 24
 AXES = ("comp", "lat", "lon")
 VMEM_LIMIT = 8 * 1024 * 1024
 FRONT_VMEM_LIMIT = 4 * 1024 * 1024
@@ -113,10 +114,11 @@
 
 
 def flux_kernel(count, slices, east_west, *refs):
-    surface_ref, *packs, out_ref = refs
+    surface_ref, *packs, own_ref, first_ref, second_ref = refs
     surface = surface_ref[...]
     rows = surface.shape[0]
-    half = out_ref.shape[0] - 2 * rows - 8
+    levels = own_ref.shape[0] - 2 * rows - 8
+    half = levels // 2
     lon, lon_count = lax.axis_index("lon"), lax.axis_size("lon")
     odd = lax.rem(lon, 2) == 1
     ocean = lax.axis_index("comp") == 1
@@ -149,7 +151,7 @@
     column = lax.broadcasted_iota(jnp.int32, (rows, 128), 0) * EDGE == lane_ids((rows, 128))
     land = jnp.sum(jnp.where(column, spread_rows[0:1], 0.0), axis=1, keepdims=True)
     deep = jnp.sum(jnp.where(column, spread_rows[1:2], 0.0), axis=1, keepdims=True)
-    all_levels = float(2 * half)
+    all_levels = float(levels)
     deep = jnp.where(ocean, deep, all_levels)
     (first, first_at), (second, second_at) = east_west
     lane = lane_ids((1, 128))
@@ -172,12 +174,35 @@
         mine = (lane >= start) & (lane < start + EDGE)
         imported_beside = jnp.where(mine, jnp.where(from_east, east, west), imported_beside)
     flux_beside = coupling_rate * land_beside * (imported_beside - middle[0:1])
-    out_ref[0:half] = middle
-    out_ref[half : half + rows] = coupling_rate * land * (imported[0:rows] - surface)
-    out_ref[half + rows : half + 2 * rows] = jnp.broadcast_to(deep, (rows, 128))
-    out_ref[half + 2 * rows : half + 2 * rows + 1] = flux_beside
-    out_ref[half + 2 * rows + 1 : half + 2 * rows + 2] = deep_beside
-    out_ref[half + 2 * rows + 2 :] = jnp.zeros((6, 128), jnp.float32)
+    flux = coupling_rate * land * (imported[0:rows] - surface)
+    deep = jnp.broadcast_to(deep, (rows, 128))
+    whole = jnp.concatenate([middle, roll(middle, 64)], axis=0)
+    own_ref[0:levels] = roll(whole, STEPS * EDGE)
+    own_ref[levels : levels + rows] = flux
+    own_ref[levels + rows : levels + 2 * rows] = deep
+    own_ref[levels + 2 * rows : levels + 2 * rows + 1] = roll(flux_beside, STEPS * EDGE)
+    own_ref[levels + 2 * rows + 1 : levels + 2 * rows + 2] = roll(deep_beside, STEPS * EDGE)
+    own_ref[levels + 2 * rows + 2 :] = jnp.zeros((6, 128), jnp.float32)
+    width = STEPS * EDGE
+    sides = []
+    for at in (0, rows - STEPS):
+        lane_at = at * EDGE
+        folded = jnp.zeros((FOLD, 128), jnp.float32)
+        lane_fold = lane_ids((FOLD, 128))
+        for group in range(-(-levels // FOLD)):
+            part = whole[group * FOLD : min((group + 1) * FOLD, levels)]
+            if part.shape[0] < FOLD:
+                extra = jnp.zeros((FOLD - part.shape[0], 128), jnp.float32)
+                index = lax.broadcasted_iota(jnp.int32, extra.shape, 0)
+                extra = jnp.where(index == 0, flux_beside, jnp.where(index == 1, deep_beside, extra))
+                part = jnp.concatenate([part, extra], axis=0)
+            folded = jnp.where(lane_fold // width == group, roll(part, group * width - lane_at), folded)
+        sides.append((folded, flux[at : at + STEPS], deep[at : at + STEPS]))
+    lat_odd = lax.rem(lax.axis_index("lat"), 2) == 1
+    starts = (0, FOLD, FOLD + STEPS, FOLD + 2 * STEPS)
+    for (low, high), begin, end in zip(zip(*sides), starts, starts[1:]):
+        first_ref[begin:end] = jnp.where(lat_odd, low, high)
+        second_ref[begin:end] = jnp.where(lat_odd, high, low)
 
 
 def halves(value):
@@ -228,7 +253,6 @@
 
 def inner_kernel(state_ref, own_ref, rows1_ref, rows2_ref, mix_ref, rate_ref, x_ref, side_ref, *inner_refs):
     levels, rows, cells = state_ref.shape[1:]
-    half = levels // 2
     slots = rows + 2 * STEPS
     odd, inside = lat_place()
     first_at = jnp.where(odd, 0, rows + STEPS)
@@ -238,8 +262,8 @@
     for row in range(rows):
         x_ref[STEPS + row] = state_ref[0, :, row, :]
     update = Update(mix_ref, rate_ref)
-    flux = [own_ref[half + r : half + r + 1] for r in range(rows)]
-    deep = [own_ref[half + rows + r : half + rows + r + 1] for r in range(rows)]
+    flux = [own_ref[levels + r : levels + r + 1] for r in range(rows)]
+    deep = [own_ref[levels + rows + r : levels + rows + r + 1] for r in range(rows)]
     source, first = x_ref, 0
     for step in range(STEPS):
         target, at = inner_refs[step], STEPS + step
@@ -261,43 +285,49 @@
     side_ref[1] = right
 
 
-def outer_kernel(own_ref, msg1_ref, msg2_ref, mix_ref, rate_ref, x_ref, side_ref, *refs):
+def outer_kernel(own_ref, msg2_ref, msg1_ref, mix_ref, rate_ref, x_ref, side_ref, *refs):
     inner_refs, out_ref, outer_refs = refs[:STEPS], refs[STEPS], refs[STEPS + 1 :]
     levels, rows, cells = out_ref.shape[1:]
-    half = levels // 2
     slots = rows + 2 * STEPS
     odd, inside = lat_place()
-    own = own_ref[...]
     one, two = msg1_ref[...], jnp.where(inside, msg2_ref[...], 0.0)
     top, bottom = jnp.where(odd, one, two), jnp.where(odd, two, one)
-    parts = (top, own, bottom)
-
-    def per_slot(at, slot):
+
+    def per_slot(at, own_at, slot):
         if slot < STEPS:
-            at, value = at + rows - STEPS + slot, top
-        elif slot < STEPS + rows:
-            at, value = at + slot - STEPS, own
-        else:
-            at, value = at + slot - STEPS - rows, bottom
-        return value[at : at + 1]
-
-    flux_rows = [per_slot(half, s) for s in range(slots)]
-    deep_rows = [per_slot(half + rows, s) for s in range(slots)]
+            return top[at + slot : at + slot + 1]
+        if slot < STEPS + rows:
+            return own_ref[own_at + slot - STEPS : own_at + slot - STEPS + 1]
+        return bottom[at + slot - STEPS - rows : at + slot - STEPS - rows + 1]
+
+    flux_rows = [per_slot(FOLD, levels, s) for s in range(slots)]
+    deep_rows = [per_slot(FOLD + STEPS, levels + rows, s) for s in range(slots)]
     lane1 = lane_ids((1, 128))
     lane = lane_ids((levels, 128))
     place = lane % EDGE
-
-    def unfolded(fold):
-        a, b, c = (roll(v, s) for v, s in zip(fold, (-4 * EDGE, 4 * EDGE, 12 * EDGE)))
-        at = lane_ids(a.shape)
-        return jnp.where(at < 4 * EDGE, a, jnp.where(at < 12 * EDGE, b, c))
-
-    low = unfolded([v[:half] for v in parts])
-    high = unfolded([roll(v[:half], 64) for v in parts])
-    mid = jnp.concatenate([low, high], axis=0)
-    at = half + 2 * rows
-    flux_mid = unfolded([v[at : at + 1] for v in parts])
-    deep_mid = unfolded([v[at + 1 : at + 2] for v in parts])
+    width = STEPS * EDGE
+
+    def around(upper, own, lower, group):
+        at = lane_ids(own.shape)
+        upper, lower = roll(upper, -group * width), roll(lower, 128 - width - group * width)
+        return jnp.where(at < width, upper, jnp.where(at < 128 - width, own, lower))
+
+    pieces = []
+    for start in range(0, levels, FOLD):
+        size = min(FOLD, levels - start)
+        pieces.append(around(top[:size], own_ref[start : start + size], bottom[:size], start // FOLD))
+    mid = jnp.concatenate(pieces, axis=0)
+    beside = levels % FOLD
+    at = levels + 2 * rows
+    flux_mid, deep_mid = (
+        around(
+            top[beside + k : beside + k + 1],
+            own_ref[at + k : at + k + 1],
+            bottom[beside + k : beside + k + 1],
+            levels // FOLD,
+        )
+        for k in range(2)
+    )
     left, right = side_ref[0], side_ref[1]
     flux_left = flux_right = deep_side = jnp.zeros((1, 128), jnp.float32)
     for slot in range(slots):
@@ -308,13 +338,13 @@
         deep_side = jnp.where(mine1, deep_rows[slot], deep_side)
 
     def strip(tile, west, east):
-        around = roll(tile, EDGE) + roll(tile, -EDGE)
+        above_below = roll(tile, EDGE) + roll(tile, -EDGE)
         to_west, to_east = roll(tile, 1), roll(tile, -1)
         if west is not None:
             to_west = jnp.where(place == 0, roll(west, 1 - EDGE), to_west)
         if east is not None:
             to_east = jnp.where(place == EDGE - 1, roll(east, EDGE - 1), to_east)
-        return around + to_west + to_east
+        return above_below + to_west + to_east
 
     update = Update(mix_ref, rate_ref)
 
@@ -422,8 +452,9 @@
     east_west = ((1, 0), (2, 0))
     if lon_count == 4:
         across = exchange(crossed, "lon", lambda i: i ^ 2)
-        packs = [crossed, beside_1, beside_2, across]
-        slices = [(0, 0), (1, half), (2, half), (3, 0)]
+        packs = [crossed, beside_2, across, beside_1]
+        slices = [(0, 0), (1, half), (2, 0), (3, half)]
+        east_west = ((3, 0), (1, 0))
     else:
         packs = [crossed, beside_1, beside_2, lax.all_gather(crossed, "lon", axis=0, tiled=True)]
         slices = [(3, k * pack_rows) for k in range(lon_count)]
@@ -442,16 +473,16 @@
         vmem=FRONT_VMEM_LIMIT,
     )(mixing, diffusivity)
     rows_1, operators, packs[0] = lax.optimization_barrier((rows_1, operators, packs[0]))
-    message = kernel_call(
+    own, for_first, for_second = kernel_call(
         functools.partial(flux_kernel, count, slices, east_west),
-        f32(half + 2 * rows + 8, 128),
+        (f32(levels + 2 * rows + 8, 128),) + (f32(FOLD + 2 * STEPS, 128),) * 2,
         [vmem_spec()] * (1 + len(packs)),
         flops=3_000_000_000,
         nbytes=100_000,
         vmem=FRONT_VMEM_LIMIT,
     )(surface, *packs)
-    message_1 = exchange(message, "lat", near)
-    message_2 = exchange(message, "lat", far_lat)
+    message_2 = exchange(for_second, "lat", far_lat)
+    message_1 = exchange(for_first, "lat", near)
     laid_out = kernel_call(
         inner_kernel,
         (f32(rows + 2 * STEPS, levels, 128), f32(2, levels, 128))
@@ -459,7 +490,7 @@
         [vmem_spec()] * 6,
         flops=2_000_000_000,
         nbytes=2_000_000,
-    )(state, message, rows_1, rows_2, *operators)
+    )(state, own, rows_1, rows_2, *operators)
     return kernel_call(
         outer_kernel,
         f32(*state.shape),
@@ -467,7 +498,7 @@
         scratch=[pltpu.VMEM((6, levels, 128), jnp.float32)] * (STEPS - 1),
         flops=300_000_000,
         nbytes=2_000_000,
-    )(message, message_1, message_2, *operators, *laid_out)
+    )(own, message_2, message_1, *operators, *laid_out)
 
 
 def solution(mesh):

time: 22 us -> 21.4 us (0.973)
  waiting for transfers between devices: 3.77 us -> 2.99 us
    ppermute x8, waiting for transfers between devices: 3.77 us -> 2.99 us  [exchange(): return lax.ppermute(value, axis, pairs)]
  transfers between devices with their start and end apart: 8 -> 8, of which waited for: 2 -> 3; matrix products, arithmetic and copies ran while one was open for 0% -> 0% of each run, Pallas kernels for 11% -> 11%
where the time goes in v4:
time: 21.4 us; the launch traced here: 21.2 us
  starting transfers between devices  12 us (56%)
  Pallas kernels  5.19 us (24%)
  waiting for transfers between devices  2.99 us (14%)
  local copies, waits for them, and re-layouts  0.98 us (5%)
    ppermute x8, starting transfers between devices, exchange(): return lax.ppermute(value, axis, pairs)  12 us
    ppermute x8, waiting for transfers between devices, exchange(): return lax.ppermute(value, axis, pairs)  2.99 us
    pallas_call x1, Pallas kernels, on_device(): kernel_call(outer_kernel, f32(*state.shape), [vmem_spec()] * (5 + len(lai...  2.59 us
    pallas_call x1, Pallas kernels, on_device(): kernel_call(inner_kernel, (f32(rows + 2 * STEPS, levels, 128), f32(2, lev...  1.39 us
    unnamed x15, local copies, waits for them, and re-layouts  0.98 us
    pallas_call x1, Pallas kernels, on_device(): kernel_call(edge_kernel, (f32(half, 128), f32(STEPS, levels, 128), f32(ST...  0.53 us
  transfers between devices with their start and end apart: 8, of which 3 were waited for; matrix products, arithmetic and copies ran while one was open for 0% of the time, Pallas kernels for 11%

profile of v4, /device:TPU:0, one launch (start us, length us, event | category | flops | bytes accessed | tf_op | source)
XLA Modules:
  0.0 21.2 jit_solution(10987943168696209377)
XLA Ops:
  0.0 0.0 copy-start.2
  0.0 0.0 copy-start.3
  0.0 0.0 copy-start.4
  0.0 0.0 copy-start.5
  0.0 0.0 copy-start.6
  0.0 0.9 %copy-done.2 = f32[1,80,8,128]{3,2,1,0:T(8,128)S(1)} copy-done((f32[1,80,8,128]{3,2,1,0:T(8,128)S(1)}, f32[1,80,8,128]{3,2,1,0:T(8,128)}, u32[]{:S(2)}) %copy-start.2) | copy-done | bytes 327704
  1.0 0.0 copy-done.3
  1.0 0.0 copy-done.4
  1.0 0.0 copy-done.5
  1.0 0.0 copy-done.6
  1.0 0.2 shard_map.74
  1.2 0.5 %collective-permute-start.1 = (f32[16,128]{1,0:T(8,128)S(1)}, f32[16,128]{1,0:T(8,128)S(1)}, u32[]{:S(2)}, u32[]{:S(2)}) collective-permute-start(f32[16,128]{1,0:T(8,128)S(1)} %shard_map.74), channel_id=1, source_target_pairs={{0,16},{16,0},{1,17},{17,1},{2,18},{18,2},{3,19},{19,3},{4,20},{20... | collective-permute-start | bytes 24584 | tf_op jit(solution)/shard_map/ppermute | solution.py:409
  1.6 0.5 %shard_map.75 = (f32[40,128]{1,0:T(8,128)S(1)}, f32[4,80,128]{2,1,0:T(8,128)S(1)}, f32[4,80,128]{2,1,0:T(8,128)S(1)}, f32[8,128]{1,0:T(8,128)S(1)}) custom-call(f32[1,80,8,128]{3,2,1,0:T(8,128)S(1)} %copy-done.2), custom_call_target="tpu_custom_call" | custom-call | flops 2000000000 | bytes 900000 | tf_op jit(solution)/shard_map/pallas_call | solution.py:441
  2.2 0.0 copy-start
  2.2 2.6 %collective-permute-start = (f32[4,80,128]{2,1,0:T(8,128)S(1)}, f32[4,80,128]{2,1,0:T(8,128)S(1)}, u32[]{:S(2)}, u32[]{:S(2)}) collective-permute-start(f32[4,80,128]{2,1,0:T(8,128)S(1)} %get-tuple-element.30), channel_id=1, source_target_pairs={{0,4},{4,0},{8,12},{12,8},{1,5},{5,1},{9,13},{13,9},{2,6},{6,2},{1... | collective-permute-start | bytes 491528 | tf_op jit(solution)/shard_map/ppermute | solution.py:409
  4.7 0.0 collective-permute-done.1.refs_1_
  4.7 0.0 copy-start.1
  4.7 3.7 %collective-permute-start.2 = (f32[56,128]{1,0:T(8,128)S(1)}, f32[56,128]{1,0:T(8,128)S(1)}, u32[]{:S(2)}, u32[]{:S(2)}) collective-permute-start(f32[56,128]{1,0:T(8,128)S(1)} %constant_dynamic-update-slice_fusion), channel_id=1, source_target_pairs={{0,3},{1,2},{2,1},{3,0},{4,7},{5,6},{6,5},{7,4},{8,11},{9,10},{10,... | collective-permute-start | bytes 86024 | tf_op jit(solution)/shard_map/ppermute | solution.py:409
  8.4 0.0 collective-permute-start.4
  8.4 0.8 %collective-permute-start.3 = (f32[16,128]{1,0:T(8,128)S(1)}, f32[16,128]{1,0:T(8,128)S(1)}, u32[]{:S(2)}, u32[]{:S(2)}) collective-permute-start(f32[16,128]{1,0:T(8,128)S(1)} %collective-permute-done.1.refs_1_), channel_id=1, source_target_pairs={{0,2},{1,3},{2,0},{3,1},{4,6},{5,7},{6,4},{7,5},{8,10},{9,11},{10,... | collective-permute-start | bytes 24584 | tf_op jit(solution)/shard_map/ppermute | solution.py:409
  9.2 1.5 %collective-permute-start.7 = (f32[4,80,128]{2,1,0:T(8,128)S(1)}, f32[4,80,128]{2,1,0:T(8,128)S(1)}, u32[]{:S(2)}, u32[]{:S(2)}) collective-permute-start(f32[4,80,128]{2,1,0:T(8,128)S(1)} %get-tuple-element.44), channel_id=1, source_target_pairs={{0,12},{4,8},{8,4},{12,0},{1,13},{5,9},{9,5},{13,1},{2,14},{6,10},... | collective-permute-start | bytes 491528 | tf_op jit(solution)/shard_map/ppermute | solution.py:409
  10.7 0.0 collective-permute-done.2.refs_2_
  10.7 0.0 copy-done
  10.7 0.0 copy-done.1
  10.7 0.1 shard_map.76
  10.8 0.0 collective-permute-done.rows1_ref
  10.8 2.1 %collective-permute-done.3.refs_3_ = f32[16,128]{1,0:T(8,128)S(1)} collective-permute-done((f32[16,128]{1,0:T(8,128)S(1)}, f32[16,128]{1,0:T(8,128)S(1)}, u32[]{:S(2)}, u32[]{:S(2)}) %collective-permute-start.3) | collective-permute-done | bytes 8224 | tf_op jit(solution)/shard_map/ppermute | solution.py:409
  13.0 0.0 collective-permute-done.4.refs_4_
  13.0 0.4 %shard_map.77 = (f32[104,128]{1,0:T(8,128)S(1)}, f32[32,128]{1,0:T(8,128)S(1)}, f32[32,128]{1,0:T(8,128)S(1)}) custom-call(f32[8,128]{1,0:T(8,128)S(1)} %get-tuple-element.29.refs_0_, f32[16,128]{1,0:T(8,128)S(1)} %collective-permute-done.1.refs_1_, f32[56,128]{1,0:T(8,128)S(1)} %collective-permute-done.2.refs_2_, ...), custom_call_target="tpu_custom_call" | custom-call | flops 3000000000 | bytes 100000 | tf_op jit(solution)/shard_map/pallas_call | solution.py:476
  13.4 1.5 %collective-permute-start.5 = (f32[32,128]{1,0:T(8,128)S(1)}, f32[32,128]{1,0:T(8,128)S(1)}, u32[]{:S(2)}, u32[]{:S(2)}) collective-permute-start(f32[32,128]{1,0:T(8,128)S(1)} %get-tuple-element.39), channel_id=1, source_target_pairs={{0,12},{4,8},{8,4},{12,0},{1,13},{5,9},{9,5},{13,1},{2,14},{6,10},... | collective-permute-start | bytes 49160 | tf_op jit(solution)/shard_map/ppermute | solution.py:409
  14.9 1.5 %collective-permute-start.6 = (f32[32,128]{1,0:T(8,128)S(1)}, f32[32,128]{1,0:T(8,128)S(1)}, u32[]{:S(2)}, u32[]{:S(2)}) collective-permute-start(f32[32,128]{1,0:T(8,128)S(1)} %get-tuple-element.40), channel_id=1, source_target_pairs={{0,4},{4,0},{8,12},{12,8},{1,5},{5,1},{9,13},{13,9},{2,6},{6,2},{1... | collective-permute-start | bytes 49160 | tf_op jit(solution)/shard_map/ppermute | solution.py:409
  16.4 0.0 collective-permute-done.7.rows2_ref
  16.4 1.4 %shard_map.78 = (f32[16,80,128]{2,1,0:T(8,128)S(1)}, f32[2,80,128]{2,1,0:T(8,128)S(1)}, f32[8,80,128]{2,1,0:T(8,128)S(1)}, f32[6,80,128]{2,1,0:T(8,128)S(1)}, f3...) custom-call(f32[1,80,8,128]{3,2,1,0:T(8,128)S(1)} %copy-done.2, f32[104,128]{1,0:T(8,128)S(1)} %get-tuple-element.38.own_ref, ...), custom_call_target="tpu_custom_call" | custom-call | flops 2000000000 | bytes 2000000 | tf_op jit(solution)/shard_map/pallas_call | solution.py:486
  17.8 0.2 %collective-permute-done.5.msg2_ref = f32[32,128]{1,0:T(8,128)S(1)} collective-permute-done((f32[32,128]{1,0:T(8,128)S(1)}, f32[32,128]{1,0:T(8,128)S(1)}, u32[]{:S(2)}, u32[]{:S(2)}) %collective-permute-start.5) | collective-permute-done | bytes 16416 | tf_op jit(solution)/shard_map/ppermute | solution.py:409
  18.0 0.6 %collective-permute-done.6.msg1_ref = f32[32,128]{1,0:T(8,128)S(1)} collective-permute-done((f32[32,128]{1,0:T(8,128)S(1)}, f32[32,128]{1,0:T(8,128)S(1)}, u32[]{:S(2)}, u32[]{:S(2)}) %collective-permute-start.6) | collective-permute-done | bytes 16416 | tf_op jit(solution)/shard_map/ppermute | solution.py:409
  18.6 2.6 %shard_map.79 = f32[1,80,8,128]{3,2,1,0:T(8,128)} custom-call(f32[104,128]{1,0:T(8,128)S(1)} %get-tuple-element.38.own_ref, f32[32,128]{1,0:T(8,128)S(1)} %collective-permute-done.5.msg2_ref, f32[32,128]{1,0:T(8,128)S(1)} %collective-permute-done.6.msg1_ref, bf16[80,256]{1,0:T(8,128)(2,1)S(1)} %get-tuple-element.41.mix_ref, ...), custom_call_target="tpu_custom_call" | custom-call | flops 300000000 | bytes 2000000 | tf_op jit(solution)/shard_map/pallas_call | solution.py:494
  (3 shorter events, 0.0 us)
Async XLA Ops:
  0.0 1.0 %copy-start.2 = (f32[1,80,8,128]{3,2,1,0:T(8,128)S(1)}, f32[1,80,8,128]{3,2,1,0:T(8,128)}, u32[]{:S(2)}) copy-start(f32[1,80,8,128]{3,2,1,0:T(8,128)} %state_ref.3) | copy-start | bytes 983044
  0.0 1.0 %copy-start.3 = (s32[1,1,1,4,8]{4,3,2,1,0:T(4,128)S(1)}, s32[1,1,1,4,8]{4,3,2,1,0:T(4,128)}, u32[]{:S(2)}) copy-start(s32[1,1,1,4,8]{4,3,2,1,0:T(4,128)} %links_ref.1) | copy-start | bytes 388
  0.0 1.0 %copy-start.4 = (f32[1,64]{1,0:T(1,128)S(1)}, f32[1,64]{1,0:T(1,128)}, u32[]{:S(2)}) copy-start(f32[1,64]{1,0:T(1,128)} %weights_ref.1) | copy-start | bytes 772
  0.0 1.0 %copy-start.5 = (s32[8,1]{0,1:T(1,128)S(1)}, s32[8,1]{0,1:T(1,128)}, u32[]{:S(2)}) copy-start(s32[8,1]{0,1:T(1,128)} %param.12) | copy-start | bytes 100
  0.0 1.0 %copy-start.6 = (s32[8,1]{0,1:T(1,128)S(1)}, s32[8,1]{0,1:T(1,128)}, u32[]{:S(2)}) copy-start(s32[8,1]{0,1:T(1,128)} %param.13) | copy-start | bytes 100
  1.2 3.6 %collective-permute-start.1 = (f32[16,128]{1,0:T(8,128)S(1)}, f32[16,128]{1,0:T(8,128)S(1)}, u32[]{:S(2)}, u32[]{:S(2)}) collective-permute-start(f32[16,128]{1,0:T(8,128)S(1)} %shard_map.74), channel_id=1, source_target_pairs={{0,16},{16,0},{1,17},{17,1},{2,18},{18,2},{3,19},{19,3},{4,20},{20... | collective-permute-start | bytes 24584 | tf_op jit(solution)/shard_map/ppermute | solution.py:409
  2.2 8.5 %copy-start = (f32[1,80,80]{2,1,0:T(8,128)S(1)}, f32[1,80,80]{2,1,0:T(8,128)}, u32[]{:S(2)}) copy-start(f32[1,80,80]{2,1,0:T(8,128)} %mixing_ref) | copy-start | bytes 76804
  2.2 8.7 %collective-permute-start = (f32[4,80,128]{2,1,0:T(8,128)S(1)}, f32[4,80,128]{2,1,0:T(8,128)S(1)}, u32[]{:S(2)}, u32[]{:S(2)}) collective-permute-start(f32[4,80,128]{2,1,0:T(8,128)S(1)} %get-tuple-element.30), channel_id=1, source_target_pairs={{0,4},{4,0},{8,12},{12,8},{1,5},{5,1},{9,13},{13,9},{2,6},{6,2},{1... | collective-permute-start | bytes 491528 | tf_op jit(solution)/shard_map/ppermute | solution.py:409
  4.7 6.0 %copy-start.1 = (f32[1,80]{1,0:T(1,128)S(1)}, f32[1,80]{1,0:T(1,128)}, u32[]{:S(2)}) copy-start(f32[1,80]{1,0:T(1,128)} %diffuse_ref.1) | copy-start | bytes 964
  4.7 5.9 %collective-permute-start.2 = (f32[56,128]{1,0:T(8,128)S(1)}, f32[56,128]{1,0:T(8,128)S(1)}, u32[]{:S(2)}, u32[]{:S(2)}) collective-permute-start(f32[56,128]{1,0:T(8,128)S(1)} %constant_dynamic-update-slice_fusion), channel_id=1, source_target_pairs={{0,3},{1,2},{2,1},{3,0},{4,7},{5,6},{6,5},{7,4},{8,11},{9,10},{10,... | collective-permute-start | bytes 86024 | tf_op jit(solution)/shard_map/ppermute | solution.py:409
  8.4 4.6 %collective-permute-start.4 = (f32[56,128]{1,0:T(8,128)S(1)}, f32[56,128]{1,0:T(8,128)S(1)}, u32[]{:S(2)}, u32[]{:S(2)}) collective-permute-start(f32[56,128]{1,0:T(8,128)S(1)} %constant_dynamic-update-slice_fusion), channel_id=1, source_target_pairs={{0,1},{1,0},{2,3},{3,2},{4,5},{5,4},{6,7},{7,6},{8,9},{9,8},{10,11... | collective-permute-start | bytes 86024 | tf_op jit(solution)/shard_map/ppermute | solution.py:409
  8.4 4.5 %collective-permute-start.3 = (f32[16,128]{1,0:T(8,128)S(1)}, f32[16,128]{1,0:T(8,128)S(1)}, u32[]{:S(2)}, u32[]{:S(2)}) collective-permute-start(f32[16,128]{1,0:T(8,128)S(1)} %collective-permute-done.1.refs_1_), channel_id=1, source_target_pairs={{0,2},{1,3},{2,0},{3,1},{4,6},{5,7},{6,4},{7,5},{8,10},{9,11},{10,... | collective-permute-start | bytes 24584 | tf_op jit(solution)/shard_map/ppermute | solution.py:409
  9.2 7.2 %collective-permute-start.7 = (f32[4,80,128]{2,1,0:T(8,128)S(1)}, f32[4,80,128]{2,1,0:T(8,128)S(1)}, u32[]{:S(2)}, u32[]{:S(2)}) collective-permute-start(f32[4,80,128]{2,1,0:T(8,128)S(1)} %get-tuple-element.44), channel_id=1, source_target_pairs={{0,12},{4,8},{8,4},{12,0},{1,13},{5,9},{9,5},{13,1},{2,14},{6,10},... | collective-permute-start | bytes 491528 | tf_op jit(solution)/shard_map/ppermute | solution.py:409
  13.4 4.7 %collective-permute-start.5 = (f32[32,128]{1,0:T(8,128)S(1)}, f32[32,128]{1,0:T(8,128)S(1)}, u32[]{:S(2)}, u32[]{:S(2)}) collective-permute-start(f32[32,128]{1,0:T(8,128)S(1)} %get-tuple-element.39), channel_id=1, source_target_pairs={{0,12},{4,8},{8,4},{12,0},{1,13},{5,9},{9,5},{13,1},{2,14},{6,10},... | collective-permute-start | bytes 49160 | tf_op jit(solution)/shard_map/ppermute | solution.py:409
  14.9 3.7 %collective-permute-start.6 = (f32[32,128]{1,0:T(8,128)S(1)}, f32[32,128]{1,0:T(8,128)S(1)}, u32[]{:S(2)}, u32[]{:S(2)}) collective-permute-start(f32[32,128]{1,0:T(8,128)S(1)} %get-tuple-element.40), channel_id=1, source_target_pairs={{0,4},{4,0},{8,12},{12,8},{1,5},{5,1},{9,13},{13,9},{2,6},{6,2},{1... | collective-permute-start | bytes 49160 | tf_op jit(solution)/shard_map/ppermute | solution.py:409

commit v5 on v4

--- a/solution.py
+++ b/solution.py
@@ -74,7 +74,8 @@
     out_ref[count + 1 : count + 2] = weight_row
     out_ref[count + 2 : count + 3] = spread(land)
     out_ref[count + 3 : count + 4] = spread(deep)
-    out_ref[count + 4 :] = zero_ref[0:4]
+    out_ref[count + 4 : count + 8] = zero_ref[0:4]
+    out_ref[count + 8 :] = surface
 
 
 def operator_kernel(mixing_ref, diffuse_ref, mix_ref, rate_ref):
@@ -91,11 +92,14 @@
     rate_ref[1] = 1.0 - 4.0 * rate
 
 
-def edge_kernel(state_ref, edge_ref, first_ref, second_ref, surface_ref):
+def fold_shift(group):
+    return group % 2 * 4 + group // 2 * 64
+
+
+def edge_kernel(state_ref, near_ref, far_ref, first_ref, second_ref):
     levels, rows, cells = state_ref.shape[1:]
-    surface_ref[...] = state_ref[0, 0]
-    half = levels // 2
-    odd = lax.rem(lax.axis_index("lat"), 2) == 1
+    lat_odd = lax.rem(lax.axis_index("lat"), 2) == 1
+    lon_odd = lax.rem(lax.axis_index("lon"), 2) == 1
     lane = lane_ids((levels, 128))
     first = last = jnp.zeros((levels, 128), jnp.float32)
     tiles = []
@@ -105,23 +109,32 @@
         turned = roll(tile, row * EDGE)
         first = jnp.where(lane // EDGE == row, turned, first)
         last = jnp.where(lane // EDGE == (row - 1) % (128 // EDGE), turned, last)
-    packed = jnp.where(lane % EDGE < 4, first, roll(last, EDGE))
-    edge_ref[...] = jnp.where(lane_ids((half, 128)) < 64, packed[:half], roll(packed[half:], 64))
+    last = roll(last, 4)
+    near, far = jnp.where(lon_odd, first, last), jnp.where(lon_odd, last, first)
+    for ref, cells_out in ((near_ref, near), (far_ref, far)):
+        folded = jnp.zeros((FOLD, 128), jnp.float32)
+        lane_fold = lane_ids((FOLD, 128))
+        for group in range(-(-levels // FOLD)):
+            part = cells_out[group * FOLD : min((group + 1) * FOLD, levels)]
+            if part.shape[0] < FOLD:
+                part = jnp.concatenate([part, jnp.zeros((FOLD - part.shape[0], 128), jnp.float32)], axis=0)
+            mine = (lane_fold // 64 == group // 2) & (lane_fold % EDGE // 4 == group % 2)
+            folded = jnp.where(mine, roll(part, fold_shift(group)), folded)
+        ref[...] = folded
     for k in range(4):
         low, high = tiles[k], tiles[rows - 4 + k]
-        first_ref[k] = jnp.where(odd, low, high)
-        second_ref[k] = jnp.where(odd, high, low)
+        first_ref[k] = jnp.where(lat_odd, low, high)
+        second_ref[k] = jnp.where(lat_odd, high, low)
 
 
 def flux_kernel(count, slices, east_west, *refs):
-    surface_ref, *packs, own_ref, first_ref, second_ref = refs
-    surface = surface_ref[...]
+    crossed_ref, *packs, own_ref, first_ref, second_ref = refs
+    surface = crossed_ref[count + 8 :]
     rows = surface.shape[0]
     levels = own_ref.shape[0] - 2 * rows - 8
-    half = levels // 2
     lon, lon_count = lax.axis_index("lon"), lax.axis_size("lon")
     odd = lax.rem(lon, 2) == 1
-    ocean = lax.axis_index("comp") == 1
+    ocean = lax.axis_index("comp") == 0
     here = lon * rows
     after = lax.rem(lon + 1, lon_count) * rows
     before = lax.rem(lon + lon_count - 1, lon_count) * rows
@@ -144,10 +157,7 @@
             hit * ref[offset + count + 1 : offset + count + 2, 0:count], axis=1, keepdims=True
         )
     imported = accum / jnp.maximum(totals, 1.0)
-    here_which, here_at = slices[0]
-    own_rows = packs[here_which]
-    at = here_at + count + 2
-    spread_rows = own_rows[at : at + 2]
+    spread_rows = packs[0][count + 2 : count + 4]
     column = lax.broadcasted_iota(jnp.int32, (rows, 128), 0) * EDGE == lane_ids((rows, 128))
     land = jnp.sum(jnp.where(column, spread_rows[0:1], 0.0), axis=1, keepdims=True)
     deep = jnp.sum(jnp.where(column, spread_rows[1:2], 0.0), axis=1, keepdims=True)
@@ -157,15 +167,25 @@
     lane = lane_ids((1, 128))
     from_east = lax.rem(lane, EDGE) < 4
 
-    def beside(offset_rows, size):
-        one = packs[first][first_at + offset_rows : first_at + offset_rows + size]
-        two = packs[second][second_at + offset_rows : second_at + offset_rows + size]
-        east_is_one = lane_ids((size, 128)) % EDGE < 4
-        return jnp.where(east_is_one != odd, one, two)
-
-    middle = beside(0, half)
-    land_beside = beside(half + count + 2, 1)
-    deep_beside = jnp.where(ocean, beside(half + count + 3, 1), all_levels)
+    one = packs[first][first_at : first_at + FOLD + count + 4]
+    two = packs[second][second_at : second_at + FOLD + count + 4]
+    to_east, to_west = jnp.where(odd, two, one), jnp.where(odd, one, two)
+
+    def beside(at):
+        return jnp.where(from_east, to_east[at : at + 1], to_west[at : at + 1])
+
+    pieces = []
+    for start in range(0, levels, FOLD):
+        size = min(FOLD, levels - start)
+        shift = fold_shift(start // FOLD)
+        pieces.append(
+            jnp.where(
+                lane_ids((size, 128)) % EDGE < 4, roll(to_east[:size], -shift), roll(to_west[:size], 4 - shift)
+            )
+        )
+    whole = jnp.concatenate(pieces, axis=0)
+    land_beside = beside(FOLD + count + 2)
+    deep_beside = jnp.where(ocean, beside(FOLD + count + 3), all_levels)
     imported_beside = jnp.zeros((1, 128), jnp.float32)
     for row in range(rows):
         start = row * EDGE
@@ -173,10 +193,9 @@
         west = roll(imported[2 * rows + row : 2 * rows + row + 1], start + 8)
         mine = (lane >= start) & (lane < start + EDGE)
         imported_beside = jnp.where(mine, jnp.where(from_east, east, west), imported_beside)
-    flux_beside = coupling_rate * land_beside * (imported_beside - middle[0:1])
+    flux_beside = coupling_rate * land_beside * (imported_beside - whole[0:1])
     flux = coupling_rate * land * (imported[0:rows] - surface)
     deep = jnp.broadcast_to(deep, (rows, 128))
-    whole = jnp.concatenate([middle, roll(middle, 64)], axis=0)
     own_ref[0:levels] = roll(whole, STEPS * EDGE)
     own_ref[levels : levels + rows] = flux
     own_ref[levels + rows : levels + 2 * rows] = deep
@@ -409,9 +428,18 @@
     return lax.ppermute(value, axis, pairs)
 
 
+def exchange_over(value, axis, partner):
+    size, sections = lax.axis_size(axis), lax.axis_size("comp")
+    pairs = [
+        (section * size + i, (sections - 1 - section) * size + partner(i))
+        for section in range(sections)
+        for i in range(size)
+    ]
+    return lax.ppermute(value, ("comp", axis), pairs)
+
+
 def on_device(state, mixing, diffusivity, weights, links, land, depth):
     levels, rows, cells = state.shape[1:]
-    half = levels // 2
     count = links.shape[-1]
     pack_rows = count + 8
     lat_count, lon_count = lax.axis_size("lat"), lax.axis_size("lon")
@@ -430,7 +458,7 @@
     )()
     pack = kernel_call(
         pack_kernel,
-        f32(pack_rows, 128),
+        f32(pack_rows + rows, 128),
         [vmem_spec()] * 6,
         flops=2_000_000_000,
         nbytes=700_000,
@@ -438,29 +466,14 @@
     )(state, weights, links, land.reshape(1, rows), depth.reshape(1, rows), zeros)
     state, pack = lax.optimization_barrier((state, pack))
     crossed = exchange(pack, "comp", near)
-    edge, up_down_1, up_down_2, surface = kernel_call(
+    edge_near, edge_far, up_down_1, up_down_2 = kernel_call(
         edge_kernel,
-        (f32(half, 128), f32(STEPS, levels, 128), f32(STEPS, levels, 128), f32(rows, cells)),
+        (f32(FOLD, 128),) * 2 + (f32(STEPS, levels, 128),) * 2,
         [vmem_spec()],
         flops=2_000_000_000,
         nbytes=900_000,
         vmem=FRONT_VMEM_LIMIT,
     )(state)
-    mine = jnp.concatenate([edge, crossed], axis=0)
-    beside_1 = exchange(mine, "lon", near)
-    beside_2 = exchange(mine, "lon", far_round)
-    east_west = ((1, 0), (2, 0))
-    if lon_count == 4:
-        across = exchange(crossed, "lon", lambda i: i ^ 2)
-        packs = [crossed, beside_2, across, beside_1]
-        slices = [(0, 0), (1, half), (2, 0), (3, half)]
-        east_west = ((3, 0), (1, 0))
-    else:
-        packs = [crossed, beside_1, beside_2, lax.all_gather(crossed, "lon", axis=0, tiled=True)]
-        slices = [(3, k * pack_rows) for k in range(lon_count)]
-    rows_1 = exchange(up_down_1, "lat", near)
-    rows_2 = exchange(up_down_2, "lat", far_lat)
-    mixing, packs[1] = lax.optimization_barrier((mixing, packs[1]))
     operators = kernel_call(
         operator_kernel,
         (
@@ -468,11 +481,25 @@
             f32(2, levels, 128),
         ),
         [vmem_spec()] * 2,
-        flops=100_000,
+        flops=2_000_000_000,
         nbytes=100_000,
         vmem=FRONT_VMEM_LIMIT,
     )(mixing, diffusivity)
-    rows_1, operators, packs[0] = lax.optimization_barrier((rows_1, operators, packs[0]))
+    operators, edge_near = lax.optimization_barrier((operators, edge_near))
+    beside_1 = exchange_over(jnp.concatenate([edge_near, crossed[:pack_rows]], axis=0), "lon", near)
+    beside_2 = exchange_over(jnp.concatenate([edge_far, crossed[:pack_rows]], axis=0), "lon", far_round)
+    if lon_count == 4:
+        across = exchange_over(crossed[:pack_rows], "lon", lambda i: i ^ 2)
+        packs = [pack, beside_1, across, beside_2]
+        slices = [(0, 0), (1, FOLD), (2, 0), (3, FOLD)]
+        east_west = ((1, 0), (3, 0))
+    else:
+        packs = [pack, beside_1, beside_2, lax.all_gather(pack[:pack_rows], "lon", axis=0, tiled=True)]
+        slices = [(3, k * pack_rows) for k in range(lon_count)]
+        east_west = ((1, 0), (2, 0))
+    rows_1 = exchange(up_down_1, "lat", near)
+    rows_2 = exchange(up_down_2, "lat", far_lat)
+    rows_1, packs[0] = lax.optimization_barrier((rows_1, packs[0]))
     own, for_first, for_second = kernel_call(
         functools.partial(flux_kernel, count, slices, east_west),
         (f32(levels + 2 * rows + 8, 128),) + (f32(FOLD + 2 * STEPS, 128),) * 2,
@@ -480,9 +507,10 @@
         flops=3_000_000_000,
         nbytes=100_000,
         vmem=FRONT_VMEM_LIMIT,
-    )(surface, *packs)
-    message_2 = exchange(for_second, "lat", far_lat)
-    message_1 = exchange(for_first, "lat", near)
+    )(crossed, *packs)
+    own = exchange(own, "comp", near)
+    message_2 = exchange_over(for_second, "lat", far_lat)
+    message_1 = exchange_over(for_first, "lat", near)
     laid_out = kernel_call(
         inner_kernel,
         (f32(rows + 2 * STEPS, levels, 128), f32(2, levels, 128))

time: 21.4 us -> 20.7 us (0.967)
  waiting for transfers between devices: 2.99 us -> 2.34 us
    ppermute x8 -> x4, starting transfers between devices: 12 us -> 5.2 us  [exchange(): return lax.ppermute(value, axis, pairs)]
    ppermute x0 -> x5, starting transfers between devices: none -> 6.73 us  [exchange_over(): return lax.ppermute(value, ('comp', axis), pairs)]
    ppermute x8 -> x4, waiting for transfers between devices: 2.99 us -> 0.39 us  [exchange(): return lax.ppermute(value, axis, pairs)]
    ppermute x0 -> x5, waiting for transfers between devices: none -> 1.95 us  [exchange_over(): return lax.ppermute(value, ('comp', axis), pairs)]
    unnamed x15 -> x14, local copies, waits for them, and re-layouts: 0.98 us -> 0.97 us
  transfers between devices with their start and end apart: 8 -> 9, of which waited for: 3 -> 3; matrix products, arithmetic and copies ran while one was open for 0% -> 0% of each run, Pallas kernels for 11% -> 12%
where the time goes in v5:
time: 20.7 us; the launch traced here: 20.5 us
  starting transfers between devices  11.9 us (57%)
  Pallas kernels  5.2 us (25%)
  waiting for transfers between devices  2.34 us (11%)
  local copies, waits for them, and re-layouts  0.98 us (5%)
    ppermute x5, starting transfers between devices, exchange_over(): return lax.ppermute(value, ('comp', axis), pairs)  6.73 us
    ppermute x4, starting transfers between devices, exchange(): return lax.ppermute(value, axis, pairs)  5.2 us
    pallas_call x1, Pallas kernels, on_device(): kernel_call(outer_kernel, f32(*state.shape), [vmem_spec()] * (5 + len(lai...  2.58 us
    ppermute x5, waiting for transfers between devices, exchange_over(): return lax.ppermute(value, ('comp', axis), pairs)  1.95 us
    pallas_call x1, Pallas kernels, on_device(): kernel_call(inner_kernel, (f32(rows + 2 * STEPS, levels, 128), f32(2, lev...  1.41 us
    unnamed x14, local copies, waits for them, and re-layouts  0.97 us
    pallas_call x1, Pallas kernels, on_device(): kernel_call(edge_kernel, (f32(FOLD, 128),) * 2 + (f32(STEPS, levels, 128)...  0.54 us
  transfers between devices with their start and end apart: 9, of which 3 were waited for; matrix products, arithmetic and copies ran while one was open for 0% of the time, Pallas kernels for 12%

profile of v5, /device:TPU:0, one launch (start us, length us, event | category | flops | bytes accessed | tf_op | source)
XLA Modules:
  0.0 20.5 jit_solution(15542026638670752789)
XLA Ops:
  0.0 0.0 copy-start
  0.0 0.0 copy-start.2
  0.0 0.0 copy-start.3
  0.0 0.0 copy-start.4
  0.0 0.0 copy-start.5
  0.0 0.9 %copy-done = f32[1,80,8,128]{3,2,1,0:T(8,128)S(1)} copy-done((f32[1,80,8,128]{3,2,1,0:T(8,128)S(1)}, f32[1,80,8,128]{3,2,1,0:T(8,128)}, u32[]{:S(2)}) %copy-start) | copy-done | bytes 327704
  1.0 0.0 copy-done.2
  1.0 0.0 copy-done.3
  1.0 0.0 copy-done.4
  1.0 0.0 copy-done.5
  1.0 0.2 shard_map.74.refs_1_
  1.2 0.0 copy-start.1
  1.2 0.5 %collective-permute-start = (f32[24,128]{1,0:T(8,128)S(1)}, f32[24,128]{1,0:T(8,128)S(1)}, u32[]{:S(2)}, u32[]{:S(2)}) collective-permute-start(f32[24,128]{1,0:T(8,128)S(1)} %shard_map.74.refs_1_), channel_id=1, source_target_pairs={{0,16},{16,0},{1,17},{17,1},{2,18},{18,2},{3,19},{19,3},{4,20},{20... | collective-permute-start | bytes 36872 | tf_op jit(solution)/shard_map/ppermute | solution.py:428
  1.7 0.5 %shard_map.75 = (f32[24,128]{1,0:T(8,128)S(1)}, f32[24,128]{1,0:T(8,128)S(1)}, f32[4,80,128]{2,1,0:T(8,128)S(1)}, f32[4,80,128]{2,1,0:T(8,128)S(1)}) custom-call(f32[1,80,8,128]{3,2,1,0:T(8,128)S(1)} %copy-done), custom_call_target="tpu_custom_call" | custom-call | flops 2000000000 | bytes 900000 | tf_op jit(solution)/shard_map/pallas_call | solution.py:469
  2.2 0.0 copy-start.6
  2.2 2.6 %collective-permute-start.1 = (f32[4,80,128]{2,1,0:T(8,128)S(1)}, f32[4,80,128]{2,1,0:T(8,128)S(1)}, u32[]{:S(2)}, u32[]{:S(2)}) collective-permute-start(f32[4,80,128]{2,1,0:T(8,128)S(1)} %get-tuple-element.29), channel_id=1, source_target_pairs={{0,4},{4,0},{8,12},{12,8},{1,5},{5,1},{9,13},{13,9},{2,6},{6,2},{1... | collective-permute-start | bytes 491528 | tf_op jit(solution)/shard_map/ppermute | solution.py:428
  4.8 0.0 copy-done.1
  4.8 0.0 copy-done.6
  4.8 0.1 shard_map.76
  4.9 0.0 collective-permute-done.refs_0_
  5.0 3.5 %collective-permute-start.4 = (f32[40,128]{1,0:T(8,128)S(1)}, f32[40,128]{1,0:T(8,128)S(1)}, u32[]{:S(2)}, u32[]{:S(2)}) collective-permute-start(f32[40,128]{1,0:T(8,128)S(1)} %get-tuple-element.49), channel_id=1, source_target_pairs={{0,19},{1,18},{2,17},{3,16},{16,3},{17,2},{18,1},{19,0},{4,23},{5,... | collective-permute-start | bytes 61448 | tf_op jit(solution)/shard_map/ppermute | solution.py:438
  8.4 0.0 collective-permute-start.2
  8.4 0.5 %collective-permute-start.3 = (f32[16,128]{1,0:T(8,128)S(1)}, f32[16,128]{1,0:T(8,128)S(1)}, u32[]{:S(2)}, u32[]{:S(2)}) collective-permute-start(f32[16,128]{1,0:T(8,128)S(1)} %slice.6), channel_id=1, source_target_pairs={{0,18},{1,19},{2,16},{3,17},{16,2},{17,3},{18,0},{19,1},{4,22},{5,... | collective-permute-start | bytes 24584 | tf_op jit(solution)/shard_map/ppermute | solution.py:438
  9.0 1.8 %collective-permute-start.8 = (f32[4,80,128]{2,1,0:T(8,128)S(1)}, f32[4,80,128]{2,1,0:T(8,128)S(1)}, u32[]{:S(2)}, u32[]{:S(2)}) collective-permute-start(f32[4,80,128]{2,1,0:T(8,128)S(1)} %get-tuple-element.42), channel_id=1, source_target_pairs={{0,12},{4,8},{8,4},{12,0},{1,13},{5,9},{9,5},{13,1},{2,14},{6,10},... | collective-permute-start | bytes 491528 | tf_op jit(solution)/shard_map/ppermute | solution.py:428
  10.8 0.0 collective-permute-done.1.rows1_ref
  10.8 1.7 %collective-permute-done.3.refs_3_ = f32[16,128]{1,0:T(8,128)S(1)} collective-permute-done((f32[16,128]{1,0:T(8,128)S(1)}, f32[16,128]{1,0:T(8,128)S(1)}, u32[]{:S(2)}, u32[]{:S(2)}) %collective-permute-start.3) | collective-permute-done | bytes 8224 | tf_op jit(solution)/shard_map/ppermute | solution.py:438
  12.4 0.0 collective-permute-done.4.refs_4_
  12.4 0.0 collective-permute-done.2.refs_2_
  12.4 0.4 %shard_map.77 = (f32[104,128]{1,0:T(8,128)S(1)}, f32[32,128]{1,0:T(8,128)S(1)}, f32[32,128]{1,0:T(8,128)S(1)}) custom-call(f32[24,128]{1,0:T(8,128)S(1)} %collective-permute-done.refs_0_, f32[24,128]{1,0:T(8,128)S(1)} %shard_map.74.refs_1_, f32[40,128]{1,0:T(8,128)S(1)} %collective-permute-done.2.refs_2_, f32[16,128]{1,0:T(8,128)S(1)} %collective-permute-done.3.refs_3_, ...), custom_call_target="tpu_custom_call" | custom-call | flops 3000000000 | bytes 100000 | tf_op jit(solution)/shard_map/pallas_call | solution.py:503
  12.8 0.3 %collective-permute-start.5 = (f32[104,128]{1,0:T(8,128)S(1)}, f32[104,128]{1,0:T(8,128)S(1)}, u32[]{:S(2)}, u32[]{:S(2)}) collective-permute-start(f32[104,128]{1,0:T(8,128)S(1)} %get-tuple-element.36), channel_id=1, source_target_pairs={{0,16},{16,0},{1,17},{17,1},{2,18},{18,2},{3,19},{19,3},{4,20},{20... | collective-permute-start | bytes 159752 | tf_op jit(solution)/shard_map/ppermute | solution.py:428
  13.2 1.6 %collective-permute-start.6 = (f32[32,128]{1,0:T(8,128)S(1)}, f32[32,128]{1,0:T(8,128)S(1)}, u32[]{:S(2)}, u32[]{:S(2)}) collective-permute-start(f32[32,128]{1,0:T(8,128)S(1)} %get-tuple-element.37), channel_id=1, source_target_pairs={{0,28},{4,24},{8,20},{12,16},{16,12},{20,8},{24,4},{28,0},{1,29},{... | collective-permute-start | bytes 49160 | tf_op jit(solution)/shard_map/ppermute | solution.py:438
  14.8 1.1 %collective-permute-start.7 = (f32[32,128]{1,0:T(8,128)S(1)}, f32[32,128]{1,0:T(8,128)S(1)}, u32[]{:S(2)}, u32[]{:S(2)}) collective-permute-start(f32[32,128]{1,0:T(8,128)S(1)} %get-tuple-element.38), channel_id=1, source_target_pairs={{0,20},{4,16},{8,28},{12,24},{16,4},{20,0},{24,12},{28,8},{1,21},{... | collective-permute-start | bytes 49160 | tf_op jit(solution)/shard_map/ppermute | solution.py:438
  15.9 0.4 %collective-permute-done.8.rows2_ref = f32[4,80,128]{2,1,0:T(8,128)S(1)} collective-permute-done((f32[4,80,128]{2,1,0:T(8,128)S(1)}, f32[4,80,128]{2,1,0:T(8,128)S(1)}, u32[]{:S(2)}, u32[]{:S(2)}) %collective-permute-start.8) | collective-permute-done | bytes 163872 | tf_op jit(solution)/shard_map/ppermute | solution.py:428
  16.3 0.0 collective-permute-done.5.own_ref
  16.3 1.4 %shard_map.78 = (f32[16,80,128]{2,1,0:T(8,128)S(1)}, f32[2,80,128]{2,1,0:T(8,128)S(1)}, f32[8,80,128]{2,1,0:T(8,128)S(1)}, f32[6,80,128]{2,1,0:T(8,128)S(1)}, f3...) custom-call(f32[1,80,8,128]{3,2,1,0:T(8,128)S(1)} %copy-done, f32[104,128]{1,0:T(8,128)S(1)} %collective-permute-done.5.own_ref, ...), custom_call_target="tpu_custom_call" | custom-call | flops 2000000000 | bytes 2000000 | tf_op jit(solution)/shard_map/pallas_call | solution.py:514
  17.7 0.0 collective-permute-done.6.msg2_ref
  17.7 0.3 %collective-permute-done.7.msg1_ref = f32[32,128]{1,0:T(8,128)S(1)} collective-permute-done((f32[32,128]{1,0:T(8,128)S(1)}, f32[32,128]{1,0:T(8,128)S(1)}, u32[]{:S(2)}, u32[]{:S(2)}) %collective-permute-start.7) | collective-permute-done | bytes 16416 | tf_op jit(solution)/shard_map/ppermute | solution.py:438
  18.0 2.6 %shard_map.79 = f32[1,80,8,128]{3,2,1,0:T(8,128)} custom-call(f32[104,128]{1,0:T(8,128)S(1)} %collective-permute-done.5.own_ref, f32[32,128]{1,0:T(8,128)S(1)} %collective-permute-done.6.msg2_ref, f32[32,128]{1,0:T(8,128)S(1)} %collective-permute-done.7.msg1_ref, bf16[80,256]{1,0:T(8,128)(2,1)S(1)} %get-tuple-element.39.mix_ref, ...), custom_call_target="tpu_custom_call" | custom-call | flops 300000000 | bytes 2000000 | tf_op jit(solution)/shard_map/pallas_call | solution.py:522
  (3 shorter events, 0.0 us)
Async XLA Ops:
  0.0 1.0 %copy-start = (f32[1,80,8,128]{3,2,1,0:T(8,128)S(1)}, f32[1,80,8,128]{3,2,1,0:T(8,128)}, u32[]{:S(2)}) copy-start(f32[1,80,8,128]{3,2,1,0:T(8,128)} %state_ref.3) | copy-start | bytes 983044
  0.0 1.0 %copy-start.2 = (s32[1,1,1,4,8]{4,3,2,1,0:T(4,128)S(1)}, s32[1,1,1,4,8]{4,3,2,1,0:T(4,128)}, u32[]{:S(2)}) copy-start(s32[1,1,1,4,8]{4,3,2,1,0:T(4,128)} %links_ref.1) | copy-start | bytes 388
  0.0 1.0 %copy-start.3 = (f32[1,64]{1,0:T(1,128)S(1)}, f32[1,64]{1,0:T(1,128)}, u32[]{:S(2)}) copy-start(f32[1,64]{1,0:T(1,128)} %weights_ref.1) | copy-start | bytes 772
  0.0 1.0 %copy-start.4 = (s32[8,1]{0,1:T(1,128)S(1)}, s32[8,1]{0,1:T(1,128)}, u32[]{:S(2)}) copy-start(s32[8,1]{0,1:T(1,128)} %param.12) | copy-start | bytes 100
  0.0 1.0 %copy-start.5 = (s32[8,1]{0,1:T(1,128)S(1)}, s32[8,1]{0,1:T(1,128)}, u32[]{:S(2)}) copy-start(s32[8,1]{0,1:T(1,128)} %param.13) | copy-start | bytes 100
  1.2 3.7 %copy-start.1 = (f32[1,80,80]{2,1,0:T(8,128)S(1)}, f32[1,80,80]{2,1,0:T(8,128)}, u32[]{:S(2)}) copy-start(f32[1,80,80]{2,1,0:T(8,128)} %mixing_ref.1) | copy-start | bytes 76804
  1.2 3.8 %collective-permute-start = (f32[24,128]{1,0:T(8,128)S(1)}, f32[24,128]{1,0:T(8,128)S(1)}, u32[]{:S(2)}, u32[]{:S(2)}) collective-permute-start(f32[24,128]{1,0:T(8,128)S(1)} %shard_map.74.refs_1_), channel_id=1, source_target_pairs={{0,16},{16,0},{1,17},{17,1},{2,18},{18,2},{3,19},{19,3},{4,20},{20... | collective-permute-start | bytes 36872 | tf_op jit(solution)/shard_map/ppermute | solution.py:428
  2.2 2.6 %copy-start.6 = (f32[1,80]{1,0:T(1,128)S(1)}, f32[1,80]{1,0:T(1,128)}, u32[]{:S(2)}) copy-start(f32[1,80]{1,0:T(1,128)} %diffuse_ref.1) | copy-start | bytes 964
  2.2 8.5 %collective-permute-start.1 = (f32[4,80,128]{2,1,0:T(8,128)S(1)}, f32[4,80,128]{2,1,0:T(8,128)S(1)}, u32[]{:S(2)}, u32[]{:S(2)}) collective-permute-start(f32[4,80,128]{2,1,0:T(8,128)S(1)} %get-tuple-element.29), channel_id=1, source_target_pairs={{0,4},{4,0},{8,12},{12,8},{1,5},{5,1},{9,13},{13,9},{2,6},{6,2},{1... | collective-permute-start | bytes 491528 | tf_op jit(solution)/shard_map/ppermute | solution.py:428
  5.0 7.5 %collective-permute-start.4 = (f32[40,128]{1,0:T(8,128)S(1)}, f32[40,128]{1,0:T(8,128)S(1)}, u32[]{:S(2)}, u32[]{:S(2)}) collective-permute-start(f32[40,128]{1,0:T(8,128)S(1)} %get-tuple-element.49), channel_id=1, source_target_pairs={{0,19},{1,18},{2,17},{3,16},{16,3},{17,2},{18,1},{19,0},{4,23},{5,... | collective-permute-start | bytes 61448 | tf_op jit(solution)/shard_map/ppermute | solution.py:438
  8.4 4.0 %collective-permute-start.2 = (f32[40,128]{1,0:T(8,128)S(1)}, f32[40,128]{1,0:T(8,128)S(1)}, u32[]{:S(2)}, u32[]{:S(2)}) collective-permute-start(f32[40,128]{1,0:T(8,128)S(1)} %get-tuple-element.50), channel_id=1, source_target_pairs={{0,17},{1,16},{2,19},{3,18},{16,1},{17,0},{18,3},{19,2},{4,21},{5,... | collective-permute-start | bytes 61448 | tf_op jit(solution)/shard_map/ppermute | solution.py:438
  8.4 4.0 %collective-permute-start.3 = (f32[16,128]{1,0:T(8,128)S(1)}, f32[16,128]{1,0:T(8,128)S(1)}, u32[]{:S(2)}, u32[]{:S(2)}) collective-permute-start(f32[16,128]{1,0:T(8,128)S(1)} %slice.6), channel_id=1, source_target_pairs={{0,18},{1,19},{2,16},{3,17},{16,2},{17,3},{18,0},{19,1},{4,22},{5,... | collective-permute-start | bytes 24584 | tf_op jit(solution)/shard_map/ppermute | solution.py:438
  9.0 7.3 %collective-permute-start.8 = (f32[4,80,128]{2,1,0:T(8,128)S(1)}, f32[4,80,128]{2,1,0:T(8,128)S(1)}, u32[]{:S(2)}, u32[]{:S(2)}) collective-permute-start(f32[4,80,128]{2,1,0:T(8,128)S(1)} %get-tuple-element.42), channel_id=1, source_target_pairs={{0,12},{4,8},{8,4},{12,0},{1,13},{5,9},{9,5},{13,1},{2,14},{6,10},... | collective-permute-start | bytes 491528 | tf_op jit(solution)/shard_map/ppermute | solution.py:428
  12.8 3.4 %collective-permute-start.5 = (f32[104,128]{1,0:T(8,128)S(1)}, f32[104,128]{1,0:T(8,128)S(1)}, u32[]{:S(2)}, u32[]{:S(2)}) collective-permute-start(f32[104,128]{1,0:T(8,128)S(1)} %get-tuple-element.36), channel_id=1, source_target_pairs={{0,16},{16,0},{1,17},{17,1},{2,18},{18,2},{3,19},{19,3},{4,20},{20... | collective-permute-start | bytes 159752 | tf_op jit(solution)/shard_map/ppermute | solution.py:428
  13.2 4.5 %collective-permute-start.6 = (f32[32,128]{1,0:T(8,128)S(1)}, f32[32,128]{1,0:T(8,128)S(1)}, u32[]{:S(2)}, u32[]{:S(2)}) collective-permute-start(f32[32,128]{1,0:T(8,128)S(1)} %get-tuple-element.37), channel_id=1, source_target_pairs={{0,28},{4,24},{8,20},{12,16},{16,12},{20,8},{24,4},{28,0},{1,29},{... | collective-permute-start | bytes 49160 | tf_op jit(solution)/shard_map/ppermute | solution.py:438
  14.8 3.2 %collective-permute-start.7 = (f32[32,128]{1,0:T(8,128)S(1)}, f32[32,128]{1,0:T(8,128)S(1)}, u32[]{:S(2)}, u32[]{:S(2)}) collective-permute-start(f32[32,128]{1,0:T(8,128)S(1)} %get-tuple-element.38), channel_id=1, source_target_pairs={{0,20},{4,16},{8,28},{12,24},{16,4},{20,0},{24,12},{28,8},{1,21},{... | collective-permute-start | bytes 49160 | tf_op jit(solution)/shard_map/ppermute | solution.py:438

commit v6 on v5

--- a/solution.py
+++ b/solution.py
@@ -102,11 +102,9 @@
     lon_odd = lax.rem(lax.axis_index("lon"), 2) == 1
     lane = lane_ids((levels, 128))
     first = last = jnp.zeros((levels, 128), jnp.float32)
-    tiles = []
+    tiles = jnp.swapaxes(state_ref[0], 0, 1)
     for row in range(rows):
-        tile = state_ref[0, :, row, :]
-        tiles.append(tile)
-        turned = roll(tile, row * EDGE)
+        turned = roll(tiles[row], row * EDGE)
         first = jnp.where(lane // EDGE == row, turned, first)
         last = jnp.where(lane // EDGE == (row - 1) % (128 // EDGE), turned, last)
     last = roll(last, 4)
@@ -278,8 +276,7 @@
     for k in range(STEPS):
         x_ref[first_at + k] = rows1_ref[k]
         x_ref[rows + STEPS - first_at + k] = jnp.where(inside, rows2_ref[k], 0.0)
-    for row in range(rows):
-        x_ref[STEPS + row] = state_ref[0, :, row, :]
+    x_ref[STEPS : STEPS + rows] = jnp.swapaxes(state_ref[0], 0, 1)
     update = Update(mix_ref, rate_ref)
     flux = [own_ref[levels + r : levels + r + 1] for r in range(rows)]
     deep = [own_ref[levels + rows + r : levels + rows + r + 1] for r in range(rows)]
@@ -374,9 +371,11 @@
             return inner_refs[step - 1][s - 3 - step]
         return outer_refs[step - 1][s - step if s < slots // 2 else s - (slots - 6 - step)]
 
+    done = [None] * rows
+
     def put(s, tile):
         tile = jnp.where((lane < 4) | (lane >= cells - 4), roll(sides, -s * EDGE), tile)
-        out_ref[0, :, s - STEPS, :] = tile
+        done[s - STEPS] = tile
 
     for step in range(STEPS):
         last = step == STEPS - 1
@@ -403,6 +402,7 @@
                     outer_refs[step][k + j] = tile
     for s in (slots // 2 - 1, slots // 2):
         put(s, inner_refs[STEPS - 1][s - slots // 2 + 1])
+    out_ref[0] = jnp.swapaxes(jnp.stack(done, axis=0), 0, 1)
 
 
 def kernel_call(body, out_shape, blocks, scratch=(), flops=0, nbytes=0, vmem=VMEM_LIMIT, grid=()):

time: 20.7 us -> 20.3 us (0.981)
  Pallas kernels: 5.2 us -> 4.78 us
    pallas_call x1, Pallas kernels: 0.54 us -> 0.27 us  [on_device(): kernel_call(edge_kernel, (f32(FOLD, 128),) * 2 + (f32(STEPS, levels, 128)...]
  transfers between devices with their start and end apart: 9 -> 9, of which waited for: 3 -> 3; matrix products, arithmetic and copies ran while one was open for 0% -> 0% of each run, Pallas kernels for 12% -> 10%
where the time goes in v6:
time: 20.3 us; the launch traced here: 20.2 us
  starting transfers between devices  11.9 us (59%)
  Pallas kernels  4.78 us (24%)
  waiting for transfers between devices  2.41 us (12%)
  local copies, waits for them, and re-layouts  0.98 us (5%)
    ppermute x5, starting transfers between devices, exchange_over(): return lax.ppermute(value, ('comp', axis), pairs)  6.73 us
    ppermute x4, starting transfers between devices, exchange(): return lax.ppermute(value, axis, pairs)  5.2 us
    pallas_call x1, Pallas kernels, on_device(): kernel_call(outer_kernel, f32(*state.shape), [vmem_spec()] * (5 + len(lai...  2.51 us
    ppermute x5, waiting for transfers between devices, exchange_over(): return lax.ppermute(value, ('comp', axis), pairs)  2.02 us
    pallas_call x1, Pallas kernels, on_device(): kernel_call(inner_kernel, (f32(rows + 2 * STEPS, levels, 128), f32(2, lev...  1.33 us
    unnamed x14, local copies, waits for them, and re-layouts  0.97 us
  transfers between devices with their start and end apart: 9, of which 3 were waited for; matrix products, arithmetic and copies ran while one was open for 0% of the time, Pallas kernels for 10%

profile of v6, /device:TPU:0, one launch (start us, length us, event | category | flops | bytes accessed | tf_op | source)
XLA Modules:
  0.0 20.2 jit_solution(7931687479018995371)
XLA Ops:
  0.0 0.0 copy-start
  0.0 0.0 copy-start.2
  0.0 0.0 copy-start.3
  0.0 0.0 copy-start.4
  0.0 0.0 copy-start.5
  0.0 0.9 %copy-done = f32[1,80,8,128]{3,2,1,0:T(8,128)S(1)} copy-done((f32[1,80,8,128]{3,2,1,0:T(8,128)S(1)}, f32[1,80,8,128]{3,2,1,0:T(8,128)}, u32[]{:S(2)}) %copy-start) | copy-done | bytes 327704
  1.0 0.0 copy-done.2
  1.0 0.0 copy-done.3
  1.0 0.0 copy-done.4
  1.0 0.0 copy-done.5
  1.0 0.2 shard_map.74.refs_1_
  1.2 0.0 copy-start.1
  1.2 0.5 %collective-permute-start = (f32[24,128]{1,0:T(8,128)S(1)}, f32[24,128]{1,0:T(8,128)S(1)}, u32[]{:S(2)}, u32[]{:S(2)}) collective-permute-start(f32[24,128]{1,0:T(8,128)S(1)} %shard_map.74.refs_1_), channel_id=1, source_target_pairs={{0,16},{16,0},{1,17},{17,1},{2,18},{18,2},{3,19},{19,3},{4,20},{20... | collective-permute-start | bytes 36872 | tf_op jit(solution)/shard_map/ppermute | solution.py:428
  1.7 0.3 %shard_map.75 = (f32[24,128]{1,0:T(8,128)S(1)}, f32[24,128]{1,0:T(8,128)S(1)}, f32[4,80,128]{2,1,0:T(8,128)S(1)}, f32[4,80,128]{2,1,0:T(8,128)S(1)}) custom-call(f32[1,80,8,128]{3,2,1,0:T(8,128)S(1)} %copy-done), custom_call_target="tpu_custom_call" | custom-call | flops 2000000000 | bytes 900000 | tf_op jit(solution)/shard_map/pallas_call | solution.py:469
  2.0 0.0 copy-start.6
  2.0 2.6 %collective-permute-start.1 = (f32[4,80,128]{2,1,0:T(8,128)S(1)}, f32[4,80,128]{2,1,0:T(8,128)S(1)}, u32[]{:S(2)}, u32[]{:S(2)}) collective-permute-start(f32[4,80,128]{2,1,0:T(8,128)S(1)} %get-tuple-element.29), channel_id=1, source_target_pairs={{0,4},{4,0},{8,12},{12,8},{1,5},{5,1},{9,13},{13,9},{2,6},{6,2},{1... | collective-permute-start | bytes 491528 | tf_op jit(solution)/shard_map/ppermute | solution.py:428
  4.5 0.0 copy-done.1
  4.5 0.0 copy-done.6
  4.5 0.1 shard_map.76
  4.7 0.0 collective-permute-done.refs_0_
  4.7 3.5 %collective-permute-start.4 = (f32[40,128]{1,0:T(8,128)S(1)}, f32[40,128]{1,0:T(8,128)S(1)}, u32[]{:S(2)}, u32[]{:S(2)}) collective-permute-start(f32[40,128]{1,0:T(8,128)S(1)} %get-tuple-element.49), channel_id=1, source_target_pairs={{0,19},{1,18},{2,17},{3,16},{16,3},{17,2},{18,1},{19,0},{4,23},{5,... | collective-permute-start | bytes 61448 | tf_op jit(solution)/shard_map/ppermute | solution.py:438
  8.2 0.0 collective-permute-start.2
  8.2 0.5 %collective-permute-start.3 = (f32[16,128]{1,0:T(8,128)S(1)}, f32[16,128]{1,0:T(8,128)S(1)}, u32[]{:S(2)}, u32[]{:S(2)}) collective-permute-start(f32[16,128]{1,0:T(8,128)S(1)} %slice.6), channel_id=1, source_target_pairs={{0,18},{1,19},{2,16},{3,17},{16,2},{17,3},{18,0},{19,1},{4,22},{5,... | collective-permute-start | bytes 24584 | tf_op jit(solution)/shard_map/ppermute | solution.py:438
  8.7 1.8 %collective-permute-start.8 = (f32[4,80,128]{2,1,0:T(8,128)S(1)}, f32[4,80,128]{2,1,0:T(8,128)S(1)}, u32[]{:S(2)}, u32[]{:S(2)}) collective-permute-start(f32[4,80,128]{2,1,0:T(8,128)S(1)} %get-tuple-element.42), channel_id=1, source_target_pairs={{0,12},{4,8},{8,4},{12,0},{1,13},{5,9},{9,5},{13,1},{2,14},{6,10},... | collective-permute-start | bytes 491528 | tf_op jit(solution)/shard_map/ppermute | solution.py:428
  10.5 0.0 collective-permute-done.1.rows1_ref
  10.5 1.7 %collective-permute-done.3.refs_3_ = f32[16,128]{1,0:T(8,128)S(1)} collective-permute-done((f32[16,128]{1,0:T(8,128)S(1)}, f32[16,128]{1,0:T(8,128)S(1)}, u32[]{:S(2)}, u32[]{:S(2)}) %collective-permute-start.3) | collective-permute-done | bytes 8224 | tf_op jit(solution)/shard_map/ppermute | solution.py:438
  12.2 0.0 collective-permute-done.4.refs_4_
  12.2 0.0 collective-permute-done.2.refs_2_
  12.2 0.4 %shard_map.77 = (f32[104,128]{1,0:T(8,128)S(1)}, f32[32,128]{1,0:T(8,128)S(1)}, f32[32,128]{1,0:T(8,128)S(1)}) custom-call(f32[24,128]{1,0:T(8,128)S(1)} %collective-permute-done.refs_0_, f32[24,128]{1,0:T(8,128)S(1)} %shard_map.74.refs_1_, f32[40,128]{1,0:T(8,128)S(1)} %collective-permute-done.2.refs_2_, f32[16,128]{1,0:T(8,128)S(1)} %collective-permute-done.3.refs_3_, ...), custom_call_target="tpu_custom_call" | custom-call | flops 3000000000 | bytes 100000 | tf_op jit(solution)/shard_map/pallas_call | solution.py:503
  12.6 0.3 %collective-permute-start.5 = (f32[104,128]{1,0:T(8,128)S(1)}, f32[104,128]{1,0:T(8,128)S(1)}, u32[]{:S(2)}, u32[]{:S(2)}) collective-permute-start(f32[104,128]{1,0:T(8,128)S(1)} %get-tuple-element.36), channel_id=1, source_target_pairs={{0,16},{16,0},{1,17},{17,1},{2,18},{18,2},{3,19},{19,3},{4,20},{20... | collective-permute-start | bytes 159752 | tf_op jit(solution)/shard_map/ppermute | solution.py:428
  12.9 1.6 %collective-permute-start.6 = (f32[32,128]{1,0:T(8,128)S(1)}, f32[32,128]{1,0:T(8,128)S(1)}, u32[]{:S(2)}, u32[]{:S(2)}) collective-permute-start(f32[32,128]{1,0:T(8,128)S(1)} %get-tuple-element.37), channel_id=1, source_target_pairs={{0,28},{4,24},{8,20},{12,16},{16,12},{20,8},{24,4},{28,0},{1,29},{... | collective-permute-start | bytes 49160 | tf_op jit(solution)/shard_map/ppermute | solution.py:438
  14.5 1.1 %collective-permute-start.7 = (f32[32,128]{1,0:T(8,128)S(1)}, f32[32,128]{1,0:T(8,128)S(1)}, u32[]{:S(2)}, u32[]{:S(2)}) collective-permute-start(f32[32,128]{1,0:T(8,128)S(1)} %get-tuple-element.38), channel_id=1, source_target_pairs={{0,20},{4,16},{8,28},{12,24},{16,4},{20,0},{24,12},{28,8},{1,21},{... | collective-permute-start | bytes 49160 | tf_op jit(solution)/shard_map/ppermute | solution.py:438
  15.6 0.4 %collective-permute-done.8.rows2_ref = f32[4,80,128]{2,1,0:T(8,128)S(1)} collective-permute-done((f32[4,80,128]{2,1,0:T(8,128)S(1)}, f32[4,80,128]{2,1,0:T(8,128)S(1)}, u32[]{:S(2)}, u32[]{:S(2)}) %collective-permute-start.8) | collective-permute-done | bytes 163872 | tf_op jit(solution)/shard_map/ppermute | solution.py:428
  16.0 0.0 collective-permute-done.5.own_ref
  16.0 1.3 %shard_map.78 = (f32[16,80,128]{2,1,0:T(8,128)S(1)}, f32[2,80,128]{2,1,0:T(8,128)S(1)}, f32[8,80,128]{2,1,0:T(8,128)S(1)}, f32[6,80,128]{2,1,0:T(8,128)S(1)}, f3...) custom-call(f32[1,80,8,128]{3,2,1,0:T(8,128)S(1)} %copy-done, f32[104,128]{1,0:T(8,128)S(1)} %collective-permute-done.5.own_ref, ...), custom_call_target="tpu_custom_call" | custom-call | flops 2000000000 | bytes 2000000 | tf_op jit(solution)/shard_map/pallas_call | solution.py:514
  17.3 0.0 collective-permute-done.6.msg2_ref
  17.3 0.4 %collective-permute-done.7.msg1_ref = f32[32,128]{1,0:T(8,128)S(1)} collective-permute-done((f32[32,128]{1,0:T(8,128)S(1)}, f32[32,128]{1,0:T(8,128)S(1)}, u32[]{:S(2)}, u32[]{:S(2)}) %collective-permute-start.7) | collective-permute-done | bytes 16416 | tf_op jit(solution)/shard_map/ppermute | solution.py:438
  17.7 2.5 %shard_map.79 = f32[1,80,8,128]{3,2,1,0:T(8,128)} custom-call(f32[104,128]{1,0:T(8,128)S(1)} %collective-permute-done.5.own_ref, f32[32,128]{1,0:T(8,128)S(1)} %collective-permute-done.6.msg2_ref, f32[32,128]{1,0:T(8,128)S(1)} %collective-permute-done.7.msg1_ref, bf16[80,256]{1,0:T(8,128)(2,1)S(1)} %get-tuple-element.39.mix_ref, ...), custom_call_target="tpu_custom_call" | custom-call | flops 300000000 | bytes 2000000 | tf_op jit(solution)/shard_map/pallas_call | solution.py:522
  (3 shorter events, 0.0 us)
Async XLA Ops:
  0.0 1.0 %copy-start = (f32[1,80,8,128]{3,2,1,0:T(8,128)S(1)}, f32[1,80,8,128]{3,2,1,0:T(8,128)}, u32[]{:S(2)}) copy-start(f32[1,80,8,128]{3,2,1,0:T(8,128)} %state_ref.3) | copy-start | bytes 983044
  0.0 1.0 %copy-start.2 = (s32[1,1,1,4,8]{4,3,2,1,0:T(4,128)S(1)}, s32[1,1,1,4,8]{4,3,2,1,0:T(4,128)}, u32[]{:S(2)}) copy-start(s32[1,1,1,4,8]{4,3,2,1,0:T(4,128)} %links_ref.1) | copy-start | bytes 388
  0.0 1.0 %copy-start.3 = (f32[1,64]{1,0:T(1,128)S(1)}, f32[1,64]{1,0:T(1,128)}, u32[]{:S(2)}) copy-start(f32[1,64]{1,0:T(1,128)} %weights_ref.1) | copy-start | bytes 772
  0.0 1.0 %copy-start.4 = (s32[8,1]{0,1:T(1,128)S(1)}, s32[8,1]{0,1:T(1,128)}, u32[]{:S(2)}) copy-start(s32[8,1]{0,1:T(1,128)} %param.12) | copy-start | bytes 100
  0.0 1.0 %copy-start.5 = (s32[8,1]{0,1:T(1,128)S(1)}, s32[8,1]{0,1:T(1,128)}, u32[]{:S(2)}) copy-start(s32[8,1]{0,1:T(1,128)} %param.13) | copy-start | bytes 100
  1.2 3.4 %copy-start.1 = (f32[1,80,80]{2,1,0:T(8,128)S(1)}, f32[1,80,80]{2,1,0:T(8,128)}, u32[]{:S(2)}) copy-start(f32[1,80,80]{2,1,0:T(8,128)} %mixing_ref.1) | copy-start | bytes 76804
  1.2 3.5 %collective-permute-start = (f32[24,128]{1,0:T(8,128)S(1)}, f32[24,128]{1,0:T(8,128)S(1)}, u32[]{:S(2)}, u32[]{:S(2)}) collective-permute-start(f32[24,128]{1,0:T(8,128)S(1)} %shard_map.74.refs_1_), channel_id=1, source_target_pairs={{0,16},{16,0},{1,17},{17,1},{2,18},{18,2},{3,19},{19,3},{4,20},{20... | collective-permute-start | bytes 36872 | tf_op jit(solution)/shard_map/ppermute | solution.py:428
  2.0 2.6 %copy-start.6 = (f32[1,80]{1,0:T(1,128)S(1)}, f32[1,80]{1,0:T(1,128)}, u32[]{:S(2)}) copy-start(f32[1,80]{1,0:T(1,128)} %diffuse_ref.1) | copy-start | bytes 964
  2.0 8.5 %collective-permute-start.1 = (f32[4,80,128]{2,1,0:T(8,128)S(1)}, f32[4,80,128]{2,1,0:T(8,128)S(1)}, u32[]{:S(2)}, u32[]{:S(2)}) collective-permute-start(f32[4,80,128]{2,1,0:T(8,128)S(1)} %get-tuple-element.29), channel_id=1, source_target_pairs={{0,4},{4,0},{8,12},{12,8},{1,5},{5,1},{9,13},{13,9},{2,6},{6,2},{1... | collective-permute-start | bytes 491528 | tf_op jit(solution)/shard_map/ppermute | solution.py:428
  4.7 7.5 %collective-permute-start.4 = (f32[40,128]{1,0:T(8,128)S(1)}, f32[40,128]{1,0:T(8,128)S(1)}, u32[]{:S(2)}, u32[]{:S(2)}) collective-permute-start(f32[40,128]{1,0:T(8,128)S(1)} %get-tuple-element.49), channel_id=1, source_target_pairs={{0,19},{1,18},{2,17},{3,16},{16,3},{17,2},{18,1},{19,0},{4,23},{5,... | collective-permute-start | bytes 61448 | tf_op jit(solution)/shard_map/ppermute | solution.py:438
  8.2 4.0 %collective-permute-start.2 = (f32[40,128]{1,0:T(8,128)S(1)}, f32[40,128]{1,0:T(8,128)S(1)}, u32[]{:S(2)}, u32[]{:S(2)}) collective-permute-start(f32[40,128]{1,0:T(8,128)S(1)} %get-tuple-element.50), channel_id=1, source_target_pairs={{0,17},{1,16},{2,19},{3,18},{16,1},{17,0},{18,3},{19,2},{4,21},{5,... | collective-permute-start | bytes 61448 | tf_op jit(solution)/shard_map/ppermute | solution.py:438
  8.2 4.0 %collective-permute-start.3 = (f32[16,128]{1,0:T(8,128)S(1)}, f32[16,128]{1,0:T(8,128)S(1)}, u32[]{:S(2)}, u32[]{:S(2)}) collective-permute-start(f32[16,128]{1,0:T(8,128)S(1)} %slice.6), channel_id=1, source_target_pairs={{0,18},{1,19},{2,16},{3,17},{16,2},{17,3},{18,0},{19,1},{4,22},{5,... | collective-permute-start | bytes 24584 | tf_op jit(solution)/shard_map/ppermute | solution.py:438
  8.7 7.3 %collective-permute-start.8 = (f32[4,80,128]{2,1,0:T(8,128)S(1)}, f32[4,80,128]{2,1,0:T(8,128)S(1)}, u32[]{:S(2)}, u32[]{:S(2)}) collective-permute-start(f32[4,80,128]{2,1,0:T(8,128)S(1)} %get-tuple-element.42), channel_id=1, source_target_pairs={{0,12},{4,8},{8,4},{12,0},{1,13},{5,9},{9,5},{13,1},{2,14},{6,10},... | collective-permute-start | bytes 491528 | tf_op jit(solution)/shard_map/ppermute | solution.py:428
  12.6 3.4 %collective-permute-start.5 = (f32[104,128]{1,0:T(8,128)S(1)}, f32[104,128]{1,0:T(8,128)S(1)}, u32[]{:S(2)}, u32[]{:S(2)}) collective-permute-start(f32[104,128]{1,0:T(8,128)S(1)} %get-tuple-element.36), channel_id=1, source_target_pairs={{0,16},{16,0},{1,17},{17,1},{2,18},{18,2},{3,19},{19,3},{4,20},{20... | collective-permute-start | bytes 159752 | tf_op jit(solution)/shard_map/ppermute | solution.py:428
  12.9 4.4 %collective-permute-start.6 = (f32[32,128]{1,0:T(8,128)S(1)}, f32[32,128]{1,0:T(8,128)S(1)}, u32[]{:S(2)}, u32[]{:S(2)}) collective-permute-start(f32[32,128]{1,0:T(8,128)S(1)} %get-tuple-element.37), channel_id=1, source_target_pairs={{0,28},{4,24},{8,20},{12,16},{16,12},{20,8},{24,4},{28,0},{1,29},{... | collective-permute-start | bytes 49160 | tf_op jit(solution)/shard_map/ppermute | solution.py:438
  14.5 3.2 %collective-permute-start.7 = (f32[32,128]{1,0:T(8,128)S(1)}, f32[32,128]{1,0:T(8,128)S(1)}, u32[]{:S(2)}, u32[]{:S(2)}) collective-permute-start(f32[32,128]{1,0:T(8,128)S(1)} %get-tuple-element.38), channel_id=1, source_target_pairs={{0,20},{4,16},{8,28},{12,24},{16,4},{20,0},{24,12},{28,8},{1,21},{... | collective-permute-start | bytes 49160 | tf_op jit(solution)/shard_map/ppermute | solution.py:438

commit v7 on v6

--- a/solution.py
+++ b/solution.py
@@ -78,7 +78,7 @@
     out_ref[count + 8 :] = surface
 
 
-def operator_kernel(mixing_ref, diffuse_ref, mix_ref, rate_ref):
+def write_operators(mixing_ref, diffuse_ref, mix_ref, rate_ref):
     levels = mixing_ref.shape[1]
     mix = mixing_ref[0]
     top = mix.astype(jnp.bfloat16)
@@ -126,7 +126,7 @@
 
 
 def flux_kernel(count, slices, east_west, *refs):
-    crossed_ref, *packs, own_ref, first_ref, second_ref = refs
+    crossed_ref, zero_ref, *packs, own_ref, first_ref, second_ref = refs
     surface = crossed_ref[count + 8 :]
     rows = surface.shape[0]
     levels = own_ref.shape[0] - 2 * rows - 8
@@ -199,7 +199,7 @@
     own_ref[levels + rows : levels + 2 * rows] = deep
     own_ref[levels + 2 * rows : levels + 2 * rows + 1] = roll(flux_beside, STEPS * EDGE)
     own_ref[levels + 2 * rows + 1 : levels + 2 * rows + 2] = roll(deep_beside, STEPS * EDGE)
-    own_ref[levels + 2 * rows + 2 :] = jnp.zeros((6, 128), jnp.float32)
+    own_ref[levels + 2 * rows + 2 :] = zero_ref[0:6]
     width = STEPS * EDGE
     sides = []
     for at in (0, rows - STEPS):
@@ -268,7 +268,9 @@
     return lax.rem(lat, 2) == 1, (lat > 0) & (lat < lax.axis_size("lat") - 1)
 
 
-def inner_kernel(state_ref, own_ref, rows1_ref, rows2_ref, mix_ref, rate_ref, x_ref, side_ref, *inner_refs):
+def inner_kernel(
+    state_ref, own_ref, rows1_ref, rows2_ref, mixing_ref, diffuse_ref, mix_ref, rate_ref, x_ref, side_ref, *inner_refs
+):
     levels, rows, cells = state_ref.shape[1:]
     slots = rows + 2 * STEPS
     odd, inside = lat_place()
@@ -277,6 +279,7 @@
         x_ref[first_at + k] = rows1_ref[k]
         x_ref[rows + STEPS - first_at + k] = jnp.where(inside, rows2_ref[k], 0.0)
     x_ref[STEPS : STEPS + rows] = jnp.swapaxes(state_ref[0], 0, 1)
+    write_operators(mixing_ref, diffuse_ref, mix_ref, rate_ref)
     update = Update(mix_ref, rate_ref)
     flux = [own_ref[levels + r : levels + r + 1] for r in range(rows)]
     deep = [own_ref[levels + rows + r : levels + rows + r + 1] for r in range(rows)]
@@ -474,18 +477,10 @@
         nbytes=900_000,
         vmem=FRONT_VMEM_LIMIT,
     )(state)
-    operators = kernel_call(
-        operator_kernel,
-        (
-            jax.ShapeDtypeStruct((levels, 256), jnp.bfloat16),
-            f32(2, levels, 128),
-        ),
-        [vmem_spec()] * 2,
-        flops=2_000_000_000,
-        nbytes=100_000,
-        vmem=FRONT_VMEM_LIMIT,
-    )(mixing, diffusivity)
-    operators, edge_near = lax.optimization_barrier((operators, edge_near))
+    spare = kernel_call(
+        zero_kernel, f32(16, 128), [], flops=2_000_000_000, nbytes=4096, vmem=FRONT_VMEM_LIMIT
+    )()
+    spare, edge_near = lax.optimization_barrier((spare, edge_near))
     beside_1 = exchange_over(jnp.concatenate([edge_near, crossed[:pack_rows]], axis=0), "lon", near)
     beside_2 = exchange_over(jnp.concatenate([edge_far, crossed[:pack_rows]], axis=0), "lon", far_round)
     if lon_count == 4:
@@ -503,30 +498,35 @@
     own, for_first, for_second = kernel_call(
         functools.partial(flux_kernel, count, slices, east_west),
         (f32(levels + 2 * rows + 8, 128),) + (f32(FOLD + 2 * STEPS, 128),) * 2,
-        [vmem_spec()] * (1 + len(packs)),
+        [vmem_spec()] * (2 + len(packs)),
         flops=3_000_000_000,
         nbytes=100_000,
         vmem=FRONT_VMEM_LIMIT,
-    )(crossed, *packs)
+    )(crossed, spare, *packs)
     own = exchange(own, "comp", near)
     message_2 = exchange_over(for_second, "lat", far_lat)
     message_1 = exchange_over(for_first, "lat", near)
     laid_out = kernel_call(
         inner_kernel,
-        (f32(rows + 2 * STEPS, levels, 128), f32(2, levels, 128))
+        (
+            jax.ShapeDtypeStruct((levels, 256), jnp.bfloat16),
+            f32(2, levels, 128),
+            f32(rows + 2 * STEPS, levels, 128),
+            f32(2, levels, 128),
+        )
         + tuple(f32(rows - 2 * k, levels, 128) for k in range(STEPS)),
         [vmem_spec()] * 6,
         flops=2_000_000_000,
         nbytes=2_000_000,
-    )(state, own, rows_1, rows_2, *operators)
+    )(state, own, rows_1, rows_2, mixing, diffusivity)
     return kernel_call(
         outer_kernel,
         f32(*state.shape),
-        [vmem_spec()] * (5 + len(laid_out)),
+        [vmem_spec()] * (3 + len(laid_out)),
         scratch=[pltpu.VMEM((6, levels, 128), jnp.float32)] * (STEPS - 1),
         flops=300_000_000,
         nbytes=2_000_000,
-    )(own, message_2, message_1, *operators, *laid_out)
+    )(own, message_2, message_1, *laid_out)
 
 
 def solution(mesh):

time: 20.3 us -> 20 us (0.985)
  transfers between devices with their start and end apart: 9 -> 9, of which waited for: 3 -> 3; matrix products, arithmetic and copies ran while one was open for 0% -> 0% of each run, Pallas kernels for 10% -> 11%
where the time goes in v7:
time: 20 us; the launch traced here: 19.9 us
  starting transfers between devices  11.8 us (59%)
  Pallas kernels  4.78 us (24%)
  waiting for transfers between devices  2.28 us (11%)
  local copies, waits for them, and re-layouts  0.97 us (5%)
    ppermute x5, starting transfers between devices, exchange_over(): return lax.ppermute(value, ('comp', axis), pairs)  6.73 us
    ppermute x4, starting transfers between devices, exchange(): return lax.ppermute(value, axis, pairs)  5.07 us
    pallas_call x1, Pallas kernels, on_device(): kernel_call(outer_kernel, f32(*state.shape), [vmem_spec()] * (3 + len(lai...  2.51 us
    ppermute x5, waiting for transfers between devices, exchange_over(): return lax.ppermute(value, ('comp', axis), pairs)  1.9 us
    pallas_call x1, Pallas kernels, on_device(): kernel_call(inner_kernel, (jax.ShapeDtypeStruct((levels, 256), jnp.bfloat...  1.42 us
    unnamed x14, local copies, waits for them, and re-layouts  0.97 us
    pallas_call x1, Pallas kernels, on_device(): kernel_call(functools.partial(flux_kernel, count, slices, east_west), (f3...  0.4 us
  transfers between devices with their start and end apart: 9, of which 3 were waited for; matrix products, arithmetic and copies ran while one was open for 0% of the time, Pallas kernels for 11%

profile of v7, /device:TPU:0, one launch (start us, length us, event | category | flops | bytes accessed | tf_op | source)
XLA Modules:
  0.0 19.9 jit_solution(12502582293666046029)
XLA Ops:
  0.0 0.0 copy-start
  0.0 0.0 copy-start.2
  0.0 0.0 copy-start.3
  0.0 0.0 copy-start.4
  0.0 0.0 copy-start.5
  0.0 0.9 %copy-done = f32[1,80,8,128]{3,2,1,0:T(8,128)S(1)} copy-done((f32[1,80,8,128]{3,2,1,0:T(8,128)S(1)}, f32[1,80,8,128]{3,2,1,0:T(8,128)}, u32[]{:S(2)}) %copy-start) | copy-done | bytes 327704
  1.0 0.0 copy-done.2
  1.0 0.0 copy-done.3
  1.0 0.0 copy-done.4
  1.0 0.0 copy-done.5
  1.0 0.2 shard_map.74.refs_2_
  1.2 0.5 %collective-permute-start = (f32[24,128]{1,0:T(8,128)S(1)}, f32[24,128]{1,0:T(8,128)S(1)}, u32[]{:S(2)}, u32[]{:S(2)}) collective-permute-start(f32[24,128]{1,0:T(8,128)S(1)} %shard_map.74.refs_2_), channel_id=1, source_target_pairs={{0,16},{16,0},{1,17},{17,1},{2,18},{18,2},{3,19},{19,3},{4,20},{20... | collective-permute-start | bytes 36872 | tf_op jit(solution)/shard_map/ppermute | solution.py:431
  1.6 0.3 %shard_map.76 = (f32[24,128]{1,0:T(8,128)S(1)}, f32[24,128]{1,0:T(8,128)S(1)}, f32[4,80,128]{2,1,0:T(8,128)S(1)}, f32[4,80,128]{2,1,0:T(8,128)S(1)}) custom-call(f32[1,80,8,128]{3,2,1,0:T(8,128)S(1)} %copy-done), custom_call_target="tpu_custom_call" | custom-call | flops 2000000000 | bytes 900000 | tf_op jit(solution)/shard_map/pallas_call | solution.py:472
  1.9 2.6 %collective-permute-start.1 = (f32[4,80,128]{2,1,0:T(8,128)S(1)}, f32[4,80,128]{2,1,0:T(8,128)S(1)}, u32[]{:S(2)}, u32[]{:S(2)}) collective-permute-start(f32[4,80,128]{2,1,0:T(8,128)S(1)} %get-tuple-element.30), channel_id=1, source_target_pairs={{0,4},{4,0},{8,12},{12,8},{1,5},{5,1},{9,13},{13,9},{2,6},{6,2},{1... | collective-permute-start | bytes 491528 | tf_op jit(solution)/shard_map/ppermute | solution.py:431
  4.5 0.0 collective-permute-done.refs_0_
  4.5 3.5 %collective-permute-start.4 = (f32[40,128]{1,0:T(8,128)S(1)}, f32[40,128]{1,0:T(8,128)S(1)}, u32[]{:S(2)}, u32[]{:S(2)}) collective-permute-start(f32[40,128]{1,0:T(8,128)S(1)} %get-tuple-element.47), channel_id=1, source_target_pairs={{0,19},{1,18},{2,17},{3,16},{16,3},{17,2},{18,1},{19,0},{4,23},{5,... | collective-permute-start | bytes 61448 | tf_op jit(solution)/shard_map/ppermute | solution.py:441
  8.0 0.0 collective-permute-start.2
  8.0 0.5 %collective-permute-start.3 = (f32[16,128]{1,0:T(8,128)S(1)}, f32[16,128]{1,0:T(8,128)S(1)}, u32[]{:S(2)}, u32[]{:S(2)}) collective-permute-start(f32[16,128]{1,0:T(8,128)S(1)} %slice.6), channel_id=1, source_target_pairs={{0,18},{1,19},{2,16},{3,17},{16,2},{17,3},{18,0},{19,1},{4,22},{5,... | collective-permute-start | bytes 24584 | tf_op jit(solution)/shard_map/ppermute | solution.py:441
  8.5 0.0 copy-start.1
  8.5 1.7 %collective-permute-start.8 = (f32[4,80,128]{2,1,0:T(8,128)S(1)}, f32[4,80,128]{2,1,0:T(8,128)S(1)}, u32[]{:S(2)}, u32[]{:S(2)}) collective-permute-start(f32[4,80,128]{2,1,0:T(8,128)S(1)} %get-tuple-element.38), channel_id=1, source_target_pairs={{0,12},{4,8},{8,4},{12,0},{1,13},{5,9},{9,5},{13,1},{2,14},{6,10},... | collective-permute-start | bytes 491528 | tf_op jit(solution)/shard_map/ppermute | solution.py:431
  10.2 0.0 collective-permute-done.1.rows1_ref
  10.2 1.7 %collective-permute-done.3.refs_4_ = f32[16,128]{1,0:T(8,128)S(1)} collective-permute-done((f32[16,128]{1,0:T(8,128)S(1)}, f32[16,128]{1,0:T(8,128)S(1)}, u32[]{:S(2)}, u32[]{:S(2)}) %collective-permute-start.3) | collective-permute-done | bytes 8224 | tf_op jit(solution)/shard_map/ppermute | solution.py:441
  11.9 0.0 collective-permute-done.4.refs_5_
  12.0 0.0 collective-permute-done.2.refs_3_
  12.0 0.4 %shard_map.77 = (f32[104,128]{1,0:T(8,128)S(1)}, f32[32,128]{1,0:T(8,128)S(1)}, f32[32,128]{1,0:T(8,128)S(1)}) custom-call(f32[24,128]{1,0:T(8,128)S(1)} %collective-permute-done.refs_0_, f32[16,128]{1,0:T(8,128)S(1)} %shard_map.75.refs_1_, f32[24,128]{1,0:T(8,128)S(1)} %shard_map.74.refs_2_, f32[40,128]{1,0:T(8,128)S(1)} %collective-permute-done.2.refs_3_, ...), custom_call_target="tpu_custom_call" | custom-call | flops 3000000000 | bytes 100000 | tf_op jit(solution)/shard_map/pallas_call | solution.py:498
  12.4 0.3 %collective-permute-start.5 = (f32[104,128]{1,0:T(8,128)S(1)}, f32[104,128]{1,0:T(8,128)S(1)}, u32[]{:S(2)}, u32[]{:S(2)}) collective-permute-start(f32[104,128]{1,0:T(8,128)S(1)} %get-tuple-element.34), channel_id=1, source_target_pairs={{0,16},{16,0},{1,17},{17,1},{2,18},{18,2},{3,19},{19,3},{4,20},{20... | collective-permute-start | bytes 159752 | tf_op jit(solution)/shard_map/ppermute | solution.py:431
  12.7 0.0 copy-start.6
  12.7 1.5 %collective-permute-start.6 = (f32[32,128]{1,0:T(8,128)S(1)}, f32[32,128]{1,0:T(8,128)S(1)}, u32[]{:S(2)}, u32[]{:S(2)}) collective-permute-start(f32[32,128]{1,0:T(8,128)S(1)} %get-tuple-element.35), channel_id=1, source_target_pairs={{0,28},{4,24},{8,20},{12,16},{16,12},{20,8},{24,4},{28,0},{1,29},{... | collective-permute-start | bytes 49160 | tf_op jit(solution)/shard_map/ppermute | solution.py:441
  14.2 1.2 %collective-permute-start.7 = (f32[32,128]{1,0:T(8,128)S(1)}, f32[32,128]{1,0:T(8,128)S(1)}, u32[]{:S(2)}, u32[]{:S(2)}) collective-permute-start(f32[32,128]{1,0:T(8,128)S(1)} %get-tuple-element.36), channel_id=1, source_target_pairs={{0,20},{4,16},{8,28},{12,24},{16,4},{20,0},{24,12},{28,8},{1,21},{... | collective-permute-start | bytes 49160 | tf_op jit(solution)/shard_map/ppermute | solution.py:441
  15.4 0.4 %collective-permute-done.8.rows2_ref = f32[4,80,128]{2,1,0:T(8,128)S(1)} collective-permute-done((f32[4,80,128]{2,1,0:T(8,128)S(1)}, f32[4,80,128]{2,1,0:T(8,128)S(1)}, u32[]{:S(2)}, u32[]{:S(2)}) %collective-permute-start.8) | collective-permute-done | bytes 163872 | tf_op jit(solution)/shard_map/ppermute | solution.py:431
  15.8 0.0 collective-permute-done.5.own_ref
  15.8 0.0 copy-done.1
  15.8 0.0 copy-done.6
  15.8 1.4 %shard_map.78 = (bf16[80,256]{1,0:T(8,128)(2,1)S(1)}, f32[2,80,128]{2,1,0:T(8,128)S(1)}, f32[16,80,128]{2,1,0:T(8,128)S(1)}, f32[2,80,128]{2,1,0:T(8,128)S(1)}, ...) custom-call(f32[1,80,8,128]{3,2,1,0:T(8,128)S(1)} %copy-done, ...), custom_call_target="tpu_custom_call" | custom-call | flops 2000000000 | bytes 2000000 | tf_op jit(solution)/shard_map/pallas_call | solution.py:509
  17.2 0.0 collective-permute-done.6.msg2_ref
  17.2 0.2 collective-permute-done.7.msg1_ref
  17.4 2.5 %shard_map.79 = f32[1,80,8,128]{3,2,1,0:T(8,128)} custom-call(f32[104,128]{1,0:T(8,128)S(1)} %collective-permute-done.5.own_ref, f32[32,128]{1,0:T(8,128)S(1)} %collective-permute-done.6.msg2_ref, f32[32,128]{1,0:T(8,128)S(1)} %collective-permute-done.7.msg1_ref, bf16[80,256]{1,0:T(8,128)(2,1)S(1)} %get-tuple-element.39.mix_ref, ...), custom_call_target="tpu_custom_call" | custom-call | flops 300000000 | bytes 2000000 | tf_op jit(solution)/shard_map/pallas_call | solution.py:522
  (4 shorter events, 0.0 us)
Async XLA Ops:
  0.0 1.0 %copy-start = (f32[1,80,8,128]{3,2,1,0:T(8,128)S(1)}, f32[1,80,8,128]{3,2,1,0:T(8,128)}, u32[]{:S(2)}) copy-start(f32[1,80,8,128]{3,2,1,0:T(8,128)} %state_ref.3) | copy-start | bytes 983044
  0.0 1.0 %copy-start.2 = (s32[1,1,1,4,8]{4,3,2,1,0:T(4,128)S(1)}, s32[1,1,1,4,8]{4,3,2,1,0:T(4,128)}, u32[]{:S(2)}) copy-start(s32[1,1,1,4,8]{4,3,2,1,0:T(4,128)} %links_ref.1) | copy-start | bytes 388
  0.0 1.0 %copy-start.3 = (f32[1,64]{1,0:T(1,128)S(1)}, f32[1,64]{1,0:T(1,128)}, u32[]{:S(2)}) copy-start(f32[1,64]{1,0:T(1,128)} %weights_ref.1) | copy-start | bytes 772
  0.0 1.0 %copy-start.4 = (s32[8,1]{0,1:T(1,128)S(1)}, s32[8,1]{0,1:T(1,128)}, u32[]{:S(2)}) copy-start(s32[8,1]{0,1:T(1,128)} %param.12) | copy-start | bytes 100
  0.0 1.0 %copy-start.5 = (s32[8,1]{0,1:T(1,128)S(1)}, s32[8,1]{0,1:T(1,128)}, u32[]{:S(2)}) copy-start(s32[8,1]{0,1:T(1,128)} %param.13) | copy-start | bytes 100
  1.2 3.3 %collective-permute-start = (f32[24,128]{1,0:T(8,128)S(1)}, f32[24,128]{1,0:T(8,128)S(1)}, u32[]{:S(2)}, u32[]{:S(2)}) collective-permute-start(f32[24,128]{1,0:T(8,128)S(1)} %shard_map.74.refs_2_), channel_id=1, source_target_pairs={{0,16},{16,0},{1,17},{17,1},{2,18},{18,2},{3,19},{19,3},{4,20},{20... | collective-permute-start | bytes 36872 | tf_op jit(solution)/shard_map/ppermute | solution.py:431
  1.9 8.3 %collective-permute-start.1 = (f32[4,80,128]{2,1,0:T(8,128)S(1)}, f32[4,80,128]{2,1,0:T(8,128)S(1)}, u32[]{:S(2)}, u32[]{:S(2)}) collective-permute-start(f32[4,80,128]{2,1,0:T(8,128)S(1)} %get-tuple-element.30), channel_id=1, source_target_pairs={{0,4},{4,0},{8,12},{12,8},{1,5},{5,1},{9,13},{13,9},{2,6},{6,2},{1... | collective-permute-start | bytes 491528 | tf_op jit(solution)/shard_map/ppermute | solution.py:431
  4.5 7.5 %collective-permute-start.4 = (f32[40,128]{1,0:T(8,128)S(1)}, f32[40,128]{1,0:T(8,128)S(1)}, u32[]{:S(2)}, u32[]{:S(2)}) collective-permute-start(f32[40,128]{1,0:T(8,128)S(1)} %get-tuple-element.47), channel_id=1, source_target_pairs={{0,19},{1,18},{2,17},{3,16},{16,3},{17,2},{18,1},{19,0},{4,23},{5,... | collective-permute-start | bytes 61448 | tf_op jit(solution)/shard_map/ppermute | solution.py:441
  8.0 4.0 %collective-permute-start.2 = (f32[40,128]{1,0:T(8,128)S(1)}, f32[40,128]{1,0:T(8,128)S(1)}, u32[]{:S(2)}, u32[]{:S(2)}) collective-permute-start(f32[40,128]{1,0:T(8,128)S(1)} %get-tuple-element.48), channel_id=1, source_target_pairs={{0,17},{1,16},{2,19},{3,18},{16,1},{17,0},{18,3},{19,2},{4,21},{5,... | collective-permute-start | bytes 61448 | tf_op jit(solution)/shard_map/ppermute | solution.py:441
  8.0 4.0 %collective-permute-start.3 = (f32[16,128]{1,0:T(8,128)S(1)}, f32[16,128]{1,0:T(8,128)S(1)}, u32[]{:S(2)}, u32[]{:S(2)}) collective-permute-start(f32[16,128]{1,0:T(8,128)S(1)} %slice.6), channel_id=1, source_target_pairs={{0,18},{1,19},{2,16},{3,17},{16,2},{17,3},{18,0},{19,1},{4,22},{5,... | collective-permute-start | bytes 24584 | tf_op jit(solution)/shard_map/ppermute | solution.py:441
  8.5 7.3 %copy-start.1 = (f32[1,80,80]{2,1,0:T(8,128)S(1)}, f32[1,80,80]{2,1,0:T(8,128)}, u32[]{:S(2)}) copy-start(f32[1,80,80]{2,1,0:T(8,128)} %mixing_ref.1) | copy-start | bytes 76804
  8.5 7.3 %collective-permute-start.8 = (f32[4,80,128]{2,1,0:T(8,128)S(1)}, f32[4,80,128]{2,1,0:T(8,128)S(1)}, u32[]{:S(2)}, u32[]{:S(2)}) collective-permute-start(f32[4,80,128]{2,1,0:T(8,128)S(1)} %get-tuple-element.38), channel_id=1, source_target_pairs={{0,12},{4,8},{8,4},{12,0},{1,13},{5,9},{9,5},{13,1},{2,14},{6,10},... | collective-permute-start | bytes 491528 | tf_op jit(solution)/shard_map/ppermute | solution.py:431
  12.4 3.4 %collective-permute-start.5 = (f32[104,128]{1,0:T(8,128)S(1)}, f32[104,128]{1,0:T(8,128)S(1)}, u32[]{:S(2)}, u32[]{:S(2)}) collective-permute-start(f32[104,128]{1,0:T(8,128)S(1)} %get-tuple-element.34), channel_id=1, source_target_pairs={{0,16},{16,0},{1,17},{17,1},{2,18},{18,2},{3,19},{19,3},{4,20},{20... | collective-permute-start | bytes 159752 | tf_op jit(solution)/shard_map/ppermute | solution.py:431
  12.7 3.1 %copy-start.6 = (f32[1,80]{1,0:T(1,128)S(1)}, f32[1,80]{1,0:T(1,128)}, u32[]{:S(2)}) copy-start(f32[1,80]{1,0:T(1,128)} %diffuse_ref.1) | copy-start | bytes 964
  12.7 4.5 %collective-permute-start.6 = (f32[32,128]{1,0:T(8,128)S(1)}, f32[32,128]{1,0:T(8,128)S(1)}, u32[]{:S(2)}, u32[]{:S(2)}) collective-permute-start(f32[32,128]{1,0:T(8,128)S(1)} %get-tuple-element.35), channel_id=1, source_target_pairs={{0,28},{4,24},{8,20},{12,16},{16,12},{20,8},{24,4},{28,0},{1,29},{... | collective-permute-start | bytes 49160 | tf_op jit(solution)/shard_map/ppermute | solution.py:441
  14.2 3.2 %collective-permute-start.7 = (f32[32,128]{1,0:T(8,128)S(1)}, f32[32,128]{1,0:T(8,128)S(1)}, u32[]{:S(2)}, u32[]{:S(2)}) collective-permute-start(f32[32,128]{1,0:T(8,128)S(1)} %get-tuple-element.36), channel_id=1, source_target_pairs={{0,20},{4,16},{8,28},{12,24},{16,4},{20,0},{24,12},{28,8},{1,21},{... | collective-permute-start | bytes 49160 | tf_op jit(solution)/shard_map/ppermute | solution.py:441

commit v8 on v7

--- a/solution.py
+++ b/solution.py
@@ -231,7 +231,7 @@
     def __init__(self, mix_ref, rate_ref):
         self.mixer, self.rate_ref = mix_ref[...], rate_ref
         self.levels = rate_ref.shape[1]
-        self.pad = jnp.zeros((self.mixer.shape[1] - 3 * self.levels, 256), jnp.bfloat16)
+        self.pad = jnp.zeros((self.mixer.shape[1] - 3 * self.levels, 128), jnp.bfloat16)
         tail = lax.broadcasted_iota(jnp.int32, (8, 128), 0)
         self.first = tail == 0
         self.tail = (tail + (self.levels - 8)).astype(jnp.float32)
@@ -243,11 +243,12 @@
         return jnp.concatenate([head, value[8:-8], tail], axis=0)
 
     def mixed(self, values):
-        value = jnp.concatenate(values, axis=1)
-        hi, lo = halves(value)
-        full = jnp.concatenate([hi, lo, hi, self.pad[:, : value.shape[1]]], axis=0)
-        out = jnp.dot(self.mixer, full, preferred_element_type=jnp.float32)
-        return [out[:, 128 * k : 128 * (k + 1)] for k in range(len(values))]
+        out = []
+        for value in values:
+            hi, lo = halves(value)
+            full = jnp.concatenate([hi, lo, hi, self.pad], axis=0)
+            out.append(jnp.dot(self.mixer, full, preferred_element_type=jnp.float32))
+        return out
 
     def settled(self, new, x, deep):
         sea = jnp.broadcast_to(deep, (self.levels - 8, 128)) > 0.0
@@ -268,18 +269,36 @@
     return lax.rem(lat, 2) == 1, (lat > 0) & (lat < lax.axis_size("lat") - 1)
 
 
-def inner_kernel(
-    state_ref, own_ref, rows1_ref, rows2_ref, mixing_ref, diffuse_ref, mix_ref, rate_ref, x_ref, side_ref, *inner_refs
-):
+def gather_sides(x_ref, slots, left, right):
+    lane = lane_ids(left.shape)
+    for slot in slots:
+        turned = roll(x_ref[slot], slot * EDGE)
+        right = jnp.where(lane // EDGE == slot, turned, right)
+        left = jnp.where(lane // EDGE == (slot - 1) % (128 // EDGE), turned, left)
+    return left, right
+
+
+def layout_kernel(state_ref, rows1_ref, mixing_ref, diffuse_ref, mix_ref, rate_ref, x_ref, side_ref):
     levels, rows, cells = state_ref.shape[1:]
-    slots = rows + 2 * STEPS
+    write_operators(mixing_ref, diffuse_ref, mix_ref, rate_ref)
     odd, inside = lat_place()
     first_at = jnp.where(odd, 0, rows + STEPS)
     for k in range(STEPS):
         x_ref[first_at + k] = rows1_ref[k]
-        x_ref[rows + STEPS - first_at + k] = jnp.where(inside, rows2_ref[k], 0.0)
     x_ref[STEPS : STEPS + rows] = jnp.swapaxes(state_ref[0], 0, 1)
-    write_operators(mixing_ref, diffuse_ref, mix_ref, rate_ref)
+    none = jnp.zeros((levels, 128), jnp.float32)
+    side_ref[0], side_ref[1] = gather_sides(x_ref, range(STEPS, STEPS + rows), none, none)
+
+
+def inner_kernel(
+    own_ref, rows2_ref, mix_ref, rate_ref, x_in_ref, side_in_ref, x_ref, side_ref, *inner_refs
+):
+    slots, levels, cells = x_ref.shape
+    rows = slots - 2 * STEPS
+    odd, inside = lat_place()
+    second_at = jnp.where(odd, rows + STEPS, 0)
+    for k in range(STEPS):
+        x_ref[second_at + k] = jnp.where(inside, rows2_ref[k], 0.0)
     update = Update(mix_ref, rate_ref)
     flux = [own_ref[levels + r : levels + r + 1] for r in range(rows)]
     deep = [own_ref[levels + rows + r : levels + rows + r + 1] for r in range(rows)]
@@ -293,18 +312,13 @@
             for s, tile in zip(pair, new):
                 target[s - at] = tile
         source, first = target, at
-    lane = lane_ids((levels, 128))
-    left = right = jnp.zeros((levels, 128), jnp.float32)
-    for slot in range(slots):
-        start = slot * EDGE
-        turned = roll(x_ref[slot], start)
-        right = jnp.where(lane // EDGE == slot, turned, right)
-        left = jnp.where(lane // EDGE == (slot - 1) % slots, turned, left)
+    halo = [*range(STEPS), *range(STEPS + rows, slots)]
+    left, right = gather_sides(x_ref, halo, side_in_ref[0], side_in_ref[1])
     side_ref[0] = roll(left, EDGE)
     side_ref[1] = right
 
 
-def outer_kernel(own_ref, msg2_ref, msg1_ref, mix_ref, rate_ref, x_ref, side_ref, *refs):
+def outer_kernel(own_ref, msg1_ref, msg2_ref, mix_ref, rate_ref, x_ref, side_ref, *refs):
     inner_refs, out_ref, outer_refs = refs[:STEPS], refs[STEPS], refs[STEPS + 1 :]
     levels, rows, cells = out_ref.shape[1:]
     slots = rows + 2 * STEPS
@@ -394,11 +408,11 @@
             sides = jnp.where(place < 4, right, roll(left, -EDGE))
         low_rows = list(range(step + 1, step + 4))
         todo = low_rows + [slots - 1 - s for s in reversed(low_rows)]
-        for k in range(0, len(todo), 2):
-            pair = todo[k : k + 2]
-            tiles = [[tile_at(step, s + j) for j in (-1, 0, 1)] for s in pair]
-            new = update.rows(tiles, [flux_rows[s] for s in pair], [deep_rows[s] for s in pair])
-            for j, (s, tile) in enumerate(zip(pair, new)):
+        for k in range(0, len(todo), 3):
+            group = todo[k : k + 3]
+            tiles = [[tile_at(step, s + j) for j in (-1, 0, 1)] for s in group]
+            new = update.rows(tiles, [flux_rows[s] for s in group], [deep_rows[s] for s in group])
+            for j, (s, tile) in enumerate(zip(group, new)):
                 if last:
                     put(s, tile)
                 else:
@@ -408,7 +422,7 @@
     out_ref[0] = jnp.swapaxes(jnp.stack(done, axis=0), 0, 1)
 
 
-def kernel_call(body, out_shape, blocks, scratch=(), flops=0, nbytes=0, vmem=VMEM_LIMIT, grid=()):
+def kernel_call(body, out_shape, blocks, scratch=(), flops=0, nbytes=0, vmem=VMEM_LIMIT, grid=(), aliases=None):
     return pl.pallas_call(
         body,
         out_shape=out_shape,
@@ -416,6 +430,7 @@
         in_specs=blocks,
         out_specs=jax.tree.map(lambda _: vmem_spec(), out_shape),
         scratch_shapes=scratch,
+        input_output_aliases=aliases or {},
         compiler_params=pltpu.CompilerParams(vmem_limit_bytes=vmem),
         cost_estimate=pl.CostEstimate(flops=flops, bytes_accessed=nbytes, transcendentals=0),
     )
@@ -494,7 +509,19 @@
         east_west = ((1, 0), (2, 0))
     rows_1 = exchange(up_down_1, "lat", near)
     rows_2 = exchange(up_down_2, "lat", far_lat)
-    rows_1, packs[0] = lax.optimization_barrier((rows_1, packs[0]))
+    *operators, tiles, sides = kernel_call(
+        layout_kernel,
+        (
+            jax.ShapeDtypeStruct((levels, 256), jnp.bfloat16),
+            f32(2, levels, 128),
+            f32(rows + 2 * STEPS, levels, 128),
+            f32(2, levels, 128),
+        ),
+        [vmem_spec()] * 4,
+        flops=100_000,
+        nbytes=100_000,
+    )(state, rows_1, mixing, diffusivity)
+    tiles, packs[0] = lax.optimization_barrier((tiles, packs[0]))
     own, for_first, for_second = kernel_call(
         functools.partial(flux_kernel, count, slices, east_west),
         (f32(levels + 2 * rows + 8, 128),) + (f32(FOLD + 2 * STEPS, 128),) * 2,
@@ -504,29 +531,25 @@
         vmem=FRONT_VMEM_LIMIT,
     )(crossed, spare, *packs)
     own = exchange(own, "comp", near)
+    message_1 = exchange_over(for_first, "lat", near)
     message_2 = exchange_over(for_second, "lat", far_lat)
-    message_1 = exchange_over(for_first, "lat", near)
-    laid_out = kernel_call(
+    stepped = kernel_call(
         inner_kernel,
-        (
-            jax.ShapeDtypeStruct((levels, 256), jnp.bfloat16),
-            f32(2, levels, 128),
-            f32(rows + 2 * STEPS, levels, 128),
-            f32(2, levels, 128),
-        )
+        (f32(rows + 2 * STEPS, levels, 128), f32(2, levels, 128))
         + tuple(f32(rows - 2 * k, levels, 128) for k in range(STEPS)),
         [vmem_spec()] * 6,
         flops=2_000_000_000,
         nbytes=2_000_000,
-    )(state, own, rows_1, rows_2, mixing, diffusivity)
+        aliases={4: 0},
+    )(own, rows_2, *operators, tiles, sides)
     return kernel_call(
         outer_kernel,
         f32(*state.shape),
-        [vmem_spec()] * (3 + len(laid_out)),
+        [vmem_spec()] * (5 + len(stepped)),
         scratch=[pltpu.VMEM((6, levels, 128), jnp.float32)] * (STEPS - 1),
         flops=300_000_000,
         nbytes=2_000_000,
-    )(own, message_2, message_1, *laid_out)
+    )(own, message_1, message_2, *operators, *stepped)
 
 
 def solution(mesh):

time: 20 us -> 20 us (level)
    pallas_call x2 -> x3, Pallas kernels: 3.94 us -> 3.87 us  [the longest x1 2.49 us: on_device(): kernel_call(outer_kernel, f32(*state.shape), [vmem_spec()] * (5 + len(ste...]
  transfers between devices with their start and end apart: 9 -> 9, of which waited for: 3 -> 3; matrix products, arithmetic and copies ran while one was open for 0% -> 0% of each run, Pallas kernels for 11% -> 10%
where the time goes in v8:
time: 20 us; the launch traced here: 19.9 us
  starting transfers between devices  11.9 us (60%)
  Pallas kernels  4.71 us (24%)
  waiting for transfers between devices  2.25 us (11%)
  local copies, waits for them, and re-layouts  0.97 us (5%)
    ppermute x5, starting transfers between devices, exchange_over(): return lax.ppermute(value, ('comp', axis), pairs)  6.74 us
    ppermute x4, starting transfers between devices, exchange(): return lax.ppermute(value, axis, pairs)  5.13 us
    pallas_call x1, Pallas kernels, on_device(): kernel_call(outer_kernel, f32(*state.shape), [vmem_spec()] * (5 + len(ste...  2.49 us
    ppermute x5, waiting for transfers between devices, exchange_over(): return lax.ppermute(value, ('comp', axis), pairs)  1.86 us
    pallas_call x1, Pallas kernels, on_device(): kernel_call(inner_kernel, (f32(rows + 2 * STEPS, levels, 128), f32(2, lev...  1.17 us
    unnamed x14, local copies, waits for them, and re-layouts  0.97 us
  transfers between devices with their start and end apart: 9, of which 3 were waited for; matrix products, arithmetic and copies ran while one was open for 0% of the time, Pallas kernels for 10%

profile of v8, /device:TPU:0, one launch (start us, length us, event | category | flops | bytes accessed | tf_op | source)
XLA Modules:
  0.0 19.9 jit_solution(13060153007200803283)
XLA Ops:
  0.0 0.0 copy-start
  0.0 0.0 copy-start.3
  0.0 0.0 copy-start.4
  0.0 0.0 copy-start.5
  0.0 0.0 copy-start.6
  0.0 0.9 %copy-done = f32[1,80,8,128]{3,2,1,0:T(8,128)S(1)} copy-done((f32[1,80,8,128]{3,2,1,0:T(8,128)S(1)}, f32[1,80,8,128]{3,2,1,0:T(8,128)}, u32[]{:S(2)}) %copy-start) | copy-done | bytes 327704
  1.0 0.0 copy-done.3
  1.0 0.0 copy-done.4
  1.0 0.0 copy-done.5
  1.0 0.0 copy-done.6
  1.0 0.2 shard_map.74.refs_2_
  1.2 0.5 %collective-permute-start = (f32[24,128]{1,0:T(8,128)S(1)}, f32[24,128]{1,0:T(8,128)S(1)}, u32[]{:S(2)}, u32[]{:S(2)}) collective-permute-start(f32[24,128]{1,0:T(8,128)S(1)} %shard_map.74.refs_2_), channel_id=1, source_target_pairs={{0,16},{16,0},{1,17},{17,1},{2,18},{18,2},{3,19},{19,3},{4,20},{20... | collective-permute-start | bytes 36872 | tf_op jit(solution)/shard_map/ppermute | solution.py:446
  1.6 0.3 %shard_map.76 = (f32[24,128]{1,0:T(8,128)S(1)}, f32[24,128]{1,0:T(8,128)S(1)}, f32[4,80,128]{2,1,0:T(8,128)S(1)}, f32[4,80,128]{2,1,0:T(8,128)S(1)}) custom-call(f32[1,80,8,128]{3,2,1,0:T(8,128)S(1)} %copy-done), custom_call_target="tpu_custom_call" | custom-call | flops 2000000000 | bytes 900000 | tf_op jit(solution)/shard_map/pallas_call | solution.py:487
  1.9 2.6 %collective-permute-start.1 = (f32[4,80,128]{2,1,0:T(8,128)S(1)}, f32[4,80,128]{2,1,0:T(8,128)S(1)}, u32[]{:S(2)}, u32[]{:S(2)}) collective-permute-start(f32[4,80,128]{2,1,0:T(8,128)S(1)} %get-tuple-element.32), channel_id=1, source_target_pairs={{0,4},{4,0},{8,12},{12,8},{1,5},{5,1},{9,13},{13,9},{2,6},{6,2},{1... | collective-permute-start | bytes 491528 | tf_op jit(solution)/shard_map/ppermute | solution.py:446
  4.5 0.0 collective-permute-done.refs_0_
  4.5 0.0 copy-start.1
  4.5 3.5 %collective-permute-start.4 = (f32[40,128]{1,0:T(8,128)S(1)}, f32[40,128]{1,0:T(8,128)S(1)}, u32[]{:S(2)}, u32[]{:S(2)}) collective-permute-start(f32[40,128]{1,0:T(8,128)S(1)} %get-tuple-element.51), channel_id=1, source_target_pairs={{0,19},{1,18},{2,17},{3,16},{16,3},{17,2},{18,1},{19,0},{4,23},{5,... | collective-permute-start | bytes 61448 | tf_op jit(solution)/shard_map/ppermute | solution.py:456
  8.0 0.0 copy-start.2
  8.0 0.0 collective-permute-start.2
  8.0 0.6 %collective-permute-start.3 = (f32[16,128]{1,0:T(8,128)S(1)}, f32[16,128]{1,0:T(8,128)S(1)}, u32[]{:S(2)}, u32[]{:S(2)}) collective-permute-start(f32[16,128]{1,0:T(8,128)S(1)} %slice.6), channel_id=1, source_target_pairs={{0,18},{1,19},{2,16},{3,17},{16,2},{17,3},{18,0},{19,1},{4,22},{5,... | collective-permute-start | bytes 24584 | tf_op jit(solution)/shard_map/ppermute | solution.py:456
  8.5 1.8 %collective-permute-start.8 = (f32[4,80,128]{2,1,0:T(8,128)S(1)}, f32[4,80,128]{2,1,0:T(8,128)S(1)}, u32[]{:S(2)}, u32[]{:S(2)}) collective-permute-start(f32[4,80,128]{2,1,0:T(8,128)S(1)} %get-tuple-element.42), channel_id=1, source_target_pairs={{0,12},{4,8},{8,4},{12,0},{1,13},{5,9},{9,5},{13,1},{2,14},{6,10},... | collective-permute-start | bytes 491528 | tf_op jit(solution)/shard_map/ppermute | solution.py:446
  10.3 0.0 collective-permute-done.1.rows1_ref
  10.3 0.0 copy-done.1
  10.3 0.0 copy-done.2
  10.3 0.2 %shard_map.77 = (bf16[80,256]{1,0:T(8,128)(2,1)S(1)}, f32[2,80,128]{2,1,0:T(8,128)S(1)}, f32[16,80,128]{2,1,0:T(8,128)S(1)}, f32[2,80,128]{2,1,0:T(8,128)S(1)}) custom-call(f32[1,80,8,128]{3,2,1,0:T(8,128)S(1)} %copy-done, f32[4,80,128]{2,1,0:T(8,128)S(1)} %collective-permute-done.1.rows1_ref, f32[1,80,80]{2,1,0:T(8,128)S(1)} %copy-done.1, f32[1,80]{1,0:T(1,128)S(1)} %copy-done.2), custom_call_target="tpu_custom_call" | custom-call | flops 100000 | bytes 100000 | tf_op jit(solution)/shard_map/pallas_call | solution.py:512
  10.5 1.4 %collective-permute-done.3.refs_4_ = f32[16,128]{1,0:T(8,128)S(1)} collective-permute-done((f32[16,128]{1,0:T(8,128)S(1)}, f32[16,128]{1,0:T(8,128)S(1)}, u32[]{:S(2)}, u32[]{:S(2)}) %collective-permute-start.3) | collective-permute-done | bytes 8224 | tf_op jit(solution)/shard_map/ppermute | solution.py:456
  12.0 0.0 collective-permute-done.4.refs_5_
  12.0 0.0 collective-permute-done.2.refs_3_
  12.0 0.4 %shard_map.78 = (f32[104,128]{1,0:T(8,128)S(1)}, f32[32,128]{1,0:T(8,128)S(1)}, f32[32,128]{1,0:T(8,128)S(1)}) custom-call(f32[24,128]{1,0:T(8,128)S(1)} %collective-permute-done.refs_0_, f32[16,128]{1,0:T(8,128)S(1)} %shard_map.75.refs_1_, f32[24,128]{1,0:T(8,128)S(1)} %shard_map.74.refs_2_, f32[40,128]{1,0:T(8,128)S(1)} %collective-permute-done.2.refs_3_, ...), custom_call_target="tpu_custom_call" | custom-call | flops 3000000000 | bytes 100000 | tf_op jit(solution)/shard_map/pallas_call | solution.py:525
  12.4 0.3 %collective-permute-start.5 = (f32[104,128]{1,0:T(8,128)S(1)}, f32[104,128]{1,0:T(8,128)S(1)}, u32[]{:S(2)}, u32[]{:S(2)}) collective-permute-start(f32[104,128]{1,0:T(8,128)S(1)} %get-tuple-element.37), channel_id=1, source_target_pairs={{0,16},{16,0},{1,17},{17,1},{2,18},{18,2},{3,19},{19,3},{4,20},{20... | collective-permute-start | bytes 159752 | tf_op jit(solution)/shard_map/ppermute | solution.py:446
  12.7 0.6 %collective-permute-start.6 = (f32[32,128]{1,0:T(8,128)S(1)}, f32[32,128]{1,0:T(8,128)S(1)}, u32[]{:S(2)}, u32[]{:S(2)}) collective-permute-start(f32[32,128]{1,0:T(8,128)S(1)} %get-tuple-element.38), channel_id=1, source_target_pairs={{0,20},{4,16},{8,28},{12,24},{16,4},{20,0},{24,12},{28,8},{1,21},{... | collective-permute-start | bytes 49160 | tf_op jit(solution)/shard_map/ppermute | solution.py:456
  13.3 2.1 %collective-permute-start.7 = (f32[32,128]{1,0:T(8,128)S(1)}, f32[32,128]{1,0:T(8,128)S(1)}, u32[]{:S(2)}, u32[]{:S(2)}) collective-permute-start(f32[32,128]{1,0:T(8,128)S(1)} %get-tuple-element.39), channel_id=1, source_target_pairs={{0,28},{4,24},{8,20},{12,16},{16,12},{20,8},{24,4},{28,0},{1,29},{... | collective-permute-start | bytes 49160 | tf_op jit(solution)/shard_map/ppermute | solution.py:456
  15.4 0.4 %collective-permute-done.8.rows2_ref = f32[4,80,128]{2,1,0:T(8,128)S(1)} collective-permute-done((f32[4,80,128]{2,1,0:T(8,128)S(1)}, f32[4,80,128]{2,1,0:T(8,128)S(1)}, u32[]{:S(2)}, u32[]{:S(2)}) %collective-permute-start.8) | collective-permute-done | bytes 163872 | tf_op jit(solution)/shard_map/ppermute | solution.py:446
  15.8 0.0 collective-permute-done.5.own_ref
  15.8 1.2 %shard_map.79 = (f32[16,80,128]{2,1,0:T(8,128)S(1)}, f32[2,80,128]{2,1,0:T(8,128)S(1)}, f32[8,80,128]{2,1,0:T(8,128)S(1)}, f32[6,80,128]{2,1,0:T(8,128)S(1)}, f3...) custom-call(f32[104,128]{1,0:T(8,128)S(1)} %collective-permute-done.5.own_ref, ...), custom_call_target="tpu_custom_call", output_to_operand_aliasing={{0}: (4, {})} | custom-call | flops 2000000000 | bytes 2000000 | tf_op jit(solution)/shard_map/pallas_call | solution.py:536
  17.0 0.0 collective-permute-done.6.msg1_ref
  17.0 0.4 %collective-permute-done.7.msg2_ref = f32[32,128]{1,0:T(8,128)S(1)} collective-permute-done((f32[32,128]{1,0:T(8,128)S(1)}, f32[32,128]{1,0:T(8,128)S(1)}, u32[]{:S(2)}, u32[]{:S(2)}) %collective-permute-start.7) | collective-permute-done | bytes 16416 | tf_op jit(solution)/shard_map/ppermute | solution.py:456
  17.4 2.5 %shard_map.80 = f32[1,80,8,128]{3,2,1,0:T(8,128)} custom-call(f32[104,128]{1,0:T(8,128)S(1)} %collective-permute-done.5.own_ref, f32[32,128]{1,0:T(8,128)S(1)} %collective-permute-done.6.msg1_ref, f32[32,128]{1,0:T(8,128)S(1)} %collective-permute-done.7.msg2_ref, bf16[80,256]{1,0:T(8,128)(2,1)S(1)} %get-tuple-element.40.mix_ref, ...), custom_call_target="tpu_custom_call" | custom-call | flops 300000000 | bytes 2000000 | tf_op jit(solution)/shard_map/pallas_call | solution.py:545
  (4 shorter events, 0.0 us)
Async XLA Ops:
  0.0 1.0 %copy-start = (f32[1,80,8,128]{3,2,1,0:T(8,128)S(1)}, f32[1,80,8,128]{3,2,1,0:T(8,128)}, u32[]{:S(2)}) copy-start(f32[1,80,8,128]{3,2,1,0:T(8,128)} %state_ref.3) | copy-start | bytes 983044
  0.0 1.0 %copy-start.3 = (s32[1,1,1,4,8]{4,3,2,1,0:T(4,128)S(1)}, s32[1,1,1,4,8]{4,3,2,1,0:T(4,128)}, u32[]{:S(2)}) copy-start(s32[1,1,1,4,8]{4,3,2,1,0:T(4,128)} %links_ref.1) | copy-start | bytes 388
  0.0 1.0 %copy-start.4 = (f32[1,64]{1,0:T(1,128)S(1)}, f32[1,64]{1,0:T(1,128)}, u32[]{:S(2)}) copy-start(f32[1,64]{1,0:T(1,128)} %weights_ref.1) | copy-start | bytes 772
  0.0 1.0 %copy-start.5 = (s32[8,1]{0,1:T(1,128)S(1)}, s32[8,1]{0,1:T(1,128)}, u32[]{:S(2)}) copy-start(s32[8,1]{0,1:T(1,128)} %param.12) | copy-start | bytes 100
  0.0 1.0 %copy-start.6 = (s32[8,1]{0,1:T(1,128)S(1)}, s32[8,1]{0,1:T(1,128)}, u32[]{:S(2)}) copy-start(s32[8,1]{0,1:T(1,128)} %param.13) | copy-start | bytes 100
  1.2 3.3 %collective-permute-start = (f32[24,128]{1,0:T(8,128)S(1)}, f32[24,128]{1,0:T(8,128)S(1)}, u32[]{:S(2)}, u32[]{:S(2)}) collective-permute-start(f32[24,128]{1,0:T(8,128)S(1)} %shard_map.74.refs_2_), channel_id=1, source_target_pairs={{0,16},{16,0},{1,17},{17,1},{2,18},{18,2},{3,19},{19,3},{4,20},{20... | collective-permute-start | bytes 36872 | tf_op jit(solution)/shard_map/ppermute | solution.py:446
  1.9 8.4 %collective-permute-start.1 = (f32[4,80,128]{2,1,0:T(8,128)S(1)}, f32[4,80,128]{2,1,0:T(8,128)S(1)}, u32[]{:S(2)}, u32[]{:S(2)}) collective-permute-start(f32[4,80,128]{2,1,0:T(8,128)S(1)} %get-tuple-element.32), channel_id=1, source_target_pairs={{0,4},{4,0},{8,12},{12,8},{1,5},{5,1},{9,13},{13,9},{2,6},{6,2},{1... | collective-permute-start | bytes 491528 | tf_op jit(solution)/shard_map/ppermute | solution.py:446
  4.5 5.8 %copy-start.1 = (f32[1,80,80]{2,1,0:T(8,128)S(1)}, f32[1,80,80]{2,1,0:T(8,128)}, u32[]{:S(2)}) copy-start(f32[1,80,80]{2,1,0:T(8,128)} %mixing_ref.1) | copy-start | bytes 76804
  4.5 7.5 %collective-permute-start.4 = (f32[40,128]{1,0:T(8,128)S(1)}, f32[40,128]{1,0:T(8,128)S(1)}, u32[]{:S(2)}, u32[]{:S(2)}) collective-permute-start(f32[40,128]{1,0:T(8,128)S(1)} %get-tuple-element.51), channel_id=1, source_target_pairs={{0,19},{1,18},{2,17},{3,16},{16,3},{17,2},{18,1},{19,0},{4,23},{5,... | collective-permute-start | bytes 61448 | tf_op jit(solution)/shard_map/ppermute | solution.py:456
  8.0 2.3 %copy-start.2 = (f32[1,80]{1,0:T(1,128)S(1)}, f32[1,80]{1,0:T(1,128)}, u32[]{:S(2)}) copy-start(f32[1,80]{1,0:T(1,128)} %diffuse_ref.1) | copy-start | bytes 964
  8.0 4.0 %collective-permute-start.2 = (f32[40,128]{1,0:T(8,128)S(1)}, f32[40,128]{1,0:T(8,128)S(1)}, u32[]{:S(2)}, u32[]{:S(2)}) collective-permute-start(f32[40,128]{1,0:T(8,128)S(1)} %get-tuple-element.52), channel_id=1, source_target_pairs={{0,17},{1,16},{2,19},{3,18},{16,1},{17,0},{18,3},{19,2},{4,21},{5,... | collective-permute-start | bytes 61448 | tf_op jit(solution)/shard_map/ppermute | solution.py:456
  8.0 4.0 %collective-permute-start.3 = (f32[16,128]{1,0:T(8,128)S(1)}, f32[16,128]{1,0:T(8,128)S(1)}, u32[]{:S(2)}, u32[]{:S(2)}) collective-permute-start(f32[16,128]{1,0:T(8,128)S(1)} %slice.6), channel_id=1, source_target_pairs={{0,18},{1,19},{2,16},{3,17},{16,2},{17,3},{18,0},{19,1},{4,22},{5,... | collective-permute-start | bytes 24584 | tf_op jit(solution)/shard_map/ppermute | solution.py:456
  8.5 7.3 %collective-permute-start.8 = (f32[4,80,128]{2,1,0:T(8,128)S(1)}, f32[4,80,128]{2,1,0:T(8,128)S(1)}, u32[]{:S(2)}, u32[]{:S(2)}) collective-permute-start(f32[4,80,128]{2,1,0:T(8,128)S(1)} %get-tuple-element.42), channel_id=1, source_target_pairs={{0,12},{4,8},{8,4},{12,0},{1,13},{5,9},{9,5},{13,1},{2,14},{6,10},... | collective-permute-start | bytes 491528 | tf_op jit(solution)/shard_map/ppermute | solution.py:446
  12.4 3.4 %collective-permute-start.5 = (f32[104,128]{1,0:T(8,128)S(1)}, f32[104,128]{1,0:T(8,128)S(1)}, u32[]{:S(2)}, u32[]{:S(2)}) collective-permute-start(f32[104,128]{1,0:T(8,128)S(1)} %get-tuple-element.37), channel_id=1, source_target_pairs={{0,16},{16,0},{1,17},{17,1},{2,18},{18,2},{3,19},{19,3},{4,20},{20... | collective-permute-start | bytes 159752 | tf_op jit(solution)/shard_map/ppermute | solution.py:446
  12.7 4.3 %collective-permute-start.6 = (f32[32,128]{1,0:T(8,128)S(1)}, f32[32,128]{1,0:T(8,128)S(1)}, u32[]{:S(2)}, u32[]{:S(2)}) collective-permute-start(f32[32,128]{1,0:T(8,128)S(1)} %get-tuple-element.38), channel_id=1, source_target_pairs={{0,20},{4,16},{8,28},{12,24},{16,4},{20,0},{24,12},{28,8},{1,21},{... | collective-permute-start | bytes 49160 | tf_op jit(solution)/shard_map/ppermute | solution.py:456
  13.3 4.1 %collective-permute-start.7 = (f32[32,128]{1,0:T(8,128)S(1)}, f32[32,128]{1,0:T(8,128)S(1)}, u32[]{:S(2)}, u32[]{:S(2)}) collective-permute-start(f32[32,128]{1,0:T(8,128)S(1)} %get-tuple-element.39), channel_id=1, source_target_pairs={{0,28},{4,24},{8,20},{12,16},{16,12},{20,8},{24,4},{28,0},{1,29},{... | collective-permute-start | bytes 49160 | tf_op jit(solution)/shard_map/ppermute | solution.py:456

commit v9 on v7

--- a/solution.py
+++ b/solution.py
@@ -231,7 +231,7 @@
     def __init__(self, mix_ref, rate_ref):
         self.mixer, self.rate_ref = mix_ref[...], rate_ref
         self.levels = rate_ref.shape[1]
-        self.pad = jnp.zeros((self.mixer.shape[1] - 3 * self.levels, 256), jnp.bfloat16)
+        self.pad = jnp.zeros((self.mixer.shape[1] - 3 * self.levels, 128), jnp.bfloat16)
         tail = lax.broadcasted_iota(jnp.int32, (8, 128), 0)
         self.first = tail == 0
         self.tail = (tail + (self.levels - 8)).astype(jnp.float32)
@@ -243,11 +243,12 @@
         return jnp.concatenate([head, value[8:-8], tail], axis=0)
 
     def mixed(self, values):
-        value = jnp.concatenate(values, axis=1)
-        hi, lo = halves(value)
-        full = jnp.concatenate([hi, lo, hi, self.pad[:, : value.shape[1]]], axis=0)
-        out = jnp.dot(self.mixer, full, preferred_element_type=jnp.float32)
-        return [out[:, 128 * k : 128 * (k + 1)] for k in range(len(values))]
+        out = []
+        for value in values:
+            hi, lo = halves(value)
+            full = jnp.concatenate([hi, lo, hi, self.pad], axis=0)
+            out.append(jnp.dot(self.mixer, full, preferred_element_type=jnp.float32))
+        return out
 
     def settled(self, new, x, deep):
         sea = jnp.broadcast_to(deep, (self.levels - 8, 128)) > 0.0
@@ -304,7 +305,7 @@
     side_ref[1] = right
 
 
-def outer_kernel(own_ref, msg2_ref, msg1_ref, mix_ref, rate_ref, x_ref, side_ref, *refs):
+def outer_kernel(own_ref, msg1_ref, msg2_ref, mix_ref, rate_ref, x_ref, side_ref, *refs):
     inner_refs, out_ref, outer_refs = refs[:STEPS], refs[STEPS], refs[STEPS + 1 :]
     levels, rows, cells = out_ref.shape[1:]
     slots = rows + 2 * STEPS
@@ -394,11 +395,11 @@
             sides = jnp.where(place < 4, right, roll(left, -EDGE))
         low_rows = list(range(step + 1, step + 4))
         todo = low_rows + [slots - 1 - s for s in reversed(low_rows)]
-        for k in range(0, len(todo), 2):
-            pair = todo[k : k + 2]
-            tiles = [[tile_at(step, s + j) for j in (-1, 0, 1)] for s in pair]
-            new = update.rows(tiles, [flux_rows[s] for s in pair], [deep_rows[s] for s in pair])
-            for j, (s, tile) in enumerate(zip(pair, new)):
+        for k in range(0, len(todo), 3):
+            group = todo[k : k + 3]
+            tiles = [[tile_at(step, s + j) for j in (-1, 0, 1)] for s in group]
+            new = update.rows(tiles, [flux_rows[s] for s in group], [deep_rows[s] for s in group])
+            for j, (s, tile) in enumerate(zip(group, new)):
                 if last:
                     put(s, tile)
                 else:
@@ -504,8 +505,8 @@
         vmem=FRONT_VMEM_LIMIT,
     )(crossed, spare, *packs)
     own = exchange(own, "comp", near)
+    message_1 = exchange_over(for_first, "lat", near)
     message_2 = exchange_over(for_second, "lat", far_lat)
-    message_1 = exchange_over(for_first, "lat", near)
     laid_out = kernel_call(
         inner_kernel,
         (
@@ -526,7 +527,7 @@
         scratch=[pltpu.VMEM((6, levels, 128), jnp.float32)] * (STEPS - 1),
         flops=300_000_000,
         nbytes=2_000_000,
-    )(own, message_2, message_1, *laid_out)
+    )(own, message_1, message_2, *laid_out)
 
 
 def solution(mesh):

time: 20 us -> 20 us (level)
  transfers between devices with their start and end apart: 9 -> 9, of which waited for: 3 -> 3; matrix products, arithmetic and copies ran while one was open for 0% -> 0% of each run, Pallas kernels for 11% -> 10%
where the time goes in v9:
time: 20 us; the launch traced here: 19.9 us
  starting transfers between devices  11.8 us (59%)
  Pallas kernels  4.66 us (23%)
  waiting for transfers between devices  2.37 us (12%)
  local copies, waits for them, and re-layouts  0.97 us (5%)
    ppermute x5, starting transfers between devices, exchange_over(): return lax.ppermute(value, ('comp', axis), pairs)  6.73 us
    ppermute x4, starting transfers between devices, exchange(): return lax.ppermute(value, axis, pairs)  5.07 us
    pallas_call x1, Pallas kernels, on_device(): kernel_call(outer_kernel, f32(*state.shape), [vmem_spec()] * (3 + len(lai...  2.48 us
    ppermute x5, waiting for transfers between devices, exchange_over(): return lax.ppermute(value, ('comp', axis), pairs)  1.98 us
    pallas_call x1, Pallas kernels, on_device(): kernel_call(inner_kernel, (jax.ShapeDtypeStruct((levels, 256), jnp.bfloat...  1.33 us
    unnamed x14, local copies, waits for them, and re-layouts  0.97 us
    pallas_call x1, Pallas kernels, on_device(): kernel_call(functools.partial(flux_kernel, count, slices, east_west), (f3...  0.4 us
  transfers between devices with their start and end apart: 9, of which 3 were waited for; matrix products, arithmetic and copies ran while one was open for 0% of the time, Pallas kernels for 10%

profile of v9, /device:TPU:0, one launch (start us, length us, event | category | flops | bytes accessed | tf_op | source)
XLA Modules:
  0.0 19.9 jit_solution(13244212678175293911)
XLA Ops:
  0.0 0.0 copy-start
  0.0 0.0 copy-start.2
  0.0 0.0 copy-start.3
  0.0 0.0 copy-start.4
  0.0 0.0 copy-start.5
  0.0 0.9 %copy-done = f32[1,80,8,128]{3,2,1,0:T(8,128)S(1)} copy-done((f32[1,80,8,128]{3,2,1,0:T(8,128)S(1)}, f32[1,80,8,128]{3,2,1,0:T(8,128)}, u32[]{:S(2)}) %copy-start) | copy-done | bytes 327704
  1.0 0.0 copy-done.2
  1.0 0.0 copy-done.3
  1.0 0.0 copy-done.4
  1.0 0.0 copy-done.5
  1.0 0.2 shard_map.74.refs_2_
  1.2 0.5 %collective-permute-start = (f32[24,128]{1,0:T(8,128)S(1)}, f32[24,128]{1,0:T(8,128)S(1)}, u32[]{:S(2)}, u32[]{:S(2)}) collective-permute-start(f32[24,128]{1,0:T(8,128)S(1)} %shard_map.74.refs_2_), channel_id=1, source_target_pairs={{0,16},{16,0},{1,17},{17,1},{2,18},{18,2},{3,19},{19,3},{4,20},{20... | collective-permute-start | bytes 36872 | tf_op jit(solution)/shard_map/ppermute | solution.py:432
  1.6 0.3 %shard_map.76 = (f32[24,128]{1,0:T(8,128)S(1)}, f32[24,128]{1,0:T(8,128)S(1)}, f32[4,80,128]{2,1,0:T(8,128)S(1)}, f32[4,80,128]{2,1,0:T(8,128)S(1)}) custom-call(f32[1,80,8,128]{3,2,1,0:T(8,128)S(1)} %copy-done), custom_call_target="tpu_custom_call" | custom-call | flops 2000000000 | bytes 900000 | tf_op jit(solution)/shard_map/pallas_call | solution.py:473
  1.9 2.6 %collective-permute-start.1 = (f32[4,80,128]{2,1,0:T(8,128)S(1)}, f32[4,80,128]{2,1,0:T(8,128)S(1)}, u32[]{:S(2)}, u32[]{:S(2)}) collective-permute-start(f32[4,80,128]{2,1,0:T(8,128)S(1)} %get-tuple-element.30), channel_id=1, source_target_pairs={{0,4},{4,0},{8,12},{12,8},{1,5},{5,1},{9,13},{13,9},{2,6},{6,2},{1... | collective-permute-start | bytes 491528 | tf_op jit(solution)/shard_map/ppermute | solution.py:432
  4.5 0.0 collective-permute-done.refs_0_
  4.5 3.5 %collective-permute-start.4 = (f32[40,128]{1,0:T(8,128)S(1)}, f32[40,128]{1,0:T(8,128)S(1)}, u32[]{:S(2)}, u32[]{:S(2)}) collective-permute-start(f32[40,128]{1,0:T(8,128)S(1)} %get-tuple-element.47), channel_id=1, source_target_pairs={{0,19},{1,18},{2,17},{3,16},{16,3},{17,2},{18,1},{19,0},{4,23},{5,... | collective-permute-start | bytes 61448 | tf_op jit(solution)/shard_map/ppermute | solution.py:442
  8.0 0.0 collective-permute-start.2
  8.0 0.5 %collective-permute-start.3 = (f32[16,128]{1,0:T(8,128)S(1)}, f32[16,128]{1,0:T(8,128)S(1)}, u32[]{:S(2)}, u32[]{:S(2)}) collective-permute-start(f32[16,128]{1,0:T(8,128)S(1)} %slice.6), channel_id=1, source_target_pairs={{0,18},{1,19},{2,16},{3,17},{16,2},{17,3},{18,0},{19,1},{4,22},{5,... | collective-permute-start | bytes 24584 | tf_op jit(solution)/shard_map/ppermute | solution.py:442
  8.5 0.0 copy-start.1
  8.5 1.7 %collective-permute-start.8 = (f32[4,80,128]{2,1,0:T(8,128)S(1)}, f32[4,80,128]{2,1,0:T(8,128)S(1)}, u32[]{:S(2)}, u32[]{:S(2)}) collective-permute-start(f32[4,80,128]{2,1,0:T(8,128)S(1)} %get-tuple-element.38), channel_id=1, source_target_pairs={{0,12},{4,8},{8,4},{12,0},{1,13},{5,9},{9,5},{13,1},{2,14},{6,10},... | collective-permute-start | bytes 491528 | tf_op jit(solution)/shard_map/ppermute | solution.py:432
  10.2 0.0 collective-permute-done.1.rows1_ref
  10.2 1.7 %collective-permute-done.3.refs_4_ = f32[16,128]{1,0:T(8,128)S(1)} collective-permute-done((f32[16,128]{1,0:T(8,128)S(1)}, f32[16,128]{1,0:T(8,128)S(1)}, u32[]{:S(2)}, u32[]{:S(2)}) %collective-permute-start.3) | collective-permute-done | bytes 8224 | tf_op jit(solution)/shard_map/ppermute | solution.py:442
  11.9 0.0 collective-permute-done.4.refs_5_
  12.0 0.0 collective-permute-done.2.refs_3_
  12.0 0.4 %shard_map.77 = (f32[104,128]{1,0:T(8,128)S(1)}, f32[32,128]{1,0:T(8,128)S(1)}, f32[32,128]{1,0:T(8,128)S(1)}) custom-call(f32[24,128]{1,0:T(8,128)S(1)} %collective-permute-done.refs_0_, f32[16,128]{1,0:T(8,128)S(1)} %shard_map.75.refs_1_, f32[24,128]{1,0:T(8,128)S(1)} %shard_map.74.refs_2_, f32[40,128]{1,0:T(8,128)S(1)} %collective-permute-done.2.refs_3_, ...), custom_call_target="tpu_custom_call" | custom-call | flops 3000000000 | bytes 100000 | tf_op jit(solution)/shard_map/pallas_call | solution.py:499
  12.4 0.3 %collective-permute-start.5 = (f32[104,128]{1,0:T(8,128)S(1)}, f32[104,128]{1,0:T(8,128)S(1)}, u32[]{:S(2)}, u32[]{:S(2)}) collective-permute-start(f32[104,128]{1,0:T(8,128)S(1)} %get-tuple-element.34), channel_id=1, source_target_pairs={{0,16},{16,0},{1,17},{17,1},{2,18},{18,2},{3,19},{19,3},{4,20},{20... | collective-permute-start | bytes 159752 | tf_op jit(solution)/shard_map/ppermute | solution.py:432
  12.7 0.0 copy-start.6
  12.7 0.5 %collective-permute-start.6 = (f32[32,128]{1,0:T(8,128)S(1)}, f32[32,128]{1,0:T(8,128)S(1)}, u32[]{:S(2)}, u32[]{:S(2)}) collective-permute-start(f32[32,128]{1,0:T(8,128)S(1)} %get-tuple-element.35), channel_id=1, source_target_pairs={{0,20},{4,16},{8,28},{12,24},{16,4},{20,0},{24,12},{28,8},{1,21},{... | collective-permute-start | bytes 49160 | tf_op jit(solution)/shard_map/ppermute | solution.py:442
  13.2 2.2 %collective-permute-start.7 = (f32[32,128]{1,0:T(8,128)S(1)}, f32[32,128]{1,0:T(8,128)S(1)}, u32[]{:S(2)}, u32[]{:S(2)}) collective-permute-start(f32[32,128]{1,0:T(8,128)S(1)} %get-tuple-element.36), channel_id=1, source_target_pairs={{0,28},{4,24},{8,20},{12,16},{16,12},{20,8},{24,4},{28,0},{1,29},{... | collective-permute-start | bytes 49160 | tf_op jit(solution)/shard_map/ppermute | solution.py:442
  15.4 0.4 %collective-permute-done.8.rows2_ref = f32[4,80,128]{2,1,0:T(8,128)S(1)} collective-permute-done((f32[4,80,128]{2,1,0:T(8,128)S(1)}, f32[4,80,128]{2,1,0:T(8,128)S(1)}, u32[]{:S(2)}, u32[]{:S(2)}) %collective-permute-start.8) | collective-permute-done | bytes 163872 | tf_op jit(solution)/shard_map/ppermute | solution.py:432
  15.8 0.0 collective-permute-done.5.own_ref
  15.8 0.0 copy-done.1
  15.8 0.0 copy-done.6
  15.8 1.3 %shard_map.78 = (bf16[80,256]{1,0:T(8,128)(2,1)S(1)}, f32[2,80,128]{2,1,0:T(8,128)S(1)}, f32[16,80,128]{2,1,0:T(8,128)S(1)}, f32[2,80,128]{2,1,0:T(8,128)S(1)}, ...) custom-call(f32[1,80,8,128]{3,2,1,0:T(8,128)S(1)} %copy-done, ...), custom_call_target="tpu_custom_call" | custom-call | flops 2000000000 | bytes 2000000 | tf_op jit(solution)/shard_map/pallas_call | solution.py:510
  17.1 0.0 collective-permute-done.6.msg1_ref
  17.1 0.2 %collective-permute-done.7.msg2_ref = f32[32,128]{1,0:T(8,128)S(1)} collective-permute-done((f32[32,128]{1,0:T(8,128)S(1)}, f32[32,128]{1,0:T(8,128)S(1)}, u32[]{:S(2)}, u32[]{:S(2)}) %collective-permute-start.7) | collective-permute-done | bytes 16416 | tf_op jit(solution)/shard_map/ppermute | solution.py:442
  17.4 2.5 %shard_map.79 = f32[1,80,8,128]{3,2,1,0:T(8,128)} custom-call(f32[104,128]{1,0:T(8,128)S(1)} %collective-permute-done.5.own_ref, f32[32,128]{1,0:T(8,128)S(1)} %collective-permute-done.6.msg1_ref, f32[32,128]{1,0:T(8,128)S(1)} %collective-permute-done.7.msg2_ref, bf16[80,256]{1,0:T(8,128)(2,1)S(1)} %get-tuple-element.39.mix_ref, ...), custom_call_target="tpu_custom_call" | custom-call | flops 300000000 | bytes 2000000 | tf_op jit(solution)/shard_map/pallas_call | solution.py:523
  (4 shorter events, 0.0 us)
Async XLA Ops:
  0.0 1.0 %copy-start = (f32[1,80,8,128]{3,2,1,0:T(8,128)S(1)}, f32[1,80,8,128]{3,2,1,0:T(8,128)}, u32[]{:S(2)}) copy-start(f32[1,80,8,128]{3,2,1,0:T(8,128)} %state_ref.3) | copy-start | bytes 983044
  0.0 1.0 %copy-start.2 = (s32[1,1,1,4,8]{4,3,2,1,0:T(4,128)S(1)}, s32[1,1,1,4,8]{4,3,2,1,0:T(4,128)}, u32[]{:S(2)}) copy-start(s32[1,1,1,4,8]{4,3,2,1,0:T(4,128)} %links_ref.1) | copy-start | bytes 388
  0.0 1.0 %copy-start.3 = (f32[1,64]{1,0:T(1,128)S(1)}, f32[1,64]{1,0:T(1,128)}, u32[]{:S(2)}) copy-start(f32[1,64]{1,0:T(1,128)} %weights_ref.1) | copy-start | bytes 772
  0.0 1.0 %copy-start.4 = (s32[8,1]{0,1:T(1,128)S(1)}, s32[8,1]{0,1:T(1,128)}, u32[]{:S(2)}) copy-start(s32[8,1]{0,1:T(1,128)} %param.12) | copy-start | bytes 100
  0.0 1.0 %copy-start.5 = (s32[8,1]{0,1:T(1,128)S(1)}, s32[8,1]{0,1:T(1,128)}, u32[]{:S(2)}) copy-start(s32[8,1]{0,1:T(1,128)} %param.13) | copy-start | bytes 100
  1.2 3.3 %collective-permute-start = (f32[24,128]{1,0:T(8,128)S(1)}, f32[24,128]{1,0:T(8,128)S(1)}, u32[]{:S(2)}, u32[]{:S(2)}) collective-permute-start(f32[24,128]{1,0:T(8,128)S(1)} %shard_map.74.refs_2_), channel_id=1, source_target_pairs={{0,16},{16,0},{1,17},{17,1},{2,18},{18,2},{3,19},{19,3},{4,20},{20... | collective-permute-start | bytes 36872 | tf_op jit(solution)/shard_map/ppermute | solution.py:432
  1.9 8.3 %collective-permute-start.1 = (f32[4,80,128]{2,1,0:T(8,128)S(1)}, f32[4,80,128]{2,1,0:T(8,128)S(1)}, u32[]{:S(2)}, u32[]{:S(2)}) collective-permute-start(f32[4,80,128]{2,1,0:T(8,128)S(1)} %get-tuple-element.30), channel_id=1, source_target_pairs={{0,4},{4,0},{8,12},{12,8},{1,5},{5,1},{9,13},{13,9},{2,6},{6,2},{1... | collective-permute-start | bytes 491528 | tf_op jit(solution)/shard_map/ppermute | solution.py:432
  4.5 7.5 %collective-permute-start.4 = (f32[40,128]{1,0:T(8,128)S(1)}, f32[40,128]{1,0:T(8,128)S(1)}, u32[]{:S(2)}, u32[]{:S(2)}) collective-permute-start(f32[40,128]{1,0:T(8,128)S(1)} %get-tuple-element.47), channel_id=1, source_target_pairs={{0,19},{1,18},{2,17},{3,16},{16,3},{17,2},{18,1},{19,0},{4,23},{5,... | collective-permute-start | bytes 61448 | tf_op jit(solution)/shard_map/ppermute | solution.py:442
  8.0 4.0 %collective-permute-start.2 = (f32[40,128]{1,0:T(8,128)S(1)}, f32[40,128]{1,0:T(8,128)S(1)}, u32[]{:S(2)}, u32[]{:S(2)}) collective-permute-start(f32[40,128]{1,0:T(8,128)S(1)} %get-tuple-element.48), channel_id=1, source_target_pairs={{0,17},{1,16},{2,19},{3,18},{16,1},{17,0},{18,3},{19,2},{4,21},{5,... | collective-permute-start | bytes 61448 | tf_op jit(solution)/shard_map/ppermute | solution.py:442
  8.0 4.0 %collective-permute-start.3 = (f32[16,128]{1,0:T(8,128)S(1)}, f32[16,128]{1,0:T(8,128)S(1)}, u32[]{:S(2)}, u32[]{:S(2)}) collective-permute-start(f32[16,128]{1,0:T(8,128)S(1)} %slice.6), channel_id=1, source_target_pairs={{0,18},{1,19},{2,16},{3,17},{16,2},{17,3},{18,0},{19,1},{4,22},{5,... | collective-permute-start | bytes 24584 | tf_op jit(solution)/shard_map/ppermute | solution.py:442
  8.5 7.3 %copy-start.1 = (f32[1,80,80]{2,1,0:T(8,128)S(1)}, f32[1,80,80]{2,1,0:T(8,128)}, u32[]{:S(2)}) copy-start(f32[1,80,80]{2,1,0:T(8,128)} %mixing_ref.1) | copy-start | bytes 76804
  8.5 7.3 %collective-permute-start.8 = (f32[4,80,128]{2,1,0:T(8,128)S(1)}, f32[4,80,128]{2,1,0:T(8,128)S(1)}, u32[]{:S(2)}, u32[]{:S(2)}) collective-permute-start(f32[4,80,128]{2,1,0:T(8,128)S(1)} %get-tuple-element.38), channel_id=1, source_target_pairs={{0,12},{4,8},{8,4},{12,0},{1,13},{5,9},{9,5},{13,1},{2,14},{6,10},... | collective-permute-start | bytes 491528 | tf_op jit(solution)/shard_map/ppermute | solution.py:432
  12.4 3.4 %collective-permute-start.5 = (f32[104,128]{1,0:T(8,128)S(1)}, f32[104,128]{1,0:T(8,128)S(1)}, u32[]{:S(2)}, u32[]{:S(2)}) collective-permute-start(f32[104,128]{1,0:T(8,128)S(1)} %get-tuple-element.34), channel_id=1, source_target_pairs={{0,16},{16,0},{1,17},{17,1},{2,18},{18,2},{3,19},{19,3},{4,20},{20... | collective-permute-start | bytes 159752 | tf_op jit(solution)/shard_map/ppermute | solution.py:432
  12.7 3.1 %copy-start.6 = (f32[1,80]{1,0:T(1,128)S(1)}, f32[1,80]{1,0:T(1,128)}, u32[]{:S(2)}) copy-start(f32[1,80]{1,0:T(1,128)} %diffuse_ref.1) | copy-start | bytes 964
  12.7 4.4 %collective-permute-start.6 = (f32[32,128]{1,0:T(8,128)S(1)}, f32[32,128]{1,0:T(8,128)S(1)}, u32[]{:S(2)}, u32[]{:S(2)}) collective-permute-start(f32[32,128]{1,0:T(8,128)S(1)} %get-tuple-element.35), channel_id=1, source_target_pairs={{0,20},{4,16},{8,28},{12,24},{16,4},{20,0},{24,12},{28,8},{1,21},{... | collective-permute-start | bytes 49160 | tf_op jit(solution)/shard_map/ppermute | solution.py:442
  13.2 4.2 %collective-permute-start.7 = (f32[32,128]{1,0:T(8,128)S(1)}, f32[32,128]{1,0:T(8,128)S(1)}, u32[]{:S(2)}, u32[]{:S(2)}) collective-permute-start(f32[32,128]{1,0:T(8,128)S(1)} %get-tuple-element.36), channel_id=1, source_target_pairs={{0,28},{4,24},{8,20},{12,16},{16,12},{20,8},{24,4},{28,0},{1,29},{... | collective-permute-start | bytes 49160 | tf_op jit(solution)/shard_map/ppermute | solution.py:442

commit v10 on v9

--- a/solution.py
+++ b/solution.py
@@ -184,13 +184,12 @@
     whole = jnp.concatenate(pieces, axis=0)
     land_beside = beside(FOLD + count + 2)
     deep_beside = jnp.where(ocean, beside(FOLD + count + 3), all_levels)
-    imported_beside = jnp.zeros((1, 128), jnp.float32)
-    for row in range(rows):
-        start = row * EDGE
-        east = roll(imported[rows + row : rows + row + 1], start)
-        west = roll(imported[2 * rows + row : 2 * rows + row + 1], start + 8)
-        mine = (lane >= start) & (lane < start + EDGE)
-        imported_beside = jnp.where(mine, jnp.where(from_east, east, west), imported_beside)
+    block_lane = lane_ids((rows, 128))
+    mine = block_lane // EDGE == lax.broadcasted_iota(jnp.int32, (rows, 128), 0)
+    east = pltpu.roll(imported[rows : 2 * rows], 0, 1, stride=EDGE, stride_axis=0)
+    west = pltpu.roll(imported[2 * rows :], EDGE, 1, stride=EDGE, stride_axis=0)
+    spread_out = jnp.where(block_lane % EDGE < 4, east, west)
+    imported_beside = jnp.sum(jnp.where(mine, spread_out, 0.0), axis=0, keepdims=True)
     flux_beside = coupling_rate * land_beside * (imported_beside - whole[0:1])
     flux = coupling_rate * land * (imported[0:rows] - surface)
     deep = jnp.broadcast_to(deep, (rows, 128))

time: 20 us -> 20 us (level)
  no operation moved by 1% of the time
where the time goes in v10:
time: 20 us; the launch traced here: 19.9 us
  starting transfers between devices  11.8 us (59%)
  Pallas kernels  4.64 us (23%)
  waiting for transfers between devices  2.37 us (12%)
  local copies, waits for them, and re-layouts  0.97 us (5%)
    ppermute x5, starting transfers between devices, exchange_over(): return lax.ppermute(value, ('comp', axis), pairs)  6.73 us
    ppermute x4, starting transfers between devices, exchange(): return lax.ppermute(value, axis, pairs)  5.07 us
    pallas_call x1, Pallas kernels, on_device(): kernel_call(outer_kernel, f32(*state.shape), [vmem_spec()] * (3 + len(lai...  2.49 us
    ppermute x5, waiting for transfers between devices, exchange_over(): return lax.ppermute(value, ('comp', axis), pairs)  1.97 us
    pallas_call x1, Pallas kernels, on_device(): kernel_call(inner_kernel, (jax.ShapeDtypeStruct((levels, 256), jnp.bfloat...  1.33 us
    unnamed x14, local copies, waits for them, and re-layouts  0.97 us
    ppermute x4, waiting for transfers between devices, exchange(): return lax.ppermute(value, axis, pairs)  0.4 us
  transfers between devices with their start and end apart: 9, of which 3 were waited for; matrix products, arithmetic and copies ran while one was open for 0% of the time, Pallas kernels for 10%

profile of v10, /device:TPU:0, one launch (start us, length us, event | category | flops | bytes accessed | tf_op | source)
XLA Modules:
  0.0 19.9 jit_solution(4635982053014776320)
XLA Ops:
  0.0 0.0 copy-start
  0.0 0.0 copy-start.2
  0.0 0.0 copy-start.3
  0.0 0.0 copy-start.4
  0.0 0.0 copy-start.5
  0.0 0.9 %copy-done = f32[1,80,8,128]{3,2,1,0:T(8,128)S(1)} copy-done((f32[1,80,8,128]{3,2,1,0:T(8,128)S(1)}, f32[1,80,8,128]{3,2,1,0:T(8,128)}, u32[]{:S(2)}) %copy-start) | copy-done | bytes 327704
  1.0 0.0 copy-done.2
  1.0 0.0 copy-done.3
  1.0 0.0 copy-done.4
  1.0 0.0 copy-done.5
  1.0 0.2 shard_map.74.refs_2_
  1.2 0.5 %collective-permute-start = (f32[24,128]{1,0:T(8,128)S(1)}, f32[24,128]{1,0:T(8,128)S(1)}, u32[]{:S(2)}, u32[]{:S(2)}) collective-permute-start(f32[24,128]{1,0:T(8,128)S(1)} %shard_map.74.refs_2_), channel_id=1, source_target_pairs={{0,16},{16,0},{1,17},{17,1},{2,18},{18,2},{3,19},{19,3},{4,20},{20... | collective-permute-start | bytes 36872 | tf_op jit(solution)/shard_map/ppermute | solution.py:431
  1.6 0.3 %shard_map.76 = (f32[24,128]{1,0:T(8,128)S(1)}, f32[24,128]{1,0:T(8,128)S(1)}, f32[4,80,128]{2,1,0:T(8,128)S(1)}, f32[4,80,128]{2,1,0:T(8,128)S(1)}) custom-call(f32[1,80,8,128]{3,2,1,0:T(8,128)S(1)} %copy-done), custom_call_target="tpu_custom_call" | custom-call | flops 2000000000 | bytes 900000 | tf_op jit(solution)/shard_map/pallas_call | solution.py:472
  1.9 2.6 %collective-permute-start.1 = (f32[4,80,128]{2,1,0:T(8,128)S(1)}, f32[4,80,128]{2,1,0:T(8,128)S(1)}, u32[]{:S(2)}, u32[]{:S(2)}) collective-permute-start(f32[4,80,128]{2,1,0:T(8,128)S(1)} %get-tuple-element.30), channel_id=1, source_target_pairs={{0,4},{4,0},{8,12},{12,8},{1,5},{5,1},{9,13},{13,9},{2,6},{6,2},{1... | collective-permute-start | bytes 491528 | tf_op jit(solution)/shard_map/ppermute | solution.py:431
  4.5 0.0 collective-permute-done.refs_0_
  4.5 3.5 %collective-permute-start.4 = (f32[40,128]{1,0:T(8,128)S(1)}, f32[40,128]{1,0:T(8,128)S(1)}, u32[]{:S(2)}, u32[]{:S(2)}) collective-permute-start(f32[40,128]{1,0:T(8,128)S(1)} %get-tuple-element.47), channel_id=1, source_target_pairs={{0,19},{1,18},{2,17},{3,16},{16,3},{17,2},{18,1},{19,0},{4,23},{5,... | collective-permute-start | bytes 61448 | tf_op jit(solution)/shard_map/ppermute | solution.py:441
  8.0 0.0 collective-permute-start.2
  8.0 0.5 %collective-permute-start.3 = (f32[16,128]{1,0:T(8,128)S(1)}, f32[16,128]{1,0:T(8,128)S(1)}, u32[]{:S(2)}, u32[]{:S(2)}) collective-permute-start(f32[16,128]{1,0:T(8,128)S(1)} %slice.6), channel_id=1, source_target_pairs={{0,18},{1,19},{2,16},{3,17},{16,2},{17,3},{18,0},{19,1},{4,22},{5,... | collective-permute-start | bytes 24584 | tf_op jit(solution)/shard_map/ppermute | solution.py:441
  8.5 0.0 copy-start.1
  8.5 1.7 %collective-permute-start.8 = (f32[4,80,128]{2,1,0:T(8,128)S(1)}, f32[4,80,128]{2,1,0:T(8,128)S(1)}, u32[]{:S(2)}, u32[]{:S(2)}) collective-permute-start(f32[4,80,128]{2,1,0:T(8,128)S(1)} %get-tuple-element.38), channel_id=1, source_target_pairs={{0,12},{4,8},{8,4},{12,0},{1,13},{5,9},{9,5},{13,1},{2,14},{6,10},... | collective-permute-start | bytes 491528 | tf_op jit(solution)/shard_map/ppermute | solution.py:431
  10.2 0.0 collective-permute-done.1.rows1_ref
  10.2 1.7 %collective-permute-done.3.refs_4_ = f32[16,128]{1,0:T(8,128)S(1)} collective-permute-done((f32[16,128]{1,0:T(8,128)S(1)}, f32[16,128]{1,0:T(8,128)S(1)}, u32[]{:S(2)}, u32[]{:S(2)}) %collective-permute-start.3) | collective-permute-done | bytes 8224 | tf_op jit(solution)/shard_map/ppermute | solution.py:441
  11.9 0.0 collective-permute-done.4.refs_5_
  12.0 0.0 collective-permute-done.2.refs_3_
  12.0 0.4 %shard_map.77 = (f32[104,128]{1,0:T(8,128)S(1)}, f32[32,128]{1,0:T(8,128)S(1)}, f32[32,128]{1,0:T(8,128)S(1)}) custom-call(f32[24,128]{1,0:T(8,128)S(1)} %collective-permute-done.refs_0_, f32[16,128]{1,0:T(8,128)S(1)} %shard_map.75.refs_1_, f32[24,128]{1,0:T(8,128)S(1)} %shard_map.74.refs_2_, f32[40,128]{1,0:T(8,128)S(1)} %collective-permute-done.2.refs_3_, ...), custom_call_target="tpu_custom_call" | custom-call | flops 3000000000 | bytes 100000 | tf_op jit(solution)/shard_map/pallas_call | solution.py:498
  12.3 0.3 %collective-permute-start.5 = (f32[104,128]{1,0:T(8,128)S(1)}, f32[104,128]{1,0:T(8,128)S(1)}, u32[]{:S(2)}, u32[]{:S(2)}) collective-permute-start(f32[104,128]{1,0:T(8,128)S(1)} %get-tuple-element.34), channel_id=1, source_target_pairs={{0,16},{16,0},{1,17},{17,1},{2,18},{18,2},{3,19},{19,3},{4,20},{20... | collective-permute-start | bytes 159752 | tf_op jit(solution)/shard_map/ppermute | solution.py:431
  12.7 0.0 copy-start.6
  12.7 0.5 %collective-permute-start.6 = (f32[32,128]{1,0:T(8,128)S(1)}, f32[32,128]{1,0:T(8,128)S(1)}, u32[]{:S(2)}, u32[]{:S(2)}) collective-permute-start(f32[32,128]{1,0:T(8,128)S(1)} %get-tuple-element.35), channel_id=1, source_target_pairs={{0,20},{4,16},{8,28},{12,24},{16,4},{20,0},{24,12},{28,8},{1,21},{... | collective-permute-start | bytes 49160 | tf_op jit(solution)/shard_map/ppermute | solution.py:441
  13.2 2.2 %collective-permute-start.7 = (f32[32,128]{1,0:T(8,128)S(1)}, f32[32,128]{1,0:T(8,128)S(1)}, u32[]{:S(2)}, u32[]{:S(2)}) collective-permute-start(f32[32,128]{1,0:T(8,128)S(1)} %get-tuple-element.36), channel_id=1, source_target_pairs={{0,28},{4,24},{8,20},{12,16},{16,12},{20,8},{24,4},{28,0},{1,29},{... | collective-permute-start | bytes 49160 | tf_op jit(solution)/shard_map/ppermute | solution.py:441
  15.4 0.4 %collective-permute-done.8.rows2_ref = f32[4,80,128]{2,1,0:T(8,128)S(1)} collective-permute-done((f32[4,80,128]{2,1,0:T(8,128)S(1)}, f32[4,80,128]{2,1,0:T(8,128)S(1)}, u32[]{:S(2)}, u32[]{:S(2)}) %collective-permute-start.8) | collective-permute-done | bytes 163872 | tf_op jit(solution)/shard_map/ppermute | solution.py:431
  15.8 0.0 collective-permute-done.5.own_ref
  15.8 0.0 copy-done.1
  15.8 0.0 copy-done.6
  15.8 1.3 %shard_map.78 = (bf16[80,256]{1,0:T(8,128)(2,1)S(1)}, f32[2,80,128]{2,1,0:T(8,128)S(1)}, f32[16,80,128]{2,1,0:T(8,128)S(1)}, f32[2,80,128]{2,1,0:T(8,128)S(1)}, ...) custom-call(f32[1,80,8,128]{3,2,1,0:T(8,128)S(1)} %copy-done, ...), custom_call_target="tpu_custom_call" | custom-call | flops 2000000000 | bytes 2000000 | tf_op jit(solution)/shard_map/pallas_call | solution.py:509
  17.1 0.0 collective-permute-done.6.msg1_ref
  17.1 0.2 %collective-permute-done.7.msg2_ref = f32[32,128]{1,0:T(8,128)S(1)} collective-permute-done((f32[32,128]{1,0:T(8,128)S(1)}, f32[32,128]{1,0:T(8,128)S(1)}, u32[]{:S(2)}, u32[]{:S(2)}) %collective-permute-start.7) | collective-permute-done | bytes 16416 | tf_op jit(solution)/shard_map/ppermute | solution.py:441
  17.4 2.5 %shard_map.79 = f32[1,80,8,128]{3,2,1,0:T(8,128)} custom-call(f32[104,128]{1,0:T(8,128)S(1)} %collective-permute-done.5.own_ref, f32[32,128]{1,0:T(8,128)S(1)} %collective-permute-done.6.msg1_ref, f32[32,128]{1,0:T(8,128)S(1)} %collective-permute-done.7.msg2_ref, bf16[80,256]{1,0:T(8,128)(2,1)S(1)} %get-tuple-element.39.mix_ref, ...), custom_call_target="tpu_custom_call" | custom-call | flops 300000000 | bytes 2000000 | tf_op jit(solution)/shard_map/pallas_call | solution.py:522
  (4 shorter events, 0.0 us)
Async XLA Ops:
  0.0 1.0 %copy-start = (f32[1,80,8,128]{3,2,1,0:T(8,128)S(1)}, f32[1,80,8,128]{3,2,1,0:T(8,128)}, u32[]{:S(2)}) copy-start(f32[1,80,8,128]{3,2,1,0:T(8,128)} %state_ref.3) | copy-start | bytes 983044
  0.0 1.0 %copy-start.2 = (s32[1,1,1,4,8]{4,3,2,1,0:T(4,128)S(1)}, s32[1,1,1,4,8]{4,3,2,1,0:T(4,128)}, u32[]{:S(2)}) copy-start(s32[1,1,1,4,8]{4,3,2,1,0:T(4,128)} %links_ref.1) | copy-start | bytes 388
  0.0 1.0 %copy-start.3 = (f32[1,64]{1,0:T(1,128)S(1)}, f32[1,64]{1,0:T(1,128)}, u32[]{:S(2)}) copy-start(f32[1,64]{1,0:T(1,128)} %weights_ref.1) | copy-start | bytes 772
  0.0 1.0 %copy-start.4 = (s32[8,1]{0,1:T(1,128)S(1)}, s32[8,1]{0,1:T(1,128)}, u32[]{:S(2)}) copy-start(s32[8,1]{0,1:T(1,128)} %param.12) | copy-start | bytes 100
  0.0 1.0 %copy-start.5 = (s32[8,1]{0,1:T(1,128)S(1)}, s32[8,1]{0,1:T(1,128)}, u32[]{:S(2)}) copy-start(s32[8,1]{0,1:T(1,128)} %param.13) | copy-start | bytes 100
  1.2 3.3 %collective-permute-start = (f32[24,128]{1,0:T(8,128)S(1)}, f32[24,128]{1,0:T(8,128)S(1)}, u32[]{:S(2)}, u32[]{:S(2)}) collective-permute-start(f32[24,128]{1,0:T(8,128)S(1)} %shard_map.74.refs_2_), channel_id=1, source_target_pairs={{0,16},{16,0},{1,17},{17,1},{2,18},{18,2},{3,19},{19,3},{4,20},{20... | collective-permute-start | bytes 36872 | tf_op jit(solution)/shard_map/ppermute | solution.py:431
  1.9 8.3 %collective-permute-start.1 = (f32[4,80,128]{2,1,0:T(8,128)S(1)}, f32[4,80,128]{2,1,0:T(8,128)S(1)}, u32[]{:S(2)}, u32[]{:S(2)}) collective-permute-start(f32[4,80,128]{2,1,0:T(8,128)S(1)} %get-tuple-element.30), channel_id=1, source_target_pairs={{0,4},{4,0},{8,12},{12,8},{1,5},{5,1},{9,13},{13,9},{2,6},{6,2},{1... | collective-permute-start | bytes 491528 | tf_op jit(solution)/shard_map/ppermute | solution.py:431
  4.5 7.5 %collective-permute-start.4 = (f32[40,128]{1,0:T(8,128)S(1)}, f32[40,128]{1,0:T(8,128)S(1)}, u32[]{:S(2)}, u32[]{:S(2)}) collective-permute-start(f32[40,128]{1,0:T(8,128)S(1)} %get-tuple-element.47), channel_id=1, source_target_pairs={{0,19},{1,18},{2,17},{3,16},{16,3},{17,2},{18,1},{19,0},{4,23},{5,... | collective-permute-start | bytes 61448 | tf_op jit(solution)/shard_map/ppermute | solution.py:441
  8.0 4.0 %collective-permute-start.2 = (f32[40,128]{1,0:T(8,128)S(1)}, f32[40,128]{1,0:T(8,128)S(1)}, u32[]{:S(2)}, u32[]{:S(2)}) collective-permute-start(f32[40,128]{1,0:T(8,128)S(1)} %get-tuple-element.48), channel_id=1, source_target_pairs={{0,17},{1,16},{2,19},{3,18},{16,1},{17,0},{18,3},{19,2},{4,21},{5,... | collective-permute-start | bytes 61448 | tf_op jit(solution)/shard_map/ppermute | solution.py:441
  8.0 4.0 %collective-permute-start.3 = (f32[16,128]{1,0:T(8,128)S(1)}, f32[16,128]{1,0:T(8,128)S(1)}, u32[]{:S(2)}, u32[]{:S(2)}) collective-permute-start(f32[16,128]{1,0:T(8,128)S(1)} %slice.6), channel_id=1, source_target_pairs={{0,18},{1,19},{2,16},{3,17},{16,2},{17,3},{18,0},{19,1},{4,22},{5,... | collective-permute-start | bytes 24584 | tf_op jit(solution)/shard_map/ppermute | solution.py:441
  8.5 7.3 %copy-start.1 = (f32[1,80,80]{2,1,0:T(8,128)S(1)}, f32[1,80,80]{2,1,0:T(8,128)}, u32[]{:S(2)}) copy-start(f32[1,80,80]{2,1,0:T(8,128)} %mixing_ref.1) | copy-start | bytes 76804
  8.5 7.3 %collective-permute-start.8 = (f32[4,80,128]{2,1,0:T(8,128)S(1)}, f32[4,80,128]{2,1,0:T(8,128)S(1)}, u32[]{:S(2)}, u32[]{:S(2)}) collective-permute-start(f32[4,80,128]{2,1,0:T(8,128)S(1)} %get-tuple-element.38), channel_id=1, source_target_pairs={{0,12},{4,8},{8,4},{12,0},{1,13},{5,9},{9,5},{13,1},{2,14},{6,10},... | collective-permute-start | bytes 491528 | tf_op jit(solution)/shard_map/ppermute | solution.py:431
  12.3 3.4 %collective-permute-start.5 = (f32[104,128]{1,0:T(8,128)S(1)}, f32[104,128]{1,0:T(8,128)S(1)}, u32[]{:S(2)}, u32[]{:S(2)}) collective-permute-start(f32[104,128]{1,0:T(8,128)S(1)} %get-tuple-element.34), channel_id=1, source_target_pairs={{0,16},{16,0},{1,17},{17,1},{2,18},{18,2},{3,19},{19,3},{4,20},{20... | collective-permute-start | bytes 159752 | tf_op jit(solution)/shard_map/ppermute | solution.py:431
  12.7 3.1 %copy-start.6 = (f32[1,80]{1,0:T(1,128)S(1)}, f32[1,80]{1,0:T(1,128)}, u32[]{:S(2)}) copy-start(f32[1,80]{1,0:T(1,128)} %diffuse_ref.1) | copy-start | bytes 964
  12.7 4.5 %collective-permute-start.6 = (f32[32,128]{1,0:T(8,128)S(1)}, f32[32,128]{1,0:T(8,128)S(1)}, u32[]{:S(2)}, u32[]{:S(2)}) collective-permute-start(f32[32,128]{1,0:T(8,128)S(1)} %get-tuple-element.35), channel_id=1, source_target_pairs={{0,20},{4,16},{8,28},{12,24},{16,4},{20,0},{24,12},{28,8},{1,21},{... | collective-permute-start | bytes 49160 | tf_op jit(solution)/shard_map/ppermute | solution.py:441
  13.2 4.2 %collective-permute-start.7 = (f32[32,128]{1,0:T(8,128)S(1)}, f32[32,128]{1,0:T(8,128)S(1)}, u32[]{:S(2)}, u32[]{:S(2)}) collective-permute-start(f32[32,128]{1,0:T(8,128)S(1)} %get-tuple-element.36), channel_id=1, source_target_pairs={{0,28},{4,24},{8,20},{12,16},{16,12},{20,8},{24,4},{28,0},{1,29},{... | collective-permute-start | bytes 49160 | tf_op jit(solution)/shard_map/ppermute | solution.py:441

commit v11 on v10

--- a/solution.py
+++ b/solution.py
@@ -352,9 +352,11 @@
     for slot in range(slots):
         start = slot * EDGE
         mine1 = (lane1 >= start) & (lane1 < start + EDGE)
-        flux_left = jnp.where(mine1, roll(flux_rows[slot], start + EDGE), flux_left)
-        flux_right = jnp.where(mine1, roll(flux_rows[slot], start), flux_right)
+        turned = roll(flux_rows[slot], start)
+        flux_left = jnp.where(lane1 // EDGE == (slot - 1) % slots, turned, flux_left)
+        flux_right = jnp.where(mine1, turned, flux_right)
         deep_side = jnp.where(mine1, deep_rows[slot], deep_side)
+    flux_left = roll(flux_left, EDGE)
 
     def strip(tile, west, east):
         above_below = roll(tile, EDGE) + roll(tile, -EDGE)

time: 20 us -> 20 us (level)
  no operation moved by 1% of the time
where the time goes in v11:
time: 20 us; the launch traced here: 19.9 us
  starting transfers between devices  11.8 us (59%)
  Pallas kernels  4.64 us (23%)
  waiting for transfers between devices  2.37 us (12%)
  local copies, waits for them, and re-layouts  0.97 us (5%)
    ppermute x5, starting transfers between devices, exchange_over(): return lax.ppermute(value, ('comp', axis), pairs)  6.73 us
    ppermute x4, starting transfers between devices, exchange(): return lax.ppermute(value, axis, pairs)  5.07 us
    pallas_call x1, Pallas kernels, on_device(): kernel_call(outer_kernel, f32(*state.shape), [vmem_spec()] * (3 + len(lai...  2.49 us
    ppermute x5, waiting for transfers between devices, exchange_over(): return lax.ppermute(value, ('comp', axis), pairs)  1.97 us
    pallas_call x1, Pallas kernels, on_device(): kernel_call(inner_kernel, (jax.ShapeDtypeStruct((levels, 256), jnp.bfloat...  1.33 us
    unnamed x14, local copies, waits for them, and re-layouts  0.97 us
    ppermute x4, waiting for transfers between devices, exchange(): return lax.ppermute(value, axis, pairs)  0.4 us
  transfers between devices with their start and end apart: 9, of which 3 were waited for; matrix products, arithmetic and copies ran while one was open for 0% of the time, Pallas kernels for 10%

profile of v11, /device:TPU:0, one launch (start us, length us, event | category | flops | bytes accessed | tf_op | source)
XLA Modules:
  0.0 19.9 jit_solution(14833604918036731319)
XLA Ops:
  0.0 0.0 copy-start
  0.0 0.0 copy-start.2
  0.0 0.0 copy-start.3
  0.0 0.0 copy-start.4
  0.0 0.0 copy-start.5
  0.0 0.9 %copy-done = f32[1,80,8,128]{3,2,1,0:T(8,128)S(1)} copy-done((f32[1,80,8,128]{3,2,1,0:T(8,128)S(1)}, f32[1,80,8,128]{3,2,1,0:T(8,128)}, u32[]{:S(2)}) %copy-start) | copy-done | bytes 327704
  1.0 0.0 copy-done.2
  1.0 0.0 copy-done.3
  1.0 0.0 copy-done.4
  1.0 0.0 copy-done.5
  1.0 0.2 shard_map.74.refs_2_
  1.2 0.5 %collective-permute-start = (f32[24,128]{1,0:T(8,128)S(1)}, f32[24,128]{1,0:T(8,128)S(1)}, u32[]{:S(2)}, u32[]{:S(2)}) collective-permute-start(f32[24,128]{1,0:T(8,128)S(1)} %shard_map.74.refs_2_), channel_id=1, source_target_pairs={{0,16},{16,0},{1,17},{17,1},{2,18},{18,2},{3,19},{19,3},{4,20},{20... | collective-permute-start | bytes 36872 | tf_op jit(solution)/shard_map/ppermute | solution.py:433
  1.6 0.3 %shard_map.76 = (f32[24,128]{1,0:T(8,128)S(1)}, f32[24,128]{1,0:T(8,128)S(1)}, f32[4,80,128]{2,1,0:T(8,128)S(1)}, f32[4,80,128]{2,1,0:T(8,128)S(1)}) custom-call(f32[1,80,8,128]{3,2,1,0:T(8,128)S(1)} %copy-done), custom_call_target="tpu_custom_call" | custom-call | flops 2000000000 | bytes 900000 | tf_op jit(solution)/shard_map/pallas_call | solution.py:474
  1.9 2.6 %collective-permute-start.1 = (f32[4,80,128]{2,1,0:T(8,128)S(1)}, f32[4,80,128]{2,1,0:T(8,128)S(1)}, u32[]{:S(2)}, u32[]{:S(2)}) collective-permute-start(f32[4,80,128]{2,1,0:T(8,128)S(1)} %get-tuple-element.30), channel_id=1, source_target_pairs={{0,4},{4,0},{8,12},{12,8},{1,5},{5,1},{9,13},{13,9},{2,6},{6,2},{1... | collective-permute-start | bytes 491528 | tf_op jit(solution)/shard_map/ppermute | solution.py:433
  4.5 0.0 collective-permute-done.refs_0_
  4.5 3.5 %collective-permute-start.4 = (f32[40,128]{1,0:T(8,128)S(1)}, f32[40,128]{1,0:T(8,128)S(1)}, u32[]{:S(2)}, u32[]{:S(2)}) collective-permute-start(f32[40,128]{1,0:T(8,128)S(1)} %get-tuple-element.47), channel_id=1, source_target_pairs={{0,19},{1,18},{2,17},{3,16},{16,3},{17,2},{18,1},{19,0},{4,23},{5,... | collective-permute-start | bytes 61448 | tf_op jit(solution)/shard_map/ppermute | solution.py:443
  8.0 0.0 collective-permute-start.2
  8.0 0.5 %collective-permute-start.3 = (f32[16,128]{1,0:T(8,128)S(1)}, f32[16,128]{1,0:T(8,128)S(1)}, u32[]{:S(2)}, u32[]{:S(2)}) collective-permute-start(f32[16,128]{1,0:T(8,128)S(1)} %slice.6), channel_id=1, source_target_pairs={{0,18},{1,19},{2,16},{3,17},{16,2},{17,3},{18,0},{19,1},{4,22},{5,... | collective-permute-start | bytes 24584 | tf_op jit(solution)/shard_map/ppermute | solution.py:443
  8.5 0.0 copy-start.1
  8.5 1.7 %collective-permute-start.8 = (f32[4,80,128]{2,1,0:T(8,128)S(1)}, f32[4,80,128]{2,1,0:T(8,128)S(1)}, u32[]{:S(2)}, u32[]{:S(2)}) collective-permute-start(f32[4,80,128]{2,1,0:T(8,128)S(1)} %get-tuple-element.38), channel_id=1, source_target_pairs={{0,12},{4,8},{8,4},{12,0},{1,13},{5,9},{9,5},{13,1},{2,14},{6,10},... | collective-permute-start | bytes 491528 | tf_op jit(solution)/shard_map/ppermute | solution.py:433
  10.2 0.0 collective-permute-done.1.rows1_ref
  10.2 1.7 %collective-permute-done.3.refs_4_ = f32[16,128]{1,0:T(8,128)S(1)} collective-permute-done((f32[16,128]{1,0:T(8,128)S(1)}, f32[16,128]{1,0:T(8,128)S(1)}, u32[]{:S(2)}, u32[]{:S(2)}) %collective-permute-start.3) | collective-permute-done | bytes 8224 | tf_op jit(solution)/shard_map/ppermute | solution.py:443
  11.9 0.0 collective-permute-done.4.refs_5_
  12.0 0.0 collective-permute-done.2.refs_3_
  12.0 0.4 %shard_map.77 = (f32[104,128]{1,0:T(8,128)S(1)}, f32[32,128]{1,0:T(8,128)S(1)}, f32[32,128]{1,0:T(8,128)S(1)}) custom-call(f32[24,128]{1,0:T(8,128)S(1)} %collective-permute-done.refs_0_, f32[16,128]{1,0:T(8,128)S(1)} %shard_map.75.refs_1_, f32[24,128]{1,0:T(8,128)S(1)} %shard_map.74.refs_2_, f32[40,128]{1,0:T(8,128)S(1)} %collective-permute-done.2.refs_3_, ...), custom_call_target="tpu_custom_call" | custom-call | flops 3000000000 | bytes 100000 | tf_op jit(solution)/shard_map/pallas_call | solution.py:500
  12.3 0.3 %collective-permute-start.5 = (f32[104,128]{1,0:T(8,128)S(1)}, f32[104,128]{1,0:T(8,128)S(1)}, u32[]{:S(2)}, u32[]{:S(2)}) collective-permute-start(f32[104,128]{1,0:T(8,128)S(1)} %get-tuple-element.34), channel_id=1, source_target_pairs={{0,16},{16,0},{1,17},{17,1},{2,18},{18,2},{3,19},{19,3},{4,20},{20... | collective-permute-start | bytes 159752 | tf_op jit(solution)/shard_map/ppermute | solution.py:433
  12.7 0.0 copy-start.6
  12.7 0.5 %collective-permute-start.6 = (f32[32,128]{1,0:T(8,128)S(1)}, f32[32,128]{1,0:T(8,128)S(1)}, u32[]{:S(2)}, u32[]{:S(2)}) collective-permute-start(f32[32,128]{1,0:T(8,128)S(1)} %get-tuple-element.35), channel_id=1, source_target_pairs={{0,20},{4,16},{8,28},{12,24},{16,4},{20,0},{24,12},{28,8},{1,21},{... | collective-permute-start | bytes 49160 | tf_op jit(solution)/shard_map/ppermute | solution.py:443
  13.2 2.2 %collective-permute-start.7 = (f32[32,128]{1,0:T(8,128)S(1)}, f32[32,128]{1,0:T(8,128)S(1)}, u32[]{:S(2)}, u32[]{:S(2)}) collective-permute-start(f32[32,128]{1,0:T(8,128)S(1)} %get-tuple-element.36), channel_id=1, source_target_pairs={{0,28},{4,24},{8,20},{12,16},{16,12},{20,8},{24,4},{28,0},{1,29},{... | collective-permute-start | bytes 49160 | tf_op jit(solution)/shard_map/ppermute | solution.py:443
  15.4 0.4 %collective-permute-done.8.rows2_ref = f32[4,80,128]{2,1,0:T(8,128)S(1)} collective-permute-done((f32[4,80,128]{2,1,0:T(8,128)S(1)}, f32[4,80,128]{2,1,0:T(8,128)S(1)}, u32[]{:S(2)}, u32[]{:S(2)}) %collective-permute-start.8) | collective-permute-done | bytes 163872 | tf_op jit(solution)/shard_map/ppermute | solution.py:433
  15.8 0.0 collective-permute-done.5.own_ref
  15.8 0.0 copy-done.1
  15.8 0.0 copy-done.6
  15.8 1.3 %shard_map.78 = (bf16[80,256]{1,0:T(8,128)(2,1)S(1)}, f32[2,80,128]{2,1,0:T(8,128)S(1)}, f32[16,80,128]{2,1,0:T(8,128)S(1)}, f32[2,80,128]{2,1,0:T(8,128)S(1)}, ...) custom-call(f32[1,80,8,128]{3,2,1,0:T(8,128)S(1)} %copy-done, ...), custom_call_target="tpu_custom_call" | custom-call | flops 2000000000 | bytes 2000000 | tf_op jit(solution)/shard_map/pallas_call | solution.py:511
  17.1 0.0 collective-permute-done.6.msg1_ref
  17.1 0.2 %collective-permute-done.7.msg2_ref = f32[32,128]{1,0:T(8,128)S(1)} collective-permute-done((f32[32,128]{1,0:T(8,128)S(1)}, f32[32,128]{1,0:T(8,128)S(1)}, u32[]{:S(2)}, u32[]{:S(2)}) %collective-permute-start.7) | collective-permute-done | bytes 16416 | tf_op jit(solution)/shard_map/ppermute | solution.py:443
  17.4 2.5 %shard_map.79 = f32[1,80,8,128]{3,2,1,0:T(8,128)} custom-call(f32[104,128]{1,0:T(8,128)S(1)} %collective-permute-done.5.own_ref, f32[32,128]{1,0:T(8,128)S(1)} %collective-permute-done.6.msg1_ref, f32[32,128]{1,0:T(8,128)S(1)} %collective-permute-done.7.msg2_ref, bf16[80,256]{1,0:T(8,128)(2,1)S(1)} %get-tuple-element.39.mix_ref, ...), custom_call_target="tpu_custom_call" | custom-call | flops 300000000 | bytes 2000000 | tf_op jit(solution)/shard_map/pallas_call | solution.py:524
  (4 shorter events, 0.0 us)
Async XLA Ops:
  0.0 1.0 %copy-start = (f32[1,80,8,128]{3,2,1,0:T(8,128)S(1)}, f32[1,80,8,128]{3,2,1,0:T(8,128)}, u32[]{:S(2)}) copy-start(f32[1,80,8,128]{3,2,1,0:T(8,128)} %state_ref.3) | copy-start | bytes 983044
  0.0 1.0 %copy-start.2 = (s32[1,1,1,4,8]{4,3,2,1,0:T(4,128)S(1)}, s32[1,1,1,4,8]{4,3,2,1,0:T(4,128)}, u32[]{:S(2)}) copy-start(s32[1,1,1,4,8]{4,3,2,1,0:T(4,128)} %links_ref.1) | copy-start | bytes 388
  0.0 1.0 %copy-start.3 = (f32[1,64]{1,0:T(1,128)S(1)}, f32[1,64]{1,0:T(1,128)}, u32[]{:S(2)}) copy-start(f32[1,64]{1,0:T(1,128)} %weights_ref.1) | copy-start | bytes 772
  0.0 1.0 %copy-start.4 = (s32[8,1]{0,1:T(1,128)S(1)}, s32[8,1]{0,1:T(1,128)}, u32[]{:S(2)}) copy-start(s32[8,1]{0,1:T(1,128)} %param.12) | copy-start | bytes 100
  0.0 1.0 %copy-start.5 = (s32[8,1]{0,1:T(1,128)S(1)}, s32[8,1]{0,1:T(1,128)}, u32[]{:S(2)}) copy-start(s32[8,1]{0,1:T(1,128)} %param.13) | copy-start | bytes 100
  1.2 3.3 %collective-permute-start = (f32[24,128]{1,0:T(8,128)S(1)}, f32[24,128]{1,0:T(8,128)S(1)}, u32[]{:S(2)}, u32[]{:S(2)}) collective-permute-start(f32[24,128]{1,0:T(8,128)S(1)} %shard_map.74.refs_2_), channel_id=1, source_target_pairs={{0,16},{16,0},{1,17},{17,1},{2,18},{18,2},{3,19},{19,3},{4,20},{20... | collective-permute-start | bytes 36872 | tf_op jit(solution)/shard_map/ppermute | solution.py:433
  1.9 8.3 %collective-permute-start.1 = (f32[4,80,128]{2,1,0:T(8,128)S(1)}, f32[4,80,128]{2,1,0:T(8,128)S(1)}, u32[]{:S(2)}, u32[]{:S(2)}) collective-permute-start(f32[4,80,128]{2,1,0:T(8,128)S(1)} %get-tuple-element.30), channel_id=1, source_target_pairs={{0,4},{4,0},{8,12},{12,8},{1,5},{5,1},{9,13},{13,9},{2,6},{6,2},{1... | collective-permute-start | bytes 491528 | tf_op jit(solution)/shard_map/ppermute | solution.py:433
  4.5 7.5 %collective-permute-start.4 = (f32[40,128]{1,0:T(8,128)S(1)}, f32[40,128]{1,0:T(8,128)S(1)}, u32[]{:S(2)}, u32[]{:S(2)}) collective-permute-start(f32[40,128]{1,0:T(8,128)S(1)} %get-tuple-element.47), channel_id=1, source_target_pairs={{0,19},{1,18},{2,17},{3,16},{16,3},{17,2},{18,1},{19,0},{4,23},{5,... | collective-permute-start | bytes 61448 | tf_op jit(solution)/shard_map/ppermute | solution.py:443
  8.0 4.0 %collective-permute-start.2 = (f32[40,128]{1,0:T(8,128)S(1)}, f32[40,128]{1,0:T(8,128)S(1)}, u32[]{:S(2)}, u32[]{:S(2)}) collective-permute-start(f32[40,128]{1,0:T(8,128)S(1)} %get-tuple-element.48), channel_id=1, source_target_pairs={{0,17},{1,16},{2,19},{3,18},{16,1},{17,0},{18,3},{19,2},{4,21},{5,... | collective-permute-start | bytes 61448 | tf_op jit(solution)/shard_map/ppermute | solution.py:443
  8.0 4.0 %collective-permute-start.3 = (f32[16,128]{1,0:T(8,128)S(1)}, f32[16,128]{1,0:T(8,128)S(1)}, u32[]{:S(2)}, u32[]{:S(2)}) collective-permute-start(f32[16,128]{1,0:T(8,128)S(1)} %slice.6), channel_id=1, source_target_pairs={{0,18},{1,19},{2,16},{3,17},{16,2},{17,3},{18,0},{19,1},{4,22},{5,... | collective-permute-start | bytes 24584 | tf_op jit(solution)/shard_map/ppermute | solution.py:443
  8.5 7.3 %copy-start.1 = (f32[1,80,80]{2,1,0:T(8,128)S(1)}, f32[1,80,80]{2,1,0:T(8,128)}, u32[]{:S(2)}) copy-start(f32[1,80,80]{2,1,0:T(8,128)} %mixing_ref.1) | copy-start | bytes 76804
  8.5 7.3 %collective-permute-start.8 = (f32[4,80,128]{2,1,0:T(8,128)S(1)}, f32[4,80,128]{2,1,0:T(8,128)S(1)}, u32[]{:S(2)}, u32[]{:S(2)}) collective-permute-start(f32[4,80,128]{2,1,0:T(8,128)S(1)} %get-tuple-element.38), channel_id=1, source_target_pairs={{0,12},{4,8},{8,4},{12,0},{1,13},{5,9},{9,5},{13,1},{2,14},{6,10},... | collective-permute-start | bytes 491528 | tf_op jit(solution)/shard_map/ppermute | solution.py:433
  12.3 3.4 %collective-permute-start.5 = (f32[104,128]{1,0:T(8,128)S(1)}, f32[104,128]{1,0:T(8,128)S(1)}, u32[]{:S(2)}, u32[]{:S(2)}) collective-permute-start(f32[104,128]{1,0:T(8,128)S(1)} %get-tuple-element.34), channel_id=1, source_target_pairs={{0,16},{16,0},{1,17},{17,1},{2,18},{18,2},{3,19},{19,3},{4,20},{20... | collective-permute-start | bytes 159752 | tf_op jit(solution)/shard_map/ppermute | solution.py:433
  12.7 3.1 %copy-start.6 = (f32[1,80]{1,0:T(1,128)S(1)}, f32[1,80]{1,0:T(1,128)}, u32[]{:S(2)}) copy-start(f32[1,80]{1,0:T(1,128)} %diffuse_ref.1) | copy-start | bytes 964
  12.7 4.5 %collective-permute-start.6 = (f32[32,128]{1,0:T(8,128)S(1)}, f32[32,128]{1,0:T(8,128)S(1)}, u32[]{:S(2)}, u32[]{:S(2)}) collective-permute-start(f32[32,128]{1,0:T(8,128)S(1)} %get-tuple-element.35), channel_id=1, source_target_pairs={{0,20},{4,16},{8,28},{12,24},{16,4},{20,0},{24,12},{28,8},{1,21},{... | collective-permute-start | bytes 49160 | tf_op jit(solution)/shard_map/ppermute | solution.py:443
  13.2 4.2 %collective-permute-start.7 = (f32[32,128]{1,0:T(8,128)S(1)}, f32[32,128]{1,0:T(8,128)S(1)}, u32[]{:S(2)}, u32[]{:S(2)}) collective-permute-start(f32[32,128]{1,0:T(8,128)S(1)} %get-tuple-element.36), channel_id=1, source_target_pairs={{0,28},{4,24},{8,20},{12,16},{16,12},{20,8},{24,4},{28,0},{1,29},{... | collective-permute-start | bytes 49160 | tf_op jit(solution)/shard_map/ppermute | solution.py:443
